TPU v7x, 32 devices: a whole 2x2x4 slice. The times are simulated.
32 devices in a mesh: pipe: 4 (over x, core), ctx: 2 (over y), tp: 4 (over z).
Axes of the slice: x: 2, y: 2, z: 4, core: 2. Of those that a mesh axis runs over, the one named last changes fastest.
Arguments:
- query_rows: bfloat16 [1024, 64, 128], P(('pipe', 'ctx'), 'tp'), may hold values from -100 to 100
- key_rows: bfloat16 [1024, 4, 128], P(('pipe', 'ctx'), 'tp'), may hold values from -6 to 6
- value_rows: bfloat16 [1024, 4, 128], P(('pipe', 'ctx'), 'tp'), may hold values from -6 to 6
- doc_ids: int32 [1024], P(('pipe', 'ctx')), may hold values from 0 to 3, never falling along the last dimension, each value on 1 to 512 neighbouring positions
- out_weight: bfloat16 [8192, 8192], P('tp', 'ctx'), may hold values from -0.25 to 0.25
Outputs:
- projected: bfloat16 [4, 2, 4, 32, 8192], P('pipe', None, 'tp', None, 'ctx')
Inputs may be any that keep to these rules, and one draw needn't show every extreme that they name: `doc_ids`: ids never fall along the book; the longest document has exactly 512 tokens.
All inputs are finite; a program needn't handle non-finite values.
Results may differ from a plain program's by a relative error of at most 0.012.
Values may be sent and summed in bfloat16 or wider, within the bound.
No kernel may reach another device: no remote copies, remote signals or barrier semaphores. Data moves between devices by JAX's collectives and lax.ppermute only.
A program may use at most 128 MiB of HBM per device.

v0:
```python
import jax
import jax.numpy as jnp
from jax import lax
from jax.sharding import PartitionSpec as P


def shards(query_rows, key_rows, value_rows, doc_ids, out_weight):
    local_rows, head_count, head_width = query_rows.shape
    kv_local = key_rows.shape[1]
    group_size = head_count // kv_local
    my_index = lax.axis_index(("pipe", "ctx"))
    half_rows = local_rows // 2
    offsets = jnp.arange(half_rows, dtype=jnp.int32)
    first_pos = my_index * local_rows + offsets
    doc_marks = doc_ids.astype(jnp.bfloat16)
    second_query, second_doc = (query_rows[half_rows:], doc_marks[half_rows:])
    second_pos = my_index * local_rows + half_rows + offsets
    groups = (
        (
            query_rows[:half_rows].reshape(half_rows, kv_local, group_size, head_width),
            first_pos,
            doc_ids[:half_rows],
        ),
        (
            second_query.reshape(half_rows, kv_local, group_size, head_width),
            second_pos,
            second_doc.astype(jnp.int32),
        ),
    )
    inv_scale = head_width ** (-0.5)
    start_one = (
        jnp.full((half_rows, kv_local, group_size), -1e30, jnp.float32),
        jnp.zeros((half_rows, kv_local, group_size), jnp.float32),
        jnp.zeros((half_rows, kv_local, group_size, head_width), jnp.float32),
    )
    carry_states = (start_one, start_one)
    row_start = jnp.int32(0)
    key_piece = lax.all_gather(key_rows, ("pipe", "ctx"), axis=0, tiled=True)
    value_piece = lax.all_gather(value_rows, ("pipe", "ctx"), axis=0, tiled=True)
    mark_piece = lax.all_gather(doc_marks, ("pipe", "ctx"), axis=0, tiled=True)
    key_count = key_piece.shape[0]
    key_pos = jnp.arange(key_count, dtype=jnp.int32)
    key_doc = mark_piece.astype(jnp.int32)
    updated = []
    for (query_part, query_pos, query_doc), carry_state in zip(groups, carry_states):

        def update_state(
            old_state, query_part=query_part, query_pos=query_pos, query_doc=query_doc
        ):
            run_peak, running_sum, accumulated = old_state
            scores = (
                jnp.einsum(
                    "qjgd,kjd->qjgk", query_part, key_piece, preferred_element_type=jnp.float32
                )
                * inv_scale
            )
            allowed = (key_pos[None, :] <= query_pos[:, None]) & (
                key_doc[None, :] == query_doc[:, None]
            )
            wide_mask = allowed[:, None, None, :]
            masked = jnp.where(wide_mask, scores, -1e30)
            new_peak = jnp.maximum(run_peak, jnp.max(masked, axis=3))
            weights = jnp.where(wide_mask, jnp.exp(scores - new_peak[..., None]), 0.0)
            running_sum = jnp.sum(weights, axis=3)
            accumulated = jnp.einsum(
                "qjgk,kjd->qjgd",
                weights.astype(jnp.bfloat16),
                value_piece,
                preferred_element_type=jnp.float32,
            )
            return (new_peak, running_sum, accumulated)

        def keep_state(old_state):
            return old_state

        updated.append(
            lax.cond(row_start <= jnp.max(query_pos), update_state, keep_state, carry_state)
        )
    folded = tuple(updated)
    attended = [
        (state[2] / state[1][..., None])
        .astype(jnp.bfloat16)
        .reshape(half_rows, head_count * head_width)
        for state in folded
    ]
    first_out, second_out = attended
    flat_rows = jnp.concatenate([first_out, second_out], axis=0)
    tp_size = lax.axis_size("tp")
    ctx_size = lax.axis_size("ctx")
    quarter = local_rows // tp_size
    columns = out_weight.shape[1]
    partial_value = jnp.dot(
        lax.all_gather(flat_rows, "ctx", axis=0, tiled=True),
        out_weight,
        preferred_element_type=jnp.float32,
    )
    partial_value = partial_value.reshape(ctx_size, tp_size, quarter, columns)
    summed = lax.psum_scatter(
        partial_value.astype(jnp.bfloat16), "tp", scatter_dimension=1, tiled=True
    )
    return summed.reshape(1, ctx_size, 1, quarter, columns)


def solution(mesh):
    return jax.shard_map(
        shards,
        mesh=mesh,
        in_specs=(
            P(("pipe", "ctx"), "tp", None),
            P(("pipe", "ctx"), "tp", None),
            P(("pipe", "ctx"), "tp", None),
            P(("pipe", "ctx")),
            P("tp", "ctx"),
        ),
        out_specs=P("pipe", None, "tp", None, "ctx"),
        check_vma=False,
    )
```

profile of v0, /device:TPU:0, one launch (start us, length us, event | category | flops | bytes accessed | tf_op | source)
XLA Modules:
  0.0 150.5 jit_solution(14210763788949561327)
XLA Ops:
  6.5 0.7 fusion.30
  8.6 0.7 fusion.32
  9.3 13.2 %all-gather = bf16[8,1,128]{2,1,0:T(2,128)(2,1)S(1)} all-gather(bf16[1,1,128]{2,1,0:T(2,128)(2,1)S(1)} %get-tuple-element.93), channel_id=1, replica_groups=mesh['pipe'=4,'ctx'=2,'tp'=4] {'pipe','ctx'}, dimensions={0}, use_global_device_ids=true | all-gather | bytes 2304 | tf_op jit(solution)/shard_map/all_gather | solution.py:40
  22.6 16.2 %all_gather.13 = bf16[1024,1,128]{2,0,1:T(8,128)(2,1)S(1)} all-gather(bf16[128,1,128]{2,0,1:T(8,128)(2,1)} %param.10), channel_id=1, replica_groups=mesh['pipe'=4,'ctx'=2,'tp'=4] {'pipe','ctx'}, dimensions={0}, use_global_device_ids=true | all-gather | bytes 294912 | tf_op jit(solution)/shard_map/all_gather | solution.py:38
  38.8 15.6 %all_gather.14 = bf16[1024,1,128]{2,0,1:T(8,128)(2,1)S(1)} all-gather(bf16[128,1,128]{2,0,1:T(8,128)(2,1)} %param.11), channel_id=1, replica_groups=mesh['pipe'=4,'ctx'=2,'tp'=4] {'pipe','ctx'}, dimensions={0}, use_global_device_ids=true | all-gather | bytes 294912 | tf_op jit(solution)/shard_map/all_gather | solution.py:39
  54.4 4.6 %conditional.3 = (f32[64,1,16]{0,2,1:T(8,128)S(1)}, f32[64,1,16,128]{3,2,0,1:T(8,128)S(1)}) conditional(s32[]{:T(128)} %convert_element_type.37, () %tuple.23, (s32[1024]{0:T(1024)S(1)}, s32[64]{0:T(128)S(1)}, s32[1024]{0:T(1024)S(1)}, s32[64]{0:T(128)S(1)}, bf16[1024,1,128]{2,0,1:T(8,128)(2,1)S(1)}, /*index=5*/bf16[128,16,128]{2,1,0:T(8,128)(2,1)}, ...), branch_computations={%region_6.7_spmd, %region_7.10_spmd} | conditional | flops 548600832 | bytes 16286224 | solution.py:77
  54.5 1.2 copy.15
  55.7 0.9 fusion.15
  56.6 1.2 fusion.19
  57.8 0.9 fusion.21
  58.6 0.3 copy.29
  59.4 4.6 %conditional.2 = (f32[64,1,16]{0,2,1:T(8,128)S(1)}, f32[64,1,16,128]{3,2,0,1:T(8,128)S(1)}) conditional(s32[]{:T(128)} %convert_element_type.33, () %tuple.21, (s32[1024]{0:T(1024)S(1)}, s32[64]{0:T(128)S(1)}, s32[1024]{0:T(1024)S(1)}, s32[128]{0:T(128)S(1)}, bf16[1024,1,128]{2,0,1:T(8,128)(2,1)S(1)}, /*index=5*/bf16[128,16,128]{2,1,0:T(8,128)(2,1)}, ...), branch_computations={%region_1.0_spmd, %region_2.5_spmd} | conditional | flops 548600832 | bytes 16286224 | solution.py:77
  59.5 1.2 copy.13
  60.7 0.9 fusion
  61.6 1.2 fusion.4
  62.7 0.9 fusion.6
  63.6 0.3 copy.28
  64.0 0.2 divide_convert_fusion.1
  64.3 0.8 pad_maximum_fusion
  65.2 0.2 reduce-scatter.2.cloned.1.call-start
  65.4 22.1 %all-gather.3.cloned.1.call-done = bf16[256,2048]{1,0:T(8,128)(2,1)} async-done(((bf16[128,2048]{1,0:T(8,128)(2,1)}), bf16[256,2048]{1,0:T(8,128)(2,1)}) %all-gather.3.cloned.1.call-update) | async-done | bytes 1048592 | tf_op jit(solution)/shard_map/all_gather | solution.py:93
  87.5 10.6 %convolution_convert_fusion = bf16[256,4096]{1,0:T(8,128)(2,1)S(1)} fusion(bf16[256,2048]{1,0:T(8,128)(2,1)} %all-gather.3.cloned.1.call-done, bf16[2048,4096]{1,0:T(8,128)(2,1)} %param.13), kind=kOutput, calls=%fused_computation.38 | convolution fusion | flops 4296015872 | bytes 19922944 | tf_op jit(solution)/shard_map/dot_general | solution.py:92
  98.1 1.6 %copy.17 = bf16[2,4,32,4096]{3,2,0,1:T(8,128)(2,1)} copy(bf16[2,4,32,4096]{3,2,1,0:T(8,128)(2,1)S(1)} %bitcast.100) | data formatting | bytes 4194304 | tf_op jit(solution)/shard_map/convert_element_type | solution.py:99
  99.7 44.0 %reduce-scatter.2.cloned.1.call-done = bf16[2,1,32,4096]{3,2,0,1:T(8,128)(2,1)} async-done(((bf16[2,4,32,4096]{3,2,0,1:T(8,128)(2,1)}), bf16[2,1,32,4096]{3,2,0,1:T(8,128)(2,1)}) %reduce-scatter.2.cloned.1.call-update) | async-done | bytes 524304 | tf_op jit(solution)/shard_map/reduce_scatter | solution.py:98
  (20 shorter events, 0.9 us)
Async XLA Ops:
  6.5 80.9 %all-gather.3.cloned.1.call-start = ((), (), s32[]{:S(2)}) async-start(), calls=%async_computation.1 | async-start | bytes 1572864 | tf_op jit(solution)/shard_map/all_gather | solution.py:93
  54.4 5.0 %copy-start = (s32[128]{0:T(128)S(1)}, s32[128]{0:T(128)}, u32[]{:S(2)}) copy-start(s32[128]{0:T(128)} %param.12) | copy-start | bytes 1540
  65.2 78.5 %reduce-scatter.2.cloned.1.call-start = ((), (), s32[]{:S(2)}) async-start(), calls=%async_computation.2 | async-start | bytes 2621440 | tf_op jit(solution)/shard_map/reduce_scatter | solution.py:98
Sparse Core Ops, SparseCore 0:
  65.3 22.1 all-gather.2
  99.8 43.8 reduce-scatter.1
where the time goes:
time: 151 us
  waiting for transfers between devices  66.1 us (44%)
  blocking collectives  45 us (30%)
  between operations  14.8 us (10%)
  matrix products  14.1 us (9%)
  other arithmetic  5.33 us (4%)
  local copies, waits for them, and re-layouts  4.86 us (3%)
    reduce_scatter x1, waiting for transfers between devices, shards(): lax.psum_scatter(partial_value.astype(jnp.bfloat16), 'tp', scatter_dimens...  44 us
    all_gather x1, waiting for transfers between devices, shards(): lax.all_gather(flat_rows, 'ctx', axis=0, tiled=True)  22.1 us
    all_gather x1, blocking collectives, shards(): key_piece = lax.all_gather(key_rows, ('pipe', 'ctx'), axis=0, tiled=True)  16.2 us
    all_gather x1, blocking collectives, shards(): lax.all_gather(value_rows, ('pipe', 'ctx'), axis=0, tiled=True)  15.6 us
    all_gather x1, blocking collectives, shards(): mark_piece = lax.all_gather(doc_marks, ('pipe', 'ctx'), axis=0, tiled=True)  13.2 us
    dot_general x1, matrix products, shards(): jnp.dot(lax.all_gather(flat_rows, 'ctx', axis=0, tiled=True), out_weight,...  10.6 us
  transfers between devices with their start and end apart: 2, of which 2 were waited for; matrix products, arithmetic and copies ran while one was open for 0% of the time, Pallas kernels for 0%

commit v1 on v0

v1 whole, which is shorter than its diff:
```python
import functools

import jax
import jax.numpy as jnp
from jax import lax
from jax.experimental import pallas as pl
from jax.experimental.pallas import tpu as pltpu
from jax.sharding import PartitionSpec as P

BF16 = jnp.bfloat16
F32 = jnp.float32
LOG2E = 1.4426950408889634
MIB = 1 << 20

ORDER = ((3, 2, 1, 0), (3, 2, 0, 1), (0, 1, 3, 2), (0, 1, 2, 3))
PLACE = tuple(tuple(row.index(s) for s in range(4)) for row in ORDER)
OUTER = ((0, 1), (1, 0), (2, 3), (3, 2))
INNER = ((1, 2), (2, 1))


def pack_kernel(key_ref, value_ref, doc_ref, out_ref):
    rows = key_ref.shape[0]
    out_ref[:rows] = key_ref[...]
    out_ref[rows : 2 * rows] = value_ref[...]
    marks = doc_ref[...].astype(F32)
    out_ref[2 * rows :] = jnp.broadcast_to(marks, (16, rows)).astype(BF16)


def pack(key_rows, value_rows, doc_ids):
    rows, _, width = key_rows.shape
    return pl.pallas_call(
        pack_kernel,
        out_shape=jax.ShapeDtypeStruct((2 * rows + 16, width), BF16),
        compiler_params=pltpu.CompilerParams(vmem_limit_bytes=4 * MIB),
    )(key_rows.reshape(rows, width), value_rows.reshape(rows, width), doc_ids.reshape(1, rows))


def attend_kernel(window, heads, info_ref, query_ref, *refs):
    blocks = refs[:8]
    out_ref, wide, keys, values, marks, bias = refs[8:]
    rows, width = blocks[0].shape[0] // 2 - 8, blocks[0].shape[1]
    mine, asked = info_ref[0], info_ref[1]
    keys[...] = jnp.zeros_like(keys)
    values[...] = jnp.zeros_like(values)
    marks[...] = jnp.full_like(marks, -1.0)
    for m in range(8):
        slot = (mine ^ m) - asked + window - 1

        @pl.when((slot >= 0) & (slot < window))
        def _(m=m, slot=slot):
            at = pl.ds(pl.multiple_of(slot * rows, rows), rows)
            keys[at, :] = blocks[m][:rows]
            values[at, :] = blocks[m][rows : 2 * rows]
            marks[slot] = blocks[m][2 * rows :].astype(F32)[:8]

    wide[...] = query_ref[...].astype(F32)
    own = jnp.transpose(jnp.broadcast_to(marks[window - 1][:1], (rows, rows)))
    for s in range(window):
        allowed = own == marks[s][:1]
        if s == window - 1:
            at_row = lax.broadcasted_iota(jnp.int32, (rows, rows), 0)
            at_col = lax.broadcasted_iota(jnp.int32, (rows, rows), 1)
            allowed = allowed & (at_col <= at_row)
        bias[:, s * rows : (s + 1) * rows] = jnp.where(allowed, 0.0, -1e30)
    factor = LOG2E * width**-0.5
    quarter = rows // 4
    for h in range(heads):
        query = wide[pl.ds(h, rows, stride=heads), :].astype(BF16)
        scores = lax.dot_general(
            query, keys[...], (((1,), (1,)), ((), ())), preferred_element_type=F32
        )
        scores = scores + bias[...]
        peak = jnp.max(scores, axis=1, keepdims=True)
        weights = jnp.exp2((scores - peak) * factor)
        total = jnp.sum(weights, axis=1, keepdims=True)
        summed = jnp.dot(weights.astype(BF16), values[...], preferred_element_type=F32)
        result = (summed / total).astype(BF16)
        for s in range(4):
            at = pl.ds(pl.multiple_of(info_ref[2 + s] * quarter, quarter), quarter)
            out_ref[at, h * width : (h + 1) * width] = result[s * quarter : (s + 1) * quarter]


def attend(info, query, blocks, window):
    rows, heads, width = query.shape
    vmem = pl.BlockSpec(memory_space=pltpu.VMEM)
    smem = pl.BlockSpec(memory_space=pltpu.SMEM)
    return pl.pallas_call(
        functools.partial(attend_kernel, window, heads),
        out_shape=jax.ShapeDtypeStruct((rows, heads * width), BF16),
        in_specs=[smem] + [vmem] * 9,
        out_specs=vmem,
        scratch_shapes=[
            pltpu.VMEM((rows * heads, width), F32),
            pltpu.VMEM((window * rows, width), BF16),
            pltpu.VMEM((window * rows, width), BF16),
            pltpu.VMEM((window, 8, rows), F32),
            pltpu.VMEM((rows, window * rows), F32),
        ],
        compiler_params=pltpu.CompilerParams(vmem_limit_bytes=16 * MIB),
        cost_estimate=pl.CostEstimate(
            flops=4 * rows * heads * window * rows * width,
            bytes_accessed=4 * rows * heads * width,
            transcendentals=rows * heads * window * rows,
        ),
    )(info, query.reshape(rows * heads, width), *blocks)


def project_kernel(rows_ref, weight_ref, *outs):
    product = jnp.dot(rows_ref[...], weight_ref[...], preferred_element_type=F32).astype(BF16)
    quarter = product.shape[0] // 4
    for s, out in enumerate(outs):
        out[...] = product[s * quarter : (s + 1) * quarter]


def project(rows, weight):
    count, depth = rows.shape
    columns = weight.shape[1]
    tile = 512
    quarter = count // 4
    return pl.pallas_call(
        project_kernel,
        grid=(columns // tile,),
        out_shape=[jax.ShapeDtypeStruct((quarter, columns), BF16)] * 4,
        in_specs=[
            pl.BlockSpec((count, depth), lambda i: (0, 0)),
            pl.BlockSpec((depth, tile), lambda i: (0, i)),
        ],
        out_specs=[pl.BlockSpec((quarter, tile), lambda i: (0, i))] * 4,
        compiler_params=pltpu.CompilerParams(vmem_limit_bytes=16 * MIB),
        cost_estimate=pl.CostEstimate(
            flops=2 * count * depth * columns,
            bytes_accessed=2 * depth * columns,
            transcendentals=0,
        ),
    )(rows, weight)


def reduce_line(parts):
    def swap(value, pairs):
        return lax.ppermute(value, "tp", pairs)

    first, second, third, kept = parts
    first_in = swap(first, OUTER)
    second_in = swap(second, OUTER)
    first_far = swap(first + first_in, INNER)
    second_far = swap(second + second_in, INNER)
    third_in = swap(third + first_far, OUTER)
    return kept + third_in + second_far


def shards_line(query_rows, key_rows, value_rows, doc_ids, out_weight):
    rows, heads, width = query_rows.shape
    columns = out_weight.shape[1]
    mine = lax.axis_index(("pipe", "ctx"))
    place = jnp.asarray(PLACE, jnp.int32)[lax.axis_index("tp")]
    window = 5
    packed = pack(key_rows, value_rows, doc_ids)
    blocks = [packed] + [
        lax.ppermute(packed, ("pipe", "ctx"), [(i, i ^ m) for i in range(8)]) for m in range(1, 8)
    ]
    other_query = lax.ppermute(query_rows, "ctx", [(0, 1), (1, 0)])
    halves = []
    for asked, query in ((mine, query_rows), (mine ^ 1, other_query)):
        info = jnp.concatenate([jnp.stack([mine, asked]).astype(jnp.int32), place])
        rows_now = attend(info, query, blocks, window)
        halves.append(reduce_line(project(rows_now, out_weight)))
    at_first = lax.axis_index("ctx") == 0
    own, other = halves
    both = jnp.stack([jnp.where(at_first, own, other), jnp.where(at_first, other, own)])
    return both.reshape(1, 2, 1, rows // 4, columns)


def shards_any(query_rows, key_rows, value_rows, doc_ids, out_weight):
    rows, heads, width = query_rows.shape
    kv_local = key_rows.shape[1]
    group = heads // kv_local
    mine = lax.axis_index(("pipe", "ctx"))
    marks = doc_ids.astype(BF16)
    keys = lax.all_gather(key_rows, ("pipe", "ctx"), axis=0, tiled=True)
    values = lax.all_gather(value_rows, ("pipe", "ctx"), axis=0, tiled=True)
    key_doc = lax.all_gather(marks, ("pipe", "ctx"), axis=0, tiled=True).astype(jnp.int32)
    key_pos = jnp.arange(keys.shape[0], dtype=jnp.int32)
    half = rows // 2
    done = []
    for part in range(2):
        at = slice(part * half, (part + 1) * half)
        query = query_rows[at].reshape(half, kv_local, group, width)
        query_pos = mine * rows + part * half + jnp.arange(half, dtype=jnp.int32)
        scores = jnp.einsum("qjgd,kjd->qjgk", query, keys, preferred_element_type=F32)
        scores = scores * width**-0.5
        allowed = (key_pos[None, :] <= query_pos[:, None]) & (
            key_doc[None, :] == doc_ids[at][:, None]
        )
        allowed = allowed[:, None, None, :]
        masked = jnp.where(allowed, scores, -1e30)
        peak = jnp.max(masked, axis=3, keepdims=True)
        weights = jnp.where(allowed, jnp.exp(scores - peak), 0.0)
        total = jnp.sum(weights, axis=3)
        summed = jnp.einsum(
            "qjgk,kjd->qjgd", weights.astype(BF16), values, preferred_element_type=F32
        )
        done.append((summed / total[..., None]).astype(BF16).reshape(half, heads * width))
    flat = jnp.concatenate(done, axis=0)
    tp_size, ctx_size = lax.axis_size("tp"), lax.axis_size("ctx")
    quarter, columns = rows // tp_size, out_weight.shape[1]
    partial = jnp.dot(
        lax.all_gather(flat, "ctx", axis=0, tiled=True), out_weight, preferred_element_type=F32
    )
    partial = partial.reshape(ctx_size, tp_size, quarter, columns)
    summed = lax.psum_scatter(partial.astype(BF16), "tp", scatter_dimension=1, tiled=True)
    return summed.reshape(1, ctx_size, 1, quarter, columns)


def solution(mesh):
    sizes = dict(mesh.shape)
    on_line = sizes["tp"] == 4 and sizes["ctx"] == 2 and sizes["pipe"] == 4
    return jax.shard_map(
        shards_line if on_line else shards_any,
        mesh=mesh,
        in_specs=(
            P(("pipe", "ctx"), "tp", None),
            P(("pipe", "ctx"), "tp", None),
            P(("pipe", "ctx"), "tp", None),
            P(("pipe", "ctx")),
            P("tp", "ctx"),
        ),
        out_specs=P("pipe", None, "tp", None, "ctx"),
        check_vma=False,
    )
```

time: 151 us -> 88 us (0.58)
  blocking collectives: 45 us -> 0 us
  waiting for transfers between devices: 66.1 us -> 22.9 us
  starting transfers between devices: 0.22 us -> 31.3 us
  Pallas kernels: 0 us -> 22.1 us
  between operations: 14.8 us -> 0.17 us
  matrix products: 14.1 us -> 0 us
  local copies, waits for them, and re-layouts: 4.86 us -> 9.67 us
  other arithmetic: 5.33 us -> 1.38 us
    all_gather x3 -> x0, blocking collectives: 45 us -> none  [the longest x1 16.2 us: shards(): key_piece = lax.all_gather(key_rows, ('pipe', 'ctx'), axis=0, tiled=True)]
    reduce_scatter x1 -> x0, waiting for transfers between devices: 44 us -> none  [shards(): lax.psum_scatter(partial_value.astype(jnp.bfloat16), 'tp', scatter_dimens...]
    ppermute x0 -> x18, starting transfers between devices: none -> 31.3 us  [the longest x10 20.4 us: swap(): return lax.ppermute(value, 'tp', pairs)]
    ppermute x0 -> x18, waiting for transfers between devices: none -> 22.9 us  [the longest x10 12.1 us: swap(): return lax.ppermute(value, 'tp', pairs)]
    pallas_call x0 -> x5, Pallas kernels: none -> 22.1 us  [the longest x2 11.6 us: attend(): pl.pallas_call(functools.partial(attend_kernel, window, heads), out_shape...]
    all_gather x1 -> x0, waiting for transfers between devices: 22.1 us -> none  [shards(): lax.all_gather(flat_rows, 'ctx', axis=0, tiled=True)]
    dot_general x5 -> x0, matrix products: 14.1 us -> none  [the longest x1 10.6 us: shards(): jnp.dot(lax.all_gather(flat_rows, 'ctx', axis=0, tiled=True), out_weight,...]
    unnamed x4 -> x12, local copies, waits for them, and re-layouts: 0.14 us -> 8.98 us
  transfers between devices with their start and end apart: 2 -> 18, of which waited for: 2 -> 7; matrix products, arithmetic and copies ran while one was open for 0% -> 1% of each run, Pallas kernels for 0% -> 25%
where the time goes in v1:
time: 88 us; the launch traced here: 87.6 us
  starting transfers between devices  31.3 us (36%)
  waiting for transfers between devices  22.9 us (26%)
  Pallas kernels  22.1 us (25%)
  local copies, waits for them, and re-layouts  9.67 us (11%)
  other arithmetic  1.38 us (2%)
    ppermute x10, starting transfers between devices, swap(): return lax.ppermute(value, 'tp', pairs)  20.4 us
    ppermute x10, waiting for transfers between devices, swap(): return lax.ppermute(value, 'tp', pairs)  12.1 us
    pallas_call x2, Pallas kernels, attend(): pl.pallas_call(functools.partial(attend_kernel, window, heads), out_shape...  11.6 us
    ppermute x7, waiting for transfers between devices, shards_line(): lax.ppermute(packed, ('pipe', 'ctx'), [(i, i ^ m) for i in range(8)])  10.9 us
    pallas_call x2, Pallas kernels, project(): pl.pallas_call(project_kernel, grid=(columns // tile,), out_shape=[jax.Sh...  10.5 us
    unnamed x12, local copies, waits for them, and re-layouts  8.98 us
    ppermute x7, starting transfers between devices, shards_line(): lax.ppermute(packed, ('pipe', 'ctx'), [(i, i ^ m) for i in range(8)])  7.98 us
    ppermute x1, starting transfers between devices, shards_line(): other_query = lax.ppermute(query_rows, 'ctx', [(0, 1), (1, 0)])  2.97 us
  transfers between devices with their start and end apart: 18, of which 7 were waited for; matrix products, arithmetic and copies ran while one was open for 1% of the time, Pallas kernels for 25%

profile of v1, /device:TPU:0, one launch (start us, length us, event | category | flops | bytes accessed | tf_op | source)
XLA Modules:
  0.0 87.6 jit_solution(6591537999111630667)
XLA Ops:
  0.0 3.0 %collective-permute-start.12 = (bf16[128,16,128]{2,1,0:T(8,128)(2,1)}, bf16[128,16,128]{2,1,0:T(8,128)(2,1)S(1)}, u32[]{:S(2)}, u32[]{:S(2)}) collective-permute-start(bf16[128,16,128]{2,1,0:T(8,128)(2,1)} %param.6), channel_id=1, source_target_pairs={{0,4},{4,0},{1,5},{5,1},{2,6},{6,2},{3,7},{7,3},{8,12},{12,8},{9,1... | collective-permute-start | bytes 1572872 | tf_op jit(solution)/shard_map/ppermute | solution.py:161
  3.7 0.8 copy-done.3
  5.2 2.1 %collective-permute-start.2 = (bf16[272,128]{1,0:T(8,128)(2,1)S(1)}, bf16[272,128]{1,0:T(8,128)(2,1)S(1)}, u32[]{:S(2)}, u32[]{:S(2)}) collective-permute-start(bf16[272,128]{1,0:T(8,128)(2,1)S(1)} %shard_map.64.refs_0_), channel_id=1, source_target_pairs={{0,12},{4,8},{8,4},{12,0},{16,28},{20,24},{24,20},{28,16},{1,13},{... | collective-permute-start | bytes 208904 | tf_op jit(solution)/shard_map/ppermute | solution.py:159
  7.3 1.5 %collective-permute-start.3 = (bf16[272,128]{1,0:T(8,128)(2,1)S(1)}, bf16[272,128]{1,0:T(8,128)(2,1)S(1)}, u32[]{:S(2)}, u32[]{:S(2)}) collective-permute-start(bf16[272,128]{1,0:T(8,128)(2,1)S(1)} %shard_map.64.refs_0_), channel_id=1, source_target_pairs={{0,16},{4,20},{8,24},{12,28},{16,0},{20,4},{24,8},{28,12},{1,17},{... | collective-permute-start | bytes 208904 | tf_op jit(solution)/shard_map/ppermute | solution.py:159
  9.5 7.9 %collective-permute-done.refs_1_ = bf16[272,128]{1,0:T(8,128)(2,1)S(1)} collective-permute-done((bf16[272,128]{1,0:T(8,128)(2,1)S(1)}, bf16[272,128]{1,0:T(8,128)(2,1)S(1)}, u32[]{:S(2)}, u32[]{:S(2)}) %collective-permute-start) | collective-permute-done | bytes 69664 | tf_op jit(solution)/shard_map/ppermute | solution.py:159
  17.3 2.7 %collective-permute-start.4 = (bf16[272,128]{1,0:T(8,128)(2,1)S(1)}, bf16[272,128]{1,0:T(8,128)(2,1)S(1)}, u32[]{:S(2)}, u32[]{:S(2)}) collective-permute-start(bf16[272,128]{1,0:T(8,128)(2,1)S(1)} %shard_map.64.refs_0_), channel_id=1, source_target_pairs={{0,20},{4,16},{8,28},{12,24},{16,4},{20,0},{24,12},{28,8},{1,21},{... | collective-permute-start | bytes 208904 | tf_op jit(solution)/shard_map/ppermute | solution.py:159
  20.0 1.7 %collective-permute-start.6 = (bf16[272,128]{1,0:T(8,128)(2,1)S(1)}, bf16[272,128]{1,0:T(8,128)(2,1)S(1)}, u32[]{:S(2)}, u32[]{:S(2)}) collective-permute-start(bf16[272,128]{1,0:T(8,128)(2,1)S(1)} %shard_map.64.refs_0_), channel_id=1, source_target_pairs={{0,28},{4,24},{8,20},{12,16},{16,12},{20,8},{24,4},{28,0},{1,29},{... | collective-permute-start | bytes 208904 | tf_op jit(solution)/shard_map/ppermute | solution.py:159
  21.8 0.8 collective-permute-done.4.refs_5_
  22.6 1.9 %collective-permute-done.5.refs_6_ = bf16[272,128]{1,0:T(8,128)(2,1)S(1)} collective-permute-done((bf16[272,128]{1,0:T(8,128)(2,1)S(1)}, bf16[272,128]{1,0:T(8,128)(2,1)S(1)}, u32[]{:S(2)}, u32[]{:S(2)}) %collective-permute-start.5) | collective-permute-done | bytes 69664 | tf_op jit(solution)/shard_map/ppermute | solution.py:159
  24.8 1.0 %copy-done.5 = bf16[128,16,128]{2,1,0:T(8,128)(2,1)S(1)} copy-done((bf16[128,16,128]{2,1,0:T(8,128)(2,1)S(1)}, bf16[128,16,128]{2,1,0:T(8,128)(2,1)}, u32[]{:S(2)}) %copy-start.5) | copy-done | bytes 524312
  25.8 5.8 %shard_map.65.rows_ref = bf16[128,2048]{1,0:T(8,128)(2,1)S(1)} custom-call(s32[6]{0:T(128)S(1)} %get-tuple-element.24.info_ref, bf16[2048,128]{1,0:T(8,128)(2,1)S(1)} %bitcast.20, bf16[272,128]{1,0:T(8,128)(2,1)S(1)} %shard_map.64.refs_0_, bf16[272,128]{1,0:T(8,128)(2,1)S(1)} %collective-permute-done.refs_1_, ...), custom_call_target="tpu_custom_call" | custom-call | flops 671088640 | bytes 1048576 | tf_op jit(solution)/shard_map/pallas_call | solution.py:87
  31.7 5.8 %copy-done = bf16[2048,4096]{1,0:T(8,128)(2,1)S(1)} copy-done((bf16[2048,4096]{1,0:T(8,128)(2,1)S(1)}, bf16[2048,4096]{1,0:T(8,128)(2,1)}, u32[]{:S(2)}) %copy-start) | copy-done | bytes 16777240
  37.4 5.1 %shard_map.66 = (bf16[32,4096]{1,0:T(8,128)(2,1)S(1)}, bf16[32,4096]{1,0:T(8,128)(2,1)S(1)}, bf16[32,4096]{1,0:T(8,128)(2,1)S(1)}, bf16[32,4096]{1,0:T(8,128)(2,1)S(1)}) custom-call(bf16[128,2048]{1,0:T(8,128)(2,1)S(1)} %shard_map.65.rows_ref, bf16[2048,4096]{1,0:T(8,128)(2,1)S(1)} %copy-done), custom_call_target="tpu_custom_call" | custom-call | flops 2147483648 | bytes 16777216 | tf_op jit(solution)/shard_map/pallas_call | solution.py:120
  42.5 2.1 %collective-permute-start.7 = (bf16[32,4096]{1,0:T(8,128)(2,1)S(1)}, bf16[32,4096]{1,0:T(8,128)(2,1)S(1)}, u32[]{:S(2)}, u32[]{:S(2)}) collective-permute-start(bf16[32,4096]{1,0:T(8,128)(2,1)S(1)} %get-tuple-element.15), channel_id=1, source_target_pairs={{0,1},{1,0},{2,3},{3,2},{4,5},{5,4},{6,7},{7,6},{8,9},{9,8},{10,11... | collective-permute-start | bytes 786440 | tf_op jit(solution)/shard_map/ppermute | solution.py:140
  44.6 5.8 %shard_map.67.rows_ref = bf16[128,2048]{1,0:T(8,128)(2,1)S(1)} custom-call(s32[6]{0:T(128)S(1)} %get-tuple-element.23.info_ref, bf16[2048,128]{1,0:T(8,128)(2,1)S(1)} %bitcast.21, bf16[272,128]{1,0:T(8,128)(2,1)S(1)} %shard_map.64.refs_0_, bf16[272,128]{1,0:T(8,128)(2,1)S(1)} %collective-permute-done.refs_1_, ...), custom_call_target="tpu_custom_call" | custom-call | flops 671088640 | bytes 1048576 | tf_op jit(solution)/shard_map/pallas_call | solution.py:87
  50.4 5.4 %shard_map.68 = (bf16[32,4096]{1,0:T(8,128)(2,1)S(1)}, bf16[32,4096]{1,0:T(8,128)(2,1)S(1)}, bf16[32,4096]{1,0:T(8,128)(2,1)S(1)}, bf16[32,4096]{1,0:T(8,128)(2,1)S(1)}) custom-call(bf16[128,2048]{1,0:T(8,128)(2,1)S(1)} %shard_map.67.rows_ref, bf16[2048,4096]{1,0:T(8,128)(2,1)S(1)} %copy-done.1), custom_call_target="tpu_custom_call" | custom-call | flops 2147483648 | bytes 16777216 | tf_op jit(solution)/shard_map/pallas_call | solution.py:120
  55.9 2.0 %collective-permute-start.10 = (bf16[32,4096]{1,0:T(8,128)(2,1)S(1)}, bf16[32,4096]{1,0:T(8,128)(2,1)S(1)}, u32[]{:S(2)}, u32[]{:S(2)}) collective-permute-start(bf16[32,4096]{1,0:T(8,128)(2,1)S(1)} %get-tuple-element.16), channel_id=1, source_target_pairs={{0,1},{1,0},{2,3},{3,2},{4,5},{5,4},{6,7},{7,6},{8,9},{9,8},{10,11... | collective-permute-start | bytes 786440 | tf_op jit(solution)/shard_map/ppermute | solution.py:140
  58.7 4.4 %collective-permute-start.16 = (bf16[32,4096]{1,0:T(8,128)(2,1)S(1)}, bf16[32,4096]{1,0:T(8,128)(2,1)S(1)}, u32[]{:S(2)}, u32[]{:S(2)}) collective-permute-start(bf16[32,4096]{1,0:T(8,128)(2,1)S(1)} %get-tuple-element.20), channel_id=1, source_target_pairs={{0,1},{1,0},{2,3},{3,2},{4,5},{5,4},{6,7},{7,6},{8,9},{9,8},{10,11... | collective-permute-start | bytes 786440 | tf_op jit(solution)/shard_map/ppermute | solution.py:140
  63.0 2.0 %collective-permute-done.13 = bf16[32,4096]{1,0:T(8,128)(2,1)S(1)} collective-permute-done((bf16[32,4096]{1,0:T(8,128)(2,1)S(1)}, bf16[32,4096]{1,0:T(8,128)(2,1)S(1)}, u32[]{:S(2)}, u32[]{:S(2)}) %collective-permute-start.13) | collective-permute-done | bytes 262176 | tf_op jit(solution)/shard_map/ppermute | solution.py:140
  65.8 4.9 %collective-permute-done.10 = bf16[32,4096]{1,0:T(8,128)(2,1)S(1)} collective-permute-done((bf16[32,4096]{1,0:T(8,128)(2,1)S(1)}, bf16[32,4096]{1,0:T(8,128)(2,1)S(1)}, u32[]{:S(2)}, u32[]{:S(2)}) %collective-permute-start.10) | collective-permute-done | bytes 262176 | tf_op jit(solution)/shard_map/ppermute | solution.py:140
  71.5 4.4 %collective-permute-start.9 = (bf16[32,4096]{1,0:T(8,128)(2,1)S(1)}, bf16[32,4096]{1,0:T(8,128)(2,1)S(1)}, u32[]{:S(2)}, u32[]{:S(2)}) collective-permute-start(bf16[32,4096]{1,0:T(8,128)(2,1)S(1)} %add.39), channel_id=1, source_target_pairs={{0,1},{1,0},{2,3},{3,2},{4,5},{5,4},{6,7},{7,6},{8,9},{9,8},{10,11... | collective-permute-start | bytes 786440 | tf_op jit(solution)/shard_map/ppermute | solution.py:140
  76.7 4.8 %collective-permute-start.15 = (bf16[32,4096]{1,0:T(8,128)(2,1)S(1)}, bf16[32,4096]{1,0:T(8,128)(2,1)S(1)}, u32[]{:S(2)}, u32[]{:S(2)}) collective-permute-start(bf16[32,4096]{1,0:T(8,128)(2,1)S(1)} %add.44), channel_id=1, source_target_pairs={{0,1},{1,0},{2,3},{3,2},{4,5},{5,4},{6,7},{7,6},{8,9},{9,8},{10,11... | collective-permute-start | bytes 786440 | tf_op jit(solution)/shard_map/ppermute | solution.py:140
  81.5 5.2 %collective-permute-done.15 = bf16[32,4096]{1,0:T(8,128)(2,1)S(1)} collective-permute-done((bf16[32,4096]{1,0:T(8,128)(2,1)S(1)}, bf16[32,4096]{1,0:T(8,128)(2,1)S(1)}, u32[]{:S(2)}, u32[]{:S(2)}) %collective-permute-start.15) | collective-permute-done | bytes 262176 | tf_op jit(solution)/shard_map/ppermute | solution.py:140
  86.8 0.8 maximum_bitcast_fusion
  (39 shorter events, 5.9 us)
Async XLA Ops:
  0.0 44.6 %collective-permute-start.12 = (bf16[128,16,128]{2,1,0:T(8,128)(2,1)}, bf16[128,16,128]{2,1,0:T(8,128)(2,1)S(1)}, u32[]{:S(2)}, u32[]{:S(2)}) collective-permute-start(bf16[128,16,128]{2,1,0:T(8,128)(2,1)} %param.6), channel_id=1, source_target_pairs={{0,4},{4,0},{1,5},{5,1},{2,6},{6,2},{3,7},{7,3},{8,12},{12,8},{9,1... | collective-permute-start | bytes 1572872 | tf_op jit(solution)/shard_map/ppermute | solution.py:161
  3.0 0.8 copy-start.2
  3.7 0.8 copy-start.3
  4.5 0.7 copy-start.4
  5.1 12.2 %collective-permute-start = (bf16[272,128]{1,0:T(8,128)(2,1)S(1)}, bf16[272,128]{1,0:T(8,128)(2,1)S(1)}, u32[]{:S(2)}, u32[]{:S(2)}) collective-permute-start(bf16[272,128]{1,0:T(8,128)(2,1)S(1)} %shard_map.64.refs_0_), channel_id=1, source_target_pairs={{0,4},{4,0},{8,12},{12,8},{16,20},{20,16},{24,28},{28,24},{1,5},{5... | collective-permute-start | bytes 208904 | tf_op jit(solution)/shard_map/ppermute | solution.py:159
  5.2 14.9 %collective-permute-start.1 = (bf16[272,128]{1,0:T(8,128)(2,1)S(1)}, bf16[272,128]{1,0:T(8,128)(2,1)S(1)}, u32[]{:S(2)}, u32[]{:S(2)}) collective-permute-start(bf16[272,128]{1,0:T(8,128)(2,1)S(1)} %shard_map.64.refs_0_), channel_id=1, source_target_pairs={{0,8},{4,12},{8,0},{12,4},{16,24},{20,28},{24,16},{28,20},{1,9},{5... | collective-permute-start | bytes 208904 | tf_op jit(solution)/shard_map/ppermute | solution.py:159
  5.2 14.8 %collective-permute-start.2 = (bf16[272,128]{1,0:T(8,128)(2,1)S(1)}, bf16[272,128]{1,0:T(8,128)(2,1)S(1)}, u32[]{:S(2)}, u32[]{:S(2)}) collective-permute-start(bf16[272,128]{1,0:T(8,128)(2,1)S(1)} %shard_map.64.refs_0_), channel_id=1, source_target_pairs={{0,12},{4,8},{8,4},{12,0},{16,28},{20,24},{24,20},{28,16},{1,13},{... | collective-permute-start | bytes 208904 | tf_op jit(solution)/shard_map/ppermute | solution.py:159
  7.3 14.5 %collective-permute-start.3 = (bf16[272,128]{1,0:T(8,128)(2,1)S(1)}, bf16[272,128]{1,0:T(8,128)(2,1)S(1)}, u32[]{:S(2)}, u32[]{:S(2)}) collective-permute-start(bf16[272,128]{1,0:T(8,128)(2,1)S(1)} %shard_map.64.refs_0_), channel_id=1, source_target_pairs={{0,16},{4,20},{8,24},{12,28},{16,0},{20,4},{24,8},{28,12},{1,17},{... | collective-permute-start | bytes 208904 | tf_op jit(solution)/shard_map/ppermute | solution.py:159
  17.3 5.2 %collective-permute-start.4 = (bf16[272,128]{1,0:T(8,128)(2,1)S(1)}, bf16[272,128]{1,0:T(8,128)(2,1)S(1)}, u32[]{:S(2)}, u32[]{:S(2)}) collective-permute-start(bf16[272,128]{1,0:T(8,128)(2,1)S(1)} %shard_map.64.refs_0_), channel_id=1, source_target_pairs={{0,20},{4,16},{8,28},{12,24},{16,4},{20,0},{24,12},{28,8},{1,21},{... | collective-permute-start | bytes 208904 | tf_op jit(solution)/shard_map/ppermute | solution.py:159
  20.0 4.5 %collective-permute-start.5 = (bf16[272,128]{1,0:T(8,128)(2,1)S(1)}, bf16[272,128]{1,0:T(8,128)(2,1)S(1)}, u32[]{:S(2)}, u32[]{:S(2)}) collective-permute-start(bf16[272,128]{1,0:T(8,128)(2,1)S(1)} %shard_map.64.refs_0_), channel_id=1, source_target_pairs={{0,24},{4,28},{8,16},{12,20},{16,8},{20,12},{24,0},{28,4},{1,25},{... | collective-permute-start | bytes 208904 | tf_op jit(solution)/shard_map/ppermute | solution.py:159
  20.0 4.8 %collective-permute-start.6 = (bf16[272,128]{1,0:T(8,128)(2,1)S(1)}, bf16[272,128]{1,0:T(8,128)(2,1)S(1)}, u32[]{:S(2)}, u32[]{:S(2)}) collective-permute-start(bf16[272,128]{1,0:T(8,128)(2,1)S(1)} %shard_map.64.refs_0_), channel_id=1, source_target_pairs={{0,28},{4,24},{8,20},{12,16},{16,12},{20,8},{24,4},{28,0},{1,29},{... | collective-permute-start | bytes 208904 | tf_op jit(solution)/shard_map/ppermute | solution.py:159
  24.8 1.0 %copy-start.5 = (bf16[128,16,128]{2,1,0:T(8,128)(2,1)S(1)}, bf16[128,16,128]{2,1,0:T(8,128)(2,1)}, u32[]{:S(2)}) copy-start(bf16[128,16,128]{2,1,0:T(8,128)(2,1)} %param.6) | copy-start | bytes 1572868
  31.6 5.8 %copy-start = (bf16[2048,4096]{1,0:T(8,128)(2,1)S(1)}, bf16[2048,4096]{1,0:T(8,128)(2,1)}, u32[]{:S(2)}) copy-start(bf16[2048,4096]{1,0:T(8,128)(2,1)} %weight_ref.3) | copy-start | bytes 50331652
  37.4 13.0 %copy-start.1 = (bf16[2048,4096]{1,0:T(8,128)(2,1)S(1)}, bf16[2048,4096]{1,0:T(8,128)(2,1)}, u32[]{:S(2)}) copy-start(bf16[2048,4096]{1,0:T(8,128)(2,1)} %weight_ref.3) | copy-start | bytes 50331652
  42.5 15.4 %collective-permute-start.7 = (bf16[32,4096]{1,0:T(8,128)(2,1)S(1)}, bf16[32,4096]{1,0:T(8,128)(2,1)S(1)}, u32[]{:S(2)}, u32[]{:S(2)}) collective-permute-start(bf16[32,4096]{1,0:T(8,128)(2,1)S(1)} %get-tuple-element.15), channel_id=1, source_target_pairs={{0,1},{1,0},{2,3},{3,2},{4,5},{5,4},{6,7},{7,6},{8,9},{9,8},{10,11... | collective-permute-start | bytes 786440 | tf_op jit(solution)/shard_map/ppermute | solution.py:140
  55.8 9.2 %collective-permute-start.13 = (bf16[32,4096]{1,0:T(8,128)(2,1)S(1)}, bf16[32,4096]{1,0:T(8,128)(2,1)S(1)}, u32[]{:S(2)}, u32[]{:S(2)}) collective-permute-start(bf16[32,4096]{1,0:T(8,128)(2,1)S(1)} %get-tuple-element.19), channel_id=1, source_target_pairs={{0,1},{1,0},{2,3},{3,2},{4,5},{5,4},{6,7},{7,6},{8,9},{9,8},{10,11... | collective-permute-start | bytes 786440 | tf_op jit(solution)/shard_map/ppermute | solution.py:140
  55.9 14.7 %collective-permute-start.10 = (bf16[32,4096]{1,0:T(8,128)(2,1)S(1)}, bf16[32,4096]{1,0:T(8,128)(2,1)S(1)}, u32[]{:S(2)}, u32[]{:S(2)}) collective-permute-start(bf16[32,4096]{1,0:T(8,128)(2,1)S(1)} %get-tuple-element.16), channel_id=1, source_target_pairs={{0,1},{1,0},{2,3},{3,2},{4,5},{5,4},{6,7},{7,6},{8,9},{9,8},{10,11... | collective-permute-start | bytes 786440 | tf_op jit(solution)/shard_map/ppermute | solution.py:140
  58.0 13.4 %collective-permute-start.8 = (bf16[32,4096]{1,0:T(8,128)(2,1)S(1)}, bf16[32,4096]{1,0:T(8,128)(2,1)S(1)}, u32[]{:S(2)}, u32[]{:S(2)}) collective-permute-start(bf16[32,4096]{1,0:T(8,128)(2,1)S(1)} %add.38), channel_id=1, source_target_pairs={{1,2},{2,1},{5,6},{6,5},{9,10},{10,9},{13,14},{14,13},{17,18},{18,... | collective-permute-start | bytes 786440 | tf_op jit(solution)/shard_map/ppermute | solution.py:140
  58.7 17.2 %collective-permute-start.16 = (bf16[32,4096]{1,0:T(8,128)(2,1)S(1)}, bf16[32,4096]{1,0:T(8,128)(2,1)S(1)}, u32[]{:S(2)}, u32[]{:S(2)}) collective-permute-start(bf16[32,4096]{1,0:T(8,128)(2,1)S(1)} %get-tuple-element.20), channel_id=1, source_target_pairs={{0,1},{1,0},{2,3},{3,2},{4,5},{5,4},{6,7},{7,6},{8,9},{9,8},{10,11... | collective-permute-start | bytes 786440 | tf_op jit(solution)/shard_map/ppermute | solution.py:140
  65.1 11.5 %collective-permute-start.14 = (bf16[32,4096]{1,0:T(8,128)(2,1)S(1)}, bf16[32,4096]{1,0:T(8,128)(2,1)S(1)}, u32[]{:S(2)}, u32[]{:S(2)}) collective-permute-start(bf16[32,4096]{1,0:T(8,128)(2,1)S(1)} %add.43), channel_id=1, source_target_pairs={{1,2},{2,1},{5,6},{6,5},{9,10},{10,9},{13,14},{14,13},{17,18},{18,... | collective-permute-start | bytes 786440 | tf_op jit(solution)/shard_map/ppermute | solution.py:140
  70.7 10.7 %collective-permute-start.11 = (bf16[32,4096]{1,0:T(8,128)(2,1)S(1)}, bf16[32,4096]{1,0:T(8,128)(2,1)S(1)}, u32[]{:S(2)}, u32[]{:S(2)}) collective-permute-start(bf16[32,4096]{1,0:T(8,128)(2,1)S(1)} %add.41), channel_id=1, source_target_pairs={{1,2},{2,1},{5,6},{6,5},{9,10},{10,9},{13,14},{14,13},{17,18},{18,... | collective-permute-start | bytes 786440 | tf_op jit(solution)/shard_map/ppermute | solution.py:140
  71.5 10.0 %collective-permute-start.9 = (bf16[32,4096]{1,0:T(8,128)(2,1)S(1)}, bf16[32,4096]{1,0:T(8,128)(2,1)S(1)}, u32[]{:S(2)}, u32[]{:S(2)}) collective-permute-start(bf16[32,4096]{1,0:T(8,128)(2,1)S(1)} %add.39), channel_id=1, source_target_pairs={{0,1},{1,0},{2,3},{3,2},{4,5},{5,4},{6,7},{7,6},{8,9},{9,8},{10,11... | collective-permute-start | bytes 786440 | tf_op jit(solution)/shard_map/ppermute | solution.py:140
  75.9 5.6 %collective-permute-start.17 = (bf16[32,4096]{1,0:T(8,128)(2,1)S(1)}, bf16[32,4096]{1,0:T(8,128)(2,1)S(1)}, u32[]{:S(2)}, u32[]{:S(2)}) collective-permute-start(bf16[32,4096]{1,0:T(8,128)(2,1)S(1)} %add.46), channel_id=1, source_target_pairs={{1,2},{2,1},{5,6},{6,5},{9,10},{10,9},{13,14},{14,13},{17,18},{18,... | collective-permute-start | bytes 786440 | tf_op jit(solution)/shard_map/ppermute | solution.py:140
  76.7 10.0 %collective-permute-start.15 = (bf16[32,4096]{1,0:T(8,128)(2,1)S(1)}, bf16[32,4096]{1,0:T(8,128)(2,1)S(1)}, u32[]{:S(2)}, u32[]{:S(2)}) collective-permute-start(bf16[32,4096]{1,0:T(8,128)(2,1)S(1)} %add.44), channel_id=1, source_target_pairs={{0,1},{1,0},{2,3},{3,2},{4,5},{5,4},{6,7},{7,6},{8,9},{9,8},{10,11... | collective-permute-start | bytes 786440 | tf_op jit(solution)/shard_map/ppermute | solution.py:140

commit v2 on v1

v2 whole, which is shorter than its diff:
```python
import functools

import jax
import jax.numpy as jnp
from jax import lax
from jax.experimental import pallas as pl
from jax.experimental.pallas import tpu as pltpu
from jax.sharding import PartitionSpec as P

BF16 = jnp.bfloat16
F32 = jnp.float32
LOG2E = 1.4426950408889634
MIB = 1 << 20

WEIGHT_CUTS = 4
OUTER = ((0, 1), (1, 0), (2, 3), (3, 2))
INNER = ((1, 2), (2, 1))


def pin(value):
    return pltpu.with_memory_space_constraint(value, pltpu.HBM)


def pack_kernel(key_ref, value_ref, doc_ref, out_ref, marks, sems):
    rows = key_ref.shape[0]
    copies = [
        pltpu.make_async_copy(doc_ref, marks, sems.at[0]),
        pltpu.make_async_copy(key_ref, out_ref.at[pl.ds(0, rows)], sems.at[1]),
        pltpu.make_async_copy(value_ref, out_ref.at[pl.ds(rows, rows)], sems.at[2]),
    ]
    for copy in copies:
        copy.start()
    copies[0].wait()
    out_ref[2 * rows :] = jnp.broadcast_to(marks[...].astype(F32), (16, rows)).astype(BF16)
    copies[1].wait()
    copies[2].wait()


def pack(key_rows, value_rows, doc_ids):
    rows, _, width = key_rows.shape
    return pl.pallas_call(
        pack_kernel,
        out_shape=jax.ShapeDtypeStruct((2 * rows + 16, width), BF16),
        in_specs=[pl.BlockSpec(memory_space=pltpu.HBM)] * 3,
        out_specs=pl.BlockSpec(memory_space=pltpu.VMEM),
        scratch_shapes=[pltpu.VMEM((1, rows), jnp.int32), pltpu.SemaphoreType.DMA((3,))],
        compiler_params=pltpu.CompilerParams(vmem_limit_bytes=40 * MIB),
    )(
        *(
            pin(value)
            for value in (
                key_rows.reshape(rows, width),
                value_rows.reshape(rows, width),
                doc_ids.reshape(1, rows),
            )
        )
    )


def block_kernel(window, heads, flip, query_ref, weight_ref, *refs):
    blocks, outs = refs[:8], refs[8:-10]
    query_in, wide, query_all, keys, values, marks, bias, result, weight, sems = refs[-10:]
    rows, width = blocks[0].shape[0] // 2 - 8, blocks[0].shape[1]
    mine = lax.axis_index(("pipe", "ctx"))
    line = lax.axis_index("tp")
    asked = mine ^ flip
    columns = weight_ref.shape[1]
    tile = columns // WEIGHT_CUTS

    copies = [pltpu.make_async_copy(query_ref, query_in, sems.at[0])]
    for i in range(WEIGHT_CUTS):
        at = pl.ds(i * tile, tile)
        copies.append(pltpu.make_async_copy(weight_ref.at[:, at], weight.at[:, at], sems.at[1 + i]))
    for copy in copies:
        copy.start()

    keys[...] = jnp.zeros_like(keys)
    values[...] = jnp.zeros_like(values)
    marks[...] = jnp.full_like(marks, -1.0)
    for m in range(8):
        slot = (mine ^ m) - asked + window - 1

        @pl.when((slot >= 0) & (slot < window))
        def _(m=m, slot=slot):
            at = pl.ds(pl.multiple_of(slot * rows, rows), rows)
            keys[at, :] = blocks[m][:rows]
            values[at, :] = blocks[m][rows : 2 * rows]
            marks[slot] = blocks[m][2 * rows :].astype(F32)[:8]

    own = jnp.transpose(jnp.broadcast_to(marks[window - 1][:1], (rows, rows)))
    for s in range(window):
        allowed = own == marks[s][:1]
        if s == window - 1:
            at_row = lax.broadcasted_iota(jnp.int32, (rows, rows), 0)
            at_col = lax.broadcasted_iota(jnp.int32, (rows, rows), 1)
            allowed = allowed & (at_col <= at_row)
        bias[:, s * rows : (s + 1) * rows] = jnp.where(allowed, 0.0, -1e30)

    copies[0].wait()
    wide[...] = query_in[...].astype(F32)
    for h in range(heads):
        query_all[h * rows : (h + 1) * rows] = wide[pl.ds(h, rows, stride=heads), :].astype(BF16)

    quarter = rows // 4
    place = []
    for s in range(4):
        upper = jnp.where(s == line, 3, jnp.where(s > line, 3 - s, jnp.int32(2)))
        lower = jnp.where(s == line, 3, jnp.where(s < line, s, jnp.int32(2)))
        place.append(jnp.where(line < 2, upper, lower))

    factor = LOG2E * width**-0.5
    group = 4
    for g in range(heads // group):
        query = query_all[g * group * rows : (g + 1) * group * rows]
        scores = lax.dot_general(
            query, keys[...], (((1,), (1,)), ((), ())), preferred_element_type=F32
        )
        parts, totals = [], []
        for j in range(group):
            shifted = scores[j * rows : (j + 1) * rows] + bias[...]
            peak = jnp.max(shifted, axis=1, keepdims=True)
            weights = jnp.exp2((shifted - peak) * factor)
            totals.append(jnp.sum(weights, axis=1, keepdims=True))
            parts.append(weights.astype(BF16))
        summed = jnp.dot(
            jnp.concatenate(parts, axis=0), values[...], preferred_element_type=F32
        )
        for j in range(group):
            h = g * group + j
            done = (summed[j * rows : (j + 1) * rows] / totals[j]).astype(BF16)
            for s in range(4):
                at = pl.ds(pl.multiple_of(place[s] * quarter, quarter), quarter)
                result[at, h * width : (h + 1) * width] = done[s * quarter : (s + 1) * quarter]

    for i in range(WEIGHT_CUTS):
        copies[1 + i].wait()
        at = slice(i * tile, (i + 1) * tile)
        product = jnp.dot(result[...], weight[:, at], preferred_element_type=F32).astype(BF16)
        top = 0
        for out in outs:
            out[:, at] = product[top : top + out.shape[0]]
            top += out.shape[0]


def block(flip, query, blocks, weight, window, joined):
    rows, heads, width = query.shape
    depth, columns = weight.shape
    vmem = pl.BlockSpec(memory_space=pltpu.VMEM)
    quarter = rows // 4
    cuts = (2 * quarter, quarter, quarter) if joined else (quarter,) * 4
    place = pin if flip == 0 else lambda value: value
    return pl.pallas_call(
        functools.partial(block_kernel, window, heads, flip),
        out_shape=[jax.ShapeDtypeStruct((cut, columns), BF16) for cut in cuts],
        in_specs=[
            pl.BlockSpec(memory_space=pl.ANY),
            pl.BlockSpec(memory_space=pltpu.HBM),
        ]
        + [vmem] * 8,
        out_specs=[vmem] * len(cuts),
        scratch_shapes=[
            pltpu.VMEM((rows * heads, width), BF16),
            pltpu.VMEM((rows * heads, width), F32),
            pltpu.VMEM((rows * heads, width), BF16),
            pltpu.VMEM((window * rows, width), BF16),
            pltpu.VMEM((window * rows, width), BF16),
            pltpu.VMEM((window, 8, rows), F32),
            pltpu.VMEM((rows, window * rows), F32),
            pltpu.VMEM((rows, depth), BF16),
            pltpu.VMEM((depth, columns), BF16),
            pltpu.SemaphoreType.DMA((1 + WEIGHT_CUTS,)),
        ],
        compiler_params=pltpu.CompilerParams(vmem_limit_bytes=40 * MIB),
        cost_estimate=pl.CostEstimate(
            flops=4 * rows * heads * window * rows * width + 2 * rows * depth * columns,
            bytes_accessed=2 * depth * columns,
            transcendentals=rows * heads * window * rows,
        ),
    )(
        place(query.reshape(rows * heads, width)),
        pin(weight),
        *blocks,
    )


def swap(value, pairs):
    return lax.ppermute(value, "tp", pairs)


def shards_line(query_rows, key_rows, value_rows, doc_ids, out_weight):
    rows, heads, width = query_rows.shape
    columns = out_weight.shape[1]
    window = 5
    packed = pack(key_rows, value_rows, doc_ids)
    blocks = [packed] + [
        lax.ppermute(packed, ("pipe", "ctx"), [(i, i ^ m) for i in range(8)]) for m in range(1, 8)
    ]
    query_after, *_ = lax.optimization_barrier((query_rows, *blocks))
    other_query = lax.ppermute(query_after, "ctx", [(0, 1), (1, 0)])

    early, third, kept = block(0, query_rows, blocks, out_weight, window, True)
    late_first, late_second, late_third, late_kept = block(
        1, other_query, blocks, out_weight, window, False
    )
    early_in, late_first = lax.optimization_barrier((swap(early, OUTER), late_first))
    far = swap(early + early_in, INNER)
    quarter = rows // 4
    third_in = swap(third + far[:quarter], OUTER)
    late_far = swap(late_first + swap(late_first, OUTER), INNER)
    second_in, third_in = lax.optimization_barrier((swap(late_second, OUTER), third_in))
    late_near = swap(late_second + second_in, INNER)
    own = kept + third_in + far[quarter:]
    other = late_kept + swap(late_third + late_far, OUTER) + late_near
    at_first = lax.axis_index("ctx") == 0
    both = jnp.stack([jnp.where(at_first, own, other), jnp.where(at_first, other, own)])
    return both.reshape(1, 2, 1, rows // 4, columns)


def shards_any(query_rows, key_rows, value_rows, doc_ids, out_weight):
    rows, heads, width = query_rows.shape
    kv_local = key_rows.shape[1]
    group = heads // kv_local
    mine = lax.axis_index(("pipe", "ctx"))
    marks = doc_ids.astype(BF16)
    keys = lax.all_gather(key_rows, ("pipe", "ctx"), axis=0, tiled=True)
    values = lax.all_gather(value_rows, ("pipe", "ctx"), axis=0, tiled=True)
    key_doc = lax.all_gather(marks, ("pipe", "ctx"), axis=0, tiled=True).astype(jnp.int32)
    key_pos = jnp.arange(keys.shape[0], dtype=jnp.int32)
    half = rows // 2
    done = []
    for part in range(2):
        at = slice(part * half, (part + 1) * half)
        query = query_rows[at].reshape(half, kv_local, group, width)
        query_pos = mine * rows + part * half + jnp.arange(half, dtype=jnp.int32)
        scores = jnp.einsum("qjgd,kjd->qjgk", query, keys, preferred_element_type=F32)
        scores = scores * width**-0.5
        allowed = (key_pos[None, :] <= query_pos[:, None]) & (
            key_doc[None, :] == doc_ids[at][:, None]
        )
        allowed = allowed[:, None, None, :]
        masked = jnp.where(allowed, scores, -1e30)
        peak = jnp.max(masked, axis=3, keepdims=True)
        weights = jnp.where(allowed, jnp.exp(scores - peak), 0.0)
        total = jnp.sum(weights, axis=3)
        summed = jnp.einsum(
            "qjgk,kjd->qjgd", weights.astype(BF16), values, preferred_element_type=F32
        )
        done.append((summed / total[..., None]).astype(BF16).reshape(half, heads * width))
    flat = jnp.concatenate(done, axis=0)
    tp_size, ctx_size = lax.axis_size("tp"), lax.axis_size("ctx")
    quarter, columns = rows // tp_size, out_weight.shape[1]
    partial = jnp.dot(
        lax.all_gather(flat, "ctx", axis=0, tiled=True), out_weight, preferred_element_type=F32
    )
    partial = partial.reshape(ctx_size, tp_size, quarter, columns)
    summed = lax.psum_scatter(partial.astype(BF16), "tp", scatter_dimension=1, tiled=True)
    return summed.reshape(1, ctx_size, 1, quarter, columns)


def solution(mesh):
    sizes = dict(mesh.shape)
    on_line = sizes["tp"] == 4 and sizes["ctx"] == 2 and sizes["pipe"] == 4
    return jax.shard_map(
        shards_line if on_line else shards_any,
        mesh=mesh,
        in_specs=(
            P(("pipe", "ctx"), "tp", None),
            P(("pipe", "ctx"), "tp", None),
            P(("pipe", "ctx"), "tp", None),
            P(("pipe", "ctx")),
            P("tp", "ctx"),
        ),
        out_specs=P("pipe", None, "tp", None, "ctx"),
        check_vma=False,
    )
```

time: 88 us -> 69.8 us (0.79)
  the two profiles are of different devices: /device:TPU:0 before, /device:TPU:18 now
where the time goes in v2:
time: 69.8 us; the launch traced here: 69.5 us
  waiting for transfers between devices  33.9 us (49%)
  starting transfers between devices  19.9 us (29%)
  Pallas kernels  14.4 us (21%)
  other arithmetic  1.26 us (2%)
    ppermute x8, waiting for transfers between devices, swap(): return lax.ppermute(value, 'tp', pairs)  25.1 us
    pallas_call x2, Pallas kernels, block(): pl.pallas_call(functools.partial(block_kernel, window, heads, flip), out_...  13.5 us
    ppermute x8, starting transfers between devices, swap(): return lax.ppermute(value, 'tp', pairs)  11.9 us
    ppermute x7, starting transfers between devices, shards_line(): lax.ppermute(packed, ('pipe', 'ctx'), [(i, i ^ m) for i in range(8)])  6.59 us
    ppermute x7, waiting for transfers between devices, shards_line(): lax.ppermute(packed, ('pipe', 'ctx'), [(i, i ^ m) for i in range(8)])  4.82 us
    ppermute x1, waiting for transfers between devices, shards_line(): other_query = lax.ppermute(query_after, 'ctx', [(0, 1), (1, 0)])  3.92 us
    ppermute x1, starting transfers between devices, shards_line(): other_query = lax.ppermute(query_after, 'ctx', [(0, 1), (1, 0)])  1.47 us
  transfers between devices with their start and end apart: 16, of which 13 were waited for; matrix products, arithmetic and copies ran while one was open for 0% of the time, Pallas kernels for 19%

profile of v2, /device:TPU:18, one launch (start us, length us, event | category | flops | bytes accessed | tf_op | source)
XLA Modules:
  0.0 69.5 jit_solution(6504005069853491828)
XLA Ops:
  0.0 0.8 %shard_map.55.refs_0_ = bf16[272,128]{1,0:T(8,128)(2,1)S(1)} custom-call(bf16[128,128]{1,0:T(8,128)(2,1)} %bitcast.15, bf16[128,128]{1,0:T(8,128)(2,1)} %bitcast.16, s32[1,128]{1,0:T(1,128)} %bitcast.17), custom_call_target="tpu_custom_call" | custom-call | tf_op jit(solution)/shard_map/pallas_call | solution.py:41
  0.8 1.0 %collective-permute-start.6 = (bf16[272,128]{1,0:T(8,128)(2,1)S(1)}, bf16[272,128]{1,0:T(8,128)(2,1)S(1)}, u32[]{:S(2)}, u32[]{:S(2)}) collective-permute-start(bf16[272,128]{1,0:T(8,128)(2,1)S(1)} %shard_map.55.refs_0_), channel_id=1, source_target_pairs={{0,28},{4,24},{8,20},{12,16},{16,12},{20,8},{24,4},{28,0},{1,29},{... | collective-permute-start | bytes 208904 | tf_op jit(solution)/shard_map/ppermute | solution.py:196
  1.8 1.8 %collective-permute-start.5 = (bf16[272,128]{1,0:T(8,128)(2,1)S(1)}, bf16[272,128]{1,0:T(8,128)(2,1)S(1)}, u32[]{:S(2)}, u32[]{:S(2)}) collective-permute-start(bf16[272,128]{1,0:T(8,128)(2,1)S(1)} %shard_map.55.refs_0_), channel_id=1, source_target_pairs={{0,24},{4,28},{8,16},{12,20},{16,8},{20,12},{24,0},{28,4},{1,25},{... | collective-permute-start | bytes 208904 | tf_op jit(solution)/shard_map/ppermute | solution.py:196
  4.1 1.5 %collective-permute-start.3 = (bf16[272,128]{1,0:T(8,128)(2,1)S(1)}, bf16[272,128]{1,0:T(8,128)(2,1)S(1)}, u32[]{:S(2)}, u32[]{:S(2)}) collective-permute-start(bf16[272,128]{1,0:T(8,128)(2,1)S(1)} %shard_map.55.refs_0_), channel_id=1, source_target_pairs={{0,16},{4,20},{8,24},{12,28},{16,0},{20,4},{24,8},{28,12},{1,17},{... | collective-permute-start | bytes 208904 | tf_op jit(solution)/shard_map/ppermute | solution.py:196
  6.3 0.9 %collective-permute-start.1 = (bf16[272,128]{1,0:T(8,128)(2,1)S(1)}, bf16[272,128]{1,0:T(8,128)(2,1)S(1)}, u32[]{:S(2)}, u32[]{:S(2)}) collective-permute-start(bf16[272,128]{1,0:T(8,128)(2,1)S(1)} %shard_map.55.refs_0_), channel_id=1, source_target_pairs={{0,8},{4,12},{8,0},{12,4},{16,24},{20,28},{24,16},{28,20},{1,9},{5... | collective-permute-start | bytes 208904 | tf_op jit(solution)/shard_map/ppermute | solution.py:196
  8.3 1.3 %collective-permute-done.4.refs_5_ = bf16[272,128]{1,0:T(8,128)(2,1)S(1)} collective-permute-done((bf16[272,128]{1,0:T(8,128)(2,1)S(1)}, bf16[272,128]{1,0:T(8,128)(2,1)S(1)}, u32[]{:S(2)}, u32[]{:S(2)}) %collective-permute-start.4) | collective-permute-done | bytes 69664 | tf_op jit(solution)/shard_map/ppermute | solution.py:196
  9.6 1.2 %collective-permute-done.3.refs_4_ = bf16[272,128]{1,0:T(8,128)(2,1)S(1)} collective-permute-done((bf16[272,128]{1,0:T(8,128)(2,1)S(1)}, bf16[272,128]{1,0:T(8,128)(2,1)S(1)}, u32[]{:S(2)}, u32[]{:S(2)}) %collective-permute-start.3) | collective-permute-done | bytes 69664 | tf_op jit(solution)/shard_map/ppermute | solution.py:196
  10.8 1.4 %collective-permute-done.refs_1_ = bf16[272,128]{1,0:T(8,128)(2,1)S(1)} collective-permute-done((bf16[272,128]{1,0:T(8,128)(2,1)S(1)}, bf16[272,128]{1,0:T(8,128)(2,1)S(1)}, u32[]{:S(2)}, u32[]{:S(2)}) %collective-permute-start) | collective-permute-done | bytes 69664 | tf_op jit(solution)/shard_map/ppermute | solution.py:196
  12.2 1.5 %collective-permute-start.7 = (bf16[128,16,128]{2,1,0:T(8,128)(2,1)}, bf16[128,16,128]{2,1,0:T(8,128)(2,1)S(1)}, u32[]{:S(2)}, u32[]{:S(2)}) collective-permute-start(bf16[128,16,128]{2,1,0:T(8,128)(2,1)} %param.5), channel_id=1, source_target_pairs={{0,4},{4,0},{1,5},{5,1},{2,6},{6,2},{3,7},{7,3},{8,12},{12,8},{9,1... | collective-permute-start | bytes 1572872 | tf_op jit(solution)/shard_map/ppermute | solution.py:199
  13.7 6.8 %shard_map.56 = (bf16[64,4096]{1,0:T(8,128)(2,1)S(1)}, bf16[32,4096]{1,0:T(8,128)(2,1)S(1)}, bf16[32,4096]{1,0:T(8,128)(2,1)S(1)}) custom-call(bf16[2048,128]{1,0:T(8,128)(2,1)} %bitcast.14, bf16[2048,4096]{1,0:T(8,128)(2,1)} %weight_ref.3, bf16[272,128]{1,0:T(8,128)(2,1)S(1)} %shard_map.55.refs_0_, bf16[272,128]{1,0:T(8,128)(2,1)S(1)} %collective-permute-done.refs_1_, ...), custom_call_target="tpu_custom_call" | custom-call | flops 2818572288 | bytes 16777216 | tf_op jit(solution)/shard_map/pallas_call | solution.py:152
  20.6 1.6 %collective-permute-start.9 = (bf16[64,4096]{1,0:T(8,128)(2,1)S(1)}, bf16[64,4096]{1,0:T(8,128)(2,1)S(1)}, u32[]{:S(2)}, u32[]{:S(2)}) collective-permute-start(bf16[64,4096]{1,0:T(8,128)(2,1)S(1)} %get-tuple-element.21), channel_id=1, source_target_pairs={{0,1},{1,0},{2,3},{3,2},{4,5},{5,4},{6,7},{7,6},{8,9},{9,8},{10,11... | collective-permute-start | bytes 1572872 | tf_op jit(solution)/shard_map/ppermute | solution.py:187
  22.2 3.9 %collective-permute-done.7 = bf16[128,16,128]{2,1,0:T(8,128)(2,1)S(1)} collective-permute-done((bf16[128,16,128]{2,1,0:T(8,128)(2,1)}, bf16[128,16,128]{2,1,0:T(8,128)(2,1)S(1)}, u32[]{:S(2)}, u32[]{:S(2)}) %collective-permute-start.7) | collective-permute-done | bytes 524320 | tf_op jit(solution)/shard_map/ppermute | solution.py:199
  26.1 6.7 %shard_map.57 = (bf16[32,4096]{1,0:T(8,128)(2,1)S(1)}, bf16[32,4096]{1,0:T(8,128)(2,1)S(1)}, bf16[32,4096]{1,0:T(8,128)(2,1)S(1)}, bf16[32,4096]{1,0:T(8,128)(2,1)S(1)}) custom-call(bf16[2048,128]{1,0:T(8,128)(2,1)S(1)} %bitcast.13, bf16[2048,4096]{1,0:T(8,128)(2,1)} %weight_ref.3, bf16[272,128]{1,0:T(8,128)(2,1)S(1)} %shard_map.55.refs_0_, ...), custom_call_target="tpu_custom_call" | custom-call | flops 2818572288 | bytes 16777216 | tf_op jit(solution)/shard_map/pallas_call | solution.py:152
  32.8 1.5 %collective-permute-done.9 = bf16[64,4096]{1,0:T(8,128)(2,1)S(1)} collective-permute-done((bf16[64,4096]{1,0:T(8,128)(2,1)S(1)}, bf16[64,4096]{1,0:T(8,128)(2,1)S(1)}, u32[]{:S(2)}, u32[]{:S(2)}) %collective-permute-start.9) | collective-permute-done | bytes 524320 | tf_op jit(solution)/shard_map/ppermute | solution.py:187
  34.4 2.4 %collective-permute-start.10 = (bf16[64,4096]{1,0:T(8,128)(2,1)S(1)}, bf16[64,4096]{1,0:T(8,128)(2,1)S(1)}, u32[]{:S(2)}, u32[]{:S(2)}) collective-permute-start(bf16[64,4096]{1,0:T(8,128)(2,1)S(1)} %add.27), channel_id=1, source_target_pairs={{1,2},{2,1},{5,6},{6,5},{9,10},{10,9},{13,14},{14,13},{17,18},{18,... | collective-permute-start | bytes 1572872 | tf_op jit(solution)/shard_map/ppermute | solution.py:187
  36.9 2.0 %collective-permute-start.8 = (bf16[32,4096]{1,0:T(8,128)(2,1)S(1)}, bf16[32,4096]{1,0:T(8,128)(2,1)S(1)}, u32[]{:S(2)}, u32[]{:S(2)}) collective-permute-start(bf16[32,4096]{1,0:T(8,128)(2,1)S(1)} %get-tuple-element.19), channel_id=1, source_target_pairs={{0,1},{1,0},{2,3},{3,2},{4,5},{5,4},{6,7},{7,6},{8,9},{9,8},{10,11... | collective-permute-start | bytes 786440 | tf_op jit(solution)/shard_map/ppermute | solution.py:187
  38.9 7.2 %collective-permute-done.12 = bf16[32,4096]{1,0:T(8,128)(2,1)S(1)} collective-permute-done((bf16[32,4096]{1,0:T(8,128)(2,1)S(1)}, bf16[32,4096]{1,0:T(8,128)(2,1)S(1)}, u32[]{:S(2)}, u32[]{:S(2)}) %collective-permute-start.12) | collective-permute-done | bytes 262176 | tf_op jit(solution)/shard_map/ppermute | solution.py:187
  46.1 3.5 %collective-permute-start.13 = (bf16[32,4096]{1,0:T(8,128)(2,1)S(1)}, bf16[32,4096]{1,0:T(8,128)(2,1)S(1)}, u32[]{:S(2)}, u32[]{:S(2)}) collective-permute-start(bf16[32,4096]{1,0:T(8,128)(2,1)S(1)} %add.31), channel_id=1, source_target_pairs={{1,2},{2,1},{5,6},{6,5},{9,10},{10,9},{13,14},{14,13},{17,18},{18,... | collective-permute-start | bytes 786440 | tf_op jit(solution)/shard_map/ppermute | solution.py:187
  49.6 1.5 %collective-permute-done.10 = bf16[64,4096]{1,0:T(8,128)(2,1)S(1)} collective-permute-done((bf16[64,4096]{1,0:T(8,128)(2,1)S(1)}, bf16[64,4096]{1,0:T(8,128)(2,1)S(1)}, u32[]{:S(2)}, u32[]{:S(2)}) %collective-permute-start.10) | collective-permute-done | bytes 524320 | tf_op jit(solution)/shard_map/ppermute | solution.py:187
  51.3 3.4 %collective-permute-done.13 = bf16[32,4096]{1,0:T(8,128)(2,1)S(1)} collective-permute-done((bf16[32,4096]{1,0:T(8,128)(2,1)S(1)}, bf16[32,4096]{1,0:T(8,128)(2,1)S(1)}, u32[]{:S(2)}, u32[]{:S(2)}) %collective-permute-start.13) | collective-permute-done | bytes 262176 | tf_op jit(solution)/shard_map/ppermute | solution.py:187
  54.9 5.4 %collective-permute-done.11 = bf16[32,4096]{1,0:T(8,128)(2,1)S(1)} collective-permute-done((bf16[32,4096]{1,0:T(8,128)(2,1)S(1)}, bf16[32,4096]{1,0:T(8,128)(2,1)S(1)}, u32[]{:S(2)}, u32[]{:S(2)}) %collective-permute-start.11) | collective-permute-done | bytes 262176 | tf_op jit(solution)/shard_map/ppermute | solution.py:187
  60.3 2.1 %collective-permute-start.15 = (bf16[32,4096]{1,0:T(8,128)(2,1)S(1)}, bf16[32,4096]{1,0:T(8,128)(2,1)S(1)}, u32[]{:S(2)}, u32[]{:S(2)}) collective-permute-start(bf16[32,4096]{1,0:T(8,128)(2,1)S(1)} %add.34), channel_id=1, source_target_pairs={{1,2},{2,1},{5,6},{6,5},{9,10},{10,9},{13,14},{14,13},{17,18},{18,... | collective-permute-start | bytes 786440 | tf_op jit(solution)/shard_map/ppermute | solution.py:187
  63.3 5.4 %collective-permute-done.15 = bf16[32,4096]{1,0:T(8,128)(2,1)S(1)} collective-permute-done((bf16[32,4096]{1,0:T(8,128)(2,1)S(1)}, bf16[32,4096]{1,0:T(8,128)(2,1)S(1)}, u32[]{:S(2)}, u32[]{:S(2)}) %collective-permute-start.15) | collective-permute-done | bytes 262176 | tf_op jit(solution)/shard_map/ppermute | solution.py:187
  68.7 0.8 %maximum_bitcast_fusion = bf16[1,2,1,32,4096]{4,3,2,1,0:T(8,128)(2,1)} fusion(bf16[1,32,4096]{2,1,0:T(8,128)(2,1)S(1)} %get-tuple-element.30, bf16[1,32,4096]{2,1,0:T(8,128)(2,1)S(1)} %get-tuple-element.29), kind=kLoop, calls=%fused_computation | loop fusion | flops 262144 | bytes 1048576 | tf_op jit(solution)/shard_map/reshape | solution.py:216
  (18 shorter events, 3.7 us)
Async XLA Ops:
  0.8 5.4 %collective-permute-start.6 = (bf16[272,128]{1,0:T(8,128)(2,1)S(1)}, bf16[272,128]{1,0:T(8,128)(2,1)S(1)}, u32[]{:S(2)}, u32[]{:S(2)}) collective-permute-start(bf16[272,128]{1,0:T(8,128)(2,1)S(1)} %shard_map.55.refs_0_), channel_id=1, source_target_pairs={{0,28},{4,24},{8,20},{12,16},{16,12},{20,8},{24,4},{28,0},{1,29},{... | collective-permute-start | bytes 208904 | tf_op jit(solution)/shard_map/ppermute | solution.py:196
  1.8 6.0 %collective-permute-start.5 = (bf16[272,128]{1,0:T(8,128)(2,1)S(1)}, bf16[272,128]{1,0:T(8,128)(2,1)S(1)}, u32[]{:S(2)}, u32[]{:S(2)}) collective-permute-start(bf16[272,128]{1,0:T(8,128)(2,1)S(1)} %shard_map.55.refs_0_), channel_id=1, source_target_pairs={{0,24},{4,28},{8,16},{12,20},{16,8},{20,12},{24,0},{28,4},{1,25},{... | collective-permute-start | bytes 208904 | tf_op jit(solution)/shard_map/ppermute | solution.py:196
  3.6 6.0 %collective-permute-start.4 = (bf16[272,128]{1,0:T(8,128)(2,1)S(1)}, bf16[272,128]{1,0:T(8,128)(2,1)S(1)}, u32[]{:S(2)}, u32[]{:S(2)}) collective-permute-start(bf16[272,128]{1,0:T(8,128)(2,1)S(1)} %shard_map.55.refs_0_), channel_id=1, source_target_pairs={{0,20},{4,16},{8,28},{12,24},{16,4},{20,0},{24,12},{28,8},{1,21},{... | collective-permute-start | bytes 208904 | tf_op jit(solution)/shard_map/ppermute | solution.py:196
  4.1 6.7 %collective-permute-start.3 = (bf16[272,128]{1,0:T(8,128)(2,1)S(1)}, bf16[272,128]{1,0:T(8,128)(2,1)S(1)}, u32[]{:S(2)}, u32[]{:S(2)}) collective-permute-start(bf16[272,128]{1,0:T(8,128)(2,1)S(1)} %shard_map.55.refs_0_), channel_id=1, source_target_pairs={{0,16},{4,20},{8,24},{12,28},{16,0},{20,4},{24,8},{28,12},{1,17},{... | collective-permute-start | bytes 208904 | tf_op jit(solution)/shard_map/ppermute | solution.py:196
  5.6 5.2 %collective-permute-start.2 = (bf16[272,128]{1,0:T(8,128)(2,1)S(1)}, bf16[272,128]{1,0:T(8,128)(2,1)S(1)}, u32[]{:S(2)}, u32[]{:S(2)}) collective-permute-start(bf16[272,128]{1,0:T(8,128)(2,1)S(1)} %shard_map.55.refs_0_), channel_id=1, source_target_pairs={{0,12},{4,8},{8,4},{12,0},{16,28},{20,24},{24,20},{28,16},{1,13},{... | collective-permute-start | bytes 208904 | tf_op jit(solution)/shard_map/ppermute | solution.py:196
  6.3 4.6 %collective-permute-start.1 = (bf16[272,128]{1,0:T(8,128)(2,1)S(1)}, bf16[272,128]{1,0:T(8,128)(2,1)S(1)}, u32[]{:S(2)}, u32[]{:S(2)}) collective-permute-start(bf16[272,128]{1,0:T(8,128)(2,1)S(1)} %shard_map.55.refs_0_), channel_id=1, source_target_pairs={{0,8},{4,12},{8,0},{12,4},{16,24},{20,28},{24,16},{28,20},{1,9},{5... | collective-permute-start | bytes 208904 | tf_op jit(solution)/shard_map/ppermute | solution.py:196
  7.8 4.4 %collective-permute-start = (bf16[272,128]{1,0:T(8,128)(2,1)S(1)}, bf16[272,128]{1,0:T(8,128)(2,1)S(1)}, u32[]{:S(2)}, u32[]{:S(2)}) collective-permute-start(bf16[272,128]{1,0:T(8,128)(2,1)S(1)} %shard_map.55.refs_0_), channel_id=1, source_target_pairs={{0,4},{4,0},{8,12},{12,8},{16,20},{20,16},{24,28},{28,24},{1,5},{5... | collective-permute-start | bytes 208904 | tf_op jit(solution)/shard_map/ppermute | solution.py:196
  12.2 13.9 %collective-permute-start.7 = (bf16[128,16,128]{2,1,0:T(8,128)(2,1)}, bf16[128,16,128]{2,1,0:T(8,128)(2,1)S(1)}, u32[]{:S(2)}, u32[]{:S(2)}) collective-permute-start(bf16[128,16,128]{2,1,0:T(8,128)(2,1)} %param.5), channel_id=1, source_target_pairs={{0,4},{4,0},{1,5},{5,1},{2,6},{6,2},{3,7},{7,3},{8,12},{12,8},{9,1... | collective-permute-start | bytes 1572872 | tf_op jit(solution)/shard_map/ppermute | solution.py:199
  20.6 13.7 %collective-permute-start.9 = (bf16[64,4096]{1,0:T(8,128)(2,1)S(1)}, bf16[64,4096]{1,0:T(8,128)(2,1)S(1)}, u32[]{:S(2)}, u32[]{:S(2)}) collective-permute-start(bf16[64,4096]{1,0:T(8,128)(2,1)S(1)} %get-tuple-element.21), channel_id=1, source_target_pairs={{0,1},{1,0},{2,3},{3,2},{4,5},{5,4},{6,7},{7,6},{8,9},{9,8},{10,11... | collective-permute-start | bytes 1572872 | tf_op jit(solution)/shard_map/ppermute | solution.py:187
  34.4 16.8 %collective-permute-start.10 = (bf16[64,4096]{1,0:T(8,128)(2,1)S(1)}, bf16[64,4096]{1,0:T(8,128)(2,1)S(1)}, u32[]{:S(2)}, u32[]{:S(2)}) collective-permute-start(bf16[64,4096]{1,0:T(8,128)(2,1)S(1)} %add.27), channel_id=1, source_target_pairs={{1,2},{2,1},{5,6},{6,5},{9,10},{10,9},{13,14},{14,13},{17,18},{18,... | collective-permute-start | bytes 1572872 | tf_op jit(solution)/shard_map/ppermute | solution.py:187
  36.8 9.3 %collective-permute-start.12 = (bf16[32,4096]{1,0:T(8,128)(2,1)S(1)}, bf16[32,4096]{1,0:T(8,128)(2,1)S(1)}, u32[]{:S(2)}, u32[]{:S(2)}) collective-permute-start(bf16[32,4096]{1,0:T(8,128)(2,1)S(1)} %get-tuple-element.27), channel_id=1, source_target_pairs={{0,1},{1,0},{2,3},{3,2},{4,5},{5,4},{6,7},{7,6},{8,9},{9,8},{10,11... | collective-permute-start | bytes 786440 | tf_op jit(solution)/shard_map/ppermute | solution.py:187
  36.9 18.0 %collective-permute-start.8 = (bf16[32,4096]{1,0:T(8,128)(2,1)S(1)}, bf16[32,4096]{1,0:T(8,128)(2,1)S(1)}, u32[]{:S(2)}, u32[]{:S(2)}) collective-permute-start(bf16[32,4096]{1,0:T(8,128)(2,1)S(1)} %get-tuple-element.19), channel_id=1, source_target_pairs={{0,1},{1,0},{2,3},{3,2},{4,5},{5,4},{6,7},{7,6},{8,9},{9,8},{10,11... | collective-permute-start | bytes 786440 | tf_op jit(solution)/shard_map/ppermute | solution.py:187
  46.1 8.6 %collective-permute-start.13 = (bf16[32,4096]{1,0:T(8,128)(2,1)S(1)}, bf16[32,4096]{1,0:T(8,128)(2,1)S(1)}, u32[]{:S(2)}, u32[]{:S(2)}) collective-permute-start(bf16[32,4096]{1,0:T(8,128)(2,1)S(1)} %add.31), channel_id=1, source_target_pairs={{1,2},{2,1},{5,6},{6,5},{9,10},{10,9},{13,14},{14,13},{17,18},{18,... | collective-permute-start | bytes 786440 | tf_op jit(solution)/shard_map/ppermute | solution.py:187
  51.2 9.1 %collective-permute-start.11 = (bf16[32,4096]{1,0:T(8,128)(2,1)S(1)}, bf16[32,4096]{1,0:T(8,128)(2,1)S(1)}, u32[]{:S(2)}, u32[]{:S(2)}) collective-permute-start(bf16[32,4096]{1,0:T(8,128)(2,1)S(1)} %slice_add_fusion.1), channel_id=1, source_target_pairs={{0,1},{1,0},{2,3},{3,2},{4,5},{5,4},{6,7},{7,6},{8,9},{9,8},{10,11... | collective-permute-start | bytes 786440 | tf_op jit(solution)/shard_map/ppermute | solution.py:187
  54.8 8.5 %collective-permute-start.14 = (bf16[32,4096]{1,0:T(8,128)(2,1)S(1)}, bf16[32,4096]{1,0:T(8,128)(2,1)S(1)}, u32[]{:S(2)}, u32[]{:S(2)}) collective-permute-start(bf16[32,4096]{1,0:T(8,128)(2,1)S(1)} %add.32), channel_id=1, source_target_pairs={{0,1},{1,0},{2,3},{3,2},{4,5},{5,4},{6,7},{7,6},{8,9},{9,8},{10,11... | collective-permute-start | bytes 786440 | tf_op jit(solution)/shard_map/ppermute | solution.py:187
  60.3 8.3 %collective-permute-start.15 = (bf16[32,4096]{1,0:T(8,128)(2,1)S(1)}, bf16[32,4096]{1,0:T(8,128)(2,1)S(1)}, u32[]{:S(2)}, u32[]{:S(2)}) collective-permute-start(bf16[32,4096]{1,0:T(8,128)(2,1)S(1)} %add.34), channel_id=1, source_target_pairs={{1,2},{2,1},{5,6},{6,5},{9,10},{10,9},{13,14},{14,13},{17,18},{18,... | collective-permute-start | bytes 786440 | tf_op jit(solution)/shard_map/ppermute | solution.py:187

commit v3 on v2

v3 whole, which is shorter than its diff:
```python
import functools

import jax
import jax.numpy as jnp
from jax import lax
from jax.experimental import pallas as pl
from jax.experimental.pallas import tpu as pltpu
from jax.sharding import PartitionSpec as P

BF16 = jnp.bfloat16
F32 = jnp.float32
LOG2E = 1.4426950408889634
MIB = 1 << 20

WEIGHT_CUTS = 4
OUTER = ((0, 1), (1, 0), (2, 3), (3, 2))
INNER = tuple(
    (p * 8 + c * 4 + t, p * 8 + c * 4 + 3 - t if t in (1, 2) else (p ^ 1) * 8 + c * 4 + t)
    for p in range(4)
    for c in range(2)
    for t in range(4)
)


def pin(value):
    return pltpu.with_memory_space_constraint(value, pltpu.HBM)


def pack_kernel(key_ref, value_ref, doc_ref, out_ref, marks, sems):
    rows = key_ref.shape[0]
    copies = [
        pltpu.make_async_copy(doc_ref, marks, sems.at[0]),
        pltpu.make_async_copy(key_ref, out_ref.at[pl.ds(0, rows)], sems.at[1]),
        pltpu.make_async_copy(value_ref, out_ref.at[pl.ds(rows, rows)], sems.at[2]),
    ]
    for copy in copies:
        copy.start()
    copies[0].wait()
    out_ref[2 * rows :] = jnp.broadcast_to(marks[...].astype(F32), (16, rows)).astype(BF16)
    copies[1].wait()
    copies[2].wait()


def pack(key_rows, value_rows, doc_ids):
    rows, _, width = key_rows.shape
    return pl.pallas_call(
        pack_kernel,
        out_shape=jax.ShapeDtypeStruct((2 * rows + 16, width), BF16),
        in_specs=[pl.BlockSpec(memory_space=pltpu.HBM)] * 3,
        out_specs=pl.BlockSpec(memory_space=pltpu.VMEM),
        scratch_shapes=[pltpu.VMEM((1, rows), jnp.int32), pltpu.SemaphoreType.DMA((3,))],
        compiler_params=pltpu.CompilerParams(vmem_limit_bytes=24 * MIB),
    )(
        *(
            pin(value)
            for value in (
                key_rows.reshape(rows, width),
                value_rows.reshape(rows, width),
                doc_ids.reshape(1, rows),
            )
        )
    )


def leaving(line):
    upper = line < 2
    inside = (line == 1) | (line == 2)
    return (
        jnp.where(upper, 3, 0),
        jnp.where(upper, 2, 1),
        jnp.where(inside, jnp.where(upper, 0, 3), jnp.where(upper, 1, 2)),
        line,
    )


def attend(window, heads, shards, query_all, blocks, scratch, result):
    keys, values, marks, own, bias = scratch
    rows, width = blocks[0].shape[0] // 2 - 8, blocks[0].shape[1]
    quarter = rows // 4
    half = 2 * quarter
    mine = lax.axis_index(("pipe", "ctx"))

    keys[...] = jnp.zeros_like(keys)
    values[...] = jnp.zeros_like(values)
    marks[...] = jnp.full_like(marks, -1.0)
    for m in range(8):
        slot = (mine ^ m) - mine + window - 1

        @pl.when((slot >= 0) & (slot < window))
        def _(m=m, slot=slot):
            at = pl.ds(pl.multiple_of(slot * rows, rows), rows)
            keys[at, :] = blocks[m][:rows]
            values[at, :] = blocks[m][rows : 2 * rows]
            marks[slot] = blocks[m][2 * rows :].astype(F32)[:8]

    own[...] = jnp.transpose(jnp.broadcast_to(marks[window - 1][:1], (rows, rows)))
    for i, shard in enumerate(shards):
        start = pl.multiple_of(shard * quarter, quarter)
        here = own[pl.ds(start, quarter), :]
        for s in range(window):
            allowed = here == marks[s][:1]
            if s == window - 1:
                at_row = lax.broadcasted_iota(jnp.int32, (quarter, rows), 0) + start
                at_col = lax.broadcasted_iota(jnp.int32, (quarter, rows), 1)
                allowed = allowed & (at_col <= at_row)
            bias[i * quarter : (i + 1) * quarter, s * rows : (s + 1) * rows] = jnp.where(
                allowed, 0.0, -1e30
            )

    factor = LOG2E * width**-0.5
    group = 8
    for g in range(heads // group):
        query = query_all[g * group * half : (g + 1) * group * half]
        scores = lax.dot_general(
            query, keys[...], (((1,), (1,)), ((), ())), preferred_element_type=F32
        )
        parts, totals = [], []
        for j in range(group):
            shifted = scores[j * half : (j + 1) * half] + bias[...]
            peak = jnp.max(shifted, axis=1, keepdims=True)
            weights = jnp.exp2((shifted - peak) * factor)
            totals.append(jnp.sum(weights, axis=1, keepdims=True))
            parts.append(weights.astype(BF16))
        summed = jnp.dot(
            jnp.concatenate(parts, axis=0), values[...], preferred_element_type=F32
        )
        for j in range(group):
            h = g * group + j
            done = (summed[j * half : (j + 1) * half] / totals[j]).astype(BF16)
            result[:, h * width : (h + 1) * width] = done


def project(rows, weight, outs):
    tile = weight.shape[1] // 4
    for i in range(4):
        at = slice(i * tile, (i + 1) * tile)
        product = jnp.dot(rows, weight[:, at], preferred_element_type=F32).astype(BF16)
        top = 0
        for out in outs:
            out[:, at] = product[top : top + out.shape[0]]
            top += out.shape[0]


def filled(rows):
    return jnp.concatenate([rows, jnp.zeros_like(rows)], axis=0)


def far_kernel(window, heads, query_ref, weight_ref, *refs):
    blocks, (rows_out, first, second), scratch = refs[:8], refs[8:11], refs[11:]
    shards = leaving(lax.axis_index("tp"))[:2]
    attend(window, heads, shards, query_ref, blocks, scratch, rows_out)
    project(filled(rows_out[...]), weight_ref, (first, second))


def near_kernel(window, heads, query_ref, *refs):
    shards = leaving(lax.axis_index("tp"))[2:]
    attend(window, heads, shards, query_ref, refs[:8], refs[9:], refs[8])


def attention_call(query, blocks, window, weight=None):
    width = query.shape[1]
    rows = blocks[0].shape[0] // 2 - 8
    half = rows // 2
    heads = query.shape[0] // half
    vmem = pl.BlockSpec(memory_space=pltpu.VMEM)
    scratch = [
        pltpu.VMEM((window * rows, width), BF16),
        pltpu.VMEM((window * rows, width), BF16),
        pltpu.VMEM((window, 8, rows), F32),
        pltpu.VMEM((rows, rows), F32),
        pltpu.VMEM((half, window * rows), F32),
    ]
    flops = 4 * half * heads * window * rows * width
    outs = [jax.ShapeDtypeStruct((half, heads * width), BF16)]
    given, specs = [query], [vmem]
    kernel = near_kernel
    if weight is not None:
        depth, columns = weight.shape
        outs += [jax.ShapeDtypeStruct((half // 2, columns), BF16)] * 2
        given.append(pltpu.with_memory_space_constraint(weight, pltpu.VMEM))
        specs.append(vmem)
        flops += 2 * half * depth * columns
        kernel = far_kernel
    return pl.pallas_call(
        functools.partial(kernel, window, heads),
        out_shape=outs,
        in_specs=specs + [vmem] * 8,
        out_specs=[vmem] * len(outs),
        scratch_shapes=scratch,
        compiler_params=pltpu.CompilerParams(vmem_limit_bytes=24 * MIB),
        cost_estimate=pl.CostEstimate(
            flops=flops, bytes_accessed=MIB, transcendentals=half * heads * window * rows
        ),
    )(*given, *blocks)


def project_kernel(count, *refs):
    weight_ref = refs[count]
    rows = [ref[...] for ref in refs[:count]]
    rows = filled(rows[0]) if count == 1 else jnp.concatenate(rows, axis=0)
    project(rows, weight_ref, refs[count + 1 :])


def project_call(parts, weight):
    depth, columns = weight.shape
    half = parts[0].shape[0]
    vmem = pl.BlockSpec(memory_space=pltpu.VMEM)
    outs = [jax.ShapeDtypeStruct((half // 2, columns), BF16)] * (2 * len(parts))
    return pl.pallas_call(
        functools.partial(project_kernel, len(parts)),
        out_shape=outs,
        in_specs=[vmem] * (len(parts) + 1),
        out_specs=[vmem] * len(outs),
        compiler_params=pltpu.CompilerParams(vmem_limit_bytes=24 * MIB),
        cost_estimate=pl.CostEstimate(
            flops=2 * half * len(parts) * depth * columns,
            bytes_accessed=2 * depth * columns,
            transcendentals=0,
        ),
    )(*parts, pltpu.with_memory_space_constraint(weight, pltpu.VMEM))


def load_kernel(heads, weight_ref, query_ref, out_ref, far_ref, near_ref, query_in, wide, sems):
    depth = weight_ref.shape[0] // WEIGHT_CUTS
    size = query_ref.shape[0] // 4
    half = 2 * size // heads
    copies = [
        pltpu.make_async_copy(
            query_ref.at[pl.ds(pl.multiple_of(shard * size, size), size)],
            query_in.at[pl.ds(i * size, size)],
            sems.at[i],
        )
        for i, shard in enumerate(leaving(lax.axis_index("tp")))
    ]
    for i in range(WEIGHT_CUTS):
        at = pl.ds(i * depth, depth)
        copies.append(pltpu.make_async_copy(weight_ref.at[at], out_ref.at[at], sems.at[4 + i]))
    for copy in copies:
        copy.start()
    for copy in copies[:4]:
        copy.wait()
    wide[...] = query_in[...].astype(F32)
    for part, ref in enumerate((far_ref, near_ref)):
        for h in range(heads):
            start = part * half * heads + h
            ref[h * half : (h + 1) * half] = wide[pl.ds(start, half, stride=heads), :].astype(BF16)
    for copy in copies[4:]:
        copy.wait()


def load(weight, query):
    rows, heads, width = query.shape
    hbm, vmem = pl.BlockSpec(memory_space=pltpu.HBM), pl.BlockSpec(memory_space=pltpu.VMEM)
    part = pltpu.VMEM((rows // 2 * heads, width), BF16)
    return pl.pallas_call(
        functools.partial(load_kernel, heads),
        out_shape=[pltpu.VMEM(weight.shape, weight.dtype), part, part],
        in_specs=[hbm, hbm],
        out_specs=[vmem] * 3,
        scratch_shapes=[
            pltpu.VMEM((rows * heads, width), BF16),
            pltpu.VMEM((rows * heads, width), F32),
            pltpu.SemaphoreType.DMA((4 + WEIGHT_CUTS,)),
        ],
        compiler_params=pltpu.CompilerParams(vmem_limit_bytes=24 * MIB),
        cost_estimate=pl.CostEstimate(flops=0, bytes_accessed=weight.size * 4, transcendentals=0),
    )(pin(weight), pin(query.reshape(rows * heads, width)))


def swap(value):
    return lax.ppermute(value, "tp", OUTER)


def swap_inner(value):
    return lax.ppermute(value, ("pipe", "ctx", "tp"), INNER)


def shards_line(query_rows, key_rows, value_rows, doc_ids, out_weight):
    rows, heads, width = query_rows.shape
    columns = out_weight.shape[1]
    window = 5
    packed = pack(key_rows, value_rows, doc_ids)

    def pair(value, m):
        return lax.ppermute(value, ("pipe", "ctx"), [(i, i ^ m) for i in range(8)])

    by_x, by_y, by_both = pair(packed, 4), pair(packed, 1), pair(packed, 5)
    by_core = pair(packed, 2)
    after = lax.optimization_barrier
    line = lax.axis_index("tp")
    weight_here, inside = after((out_weight, (line == 1) | (line == 2)))
    weight, far_query, near_query = load(weight_here, query_rows)
    by_x, by_both, by_y, weight = after((by_x, by_both, by_y, weight))
    blocks = [packed, by_y, by_core, pair(by_y, 2), by_x, by_both, pair(by_x, 2), pair(by_both, 2)]

    def trade(value):
        return lax.ppermute(value, "ctx", [(0, 1), (1, 0)])

    def passed(value):
        return jnp.where(inside, value, jnp.zeros_like(value))

    far_rows, first, second = attention_call(far_query, blocks, window, weight)
    near_query, far_rows = after((near_query, far_rows))
    (near_rows,) = attention_call(near_query, blocks, window)
    other_far, other_near = trade(far_rows), trade(near_rows)
    late_first, late_second = project_call([other_far], weight)
    third, kept, late_third, late_kept = project_call([near_rows, other_near], weight)

    far = swap_inner(first + swap(first))
    near = swap_inner(second + swap(second))
    late_far = swap_inner(late_first + swap(late_first))
    late_near = swap_inner(late_second + swap(late_second))
    own = kept + swap(third + passed(far)) + passed(near)
    other = late_kept + swap(late_third + passed(late_far)) + passed(late_near)
    quarter = rows // 4
    at_first = lax.axis_index("ctx") == 0
    both = jnp.stack([jnp.where(at_first, own, other), jnp.where(at_first, other, own)])
    return both.reshape(1, 2, 1, rows // 4, columns)


def shards_any(query_rows, key_rows, value_rows, doc_ids, out_weight):
    rows, heads, width = query_rows.shape
    kv_local = key_rows.shape[1]
    group = heads // kv_local
    mine = lax.axis_index(("pipe", "ctx"))
    marks = doc_ids.astype(BF16)
    keys = lax.all_gather(key_rows, ("pipe", "ctx"), axis=0, tiled=True)
    values = lax.all_gather(value_rows, ("pipe", "ctx"), axis=0, tiled=True)
    key_doc = lax.all_gather(marks, ("pipe", "ctx"), axis=0, tiled=True).astype(jnp.int32)
    key_pos = jnp.arange(keys.shape[0], dtype=jnp.int32)
    half = rows // 2
    done = []
    for part in range(2):
        at = slice(part * half, (part + 1) * half)
        query = query_rows[at].reshape(half, kv_local, group, width)
        query_pos = mine * rows + part * half + jnp.arange(half, dtype=jnp.int32)
        scores = jnp.einsum("qjgd,kjd->qjgk", query, keys, preferred_element_type=F32)
        scores = scores * width**-0.5
        allowed = (key_pos[None, :] <= query_pos[:, None]) & (
            key_doc[None, :] == doc_ids[at][:, None]
        )
        allowed = allowed[:, None, None, :]
        masked = jnp.where(allowed, scores, -1e30)
        peak = jnp.max(masked, axis=3, keepdims=True)
        weights = jnp.where(allowed, jnp.exp(scores - peak), 0.0)
        total = jnp.sum(weights, axis=3)
        summed = jnp.einsum(
            "qjgk,kjd->qjgd", weights.astype(BF16), values, preferred_element_type=F32
        )
        done.append((summed / total[..., None]).astype(BF16).reshape(half, heads * width))
    flat = jnp.concatenate(done, axis=0)
    tp_size, ctx_size = lax.axis_size("tp"), lax.axis_size("ctx")
    quarter, columns = rows // tp_size, out_weight.shape[1]
    partial = jnp.dot(
        lax.all_gather(flat, "ctx", axis=0, tiled=True), out_weight, preferred_element_type=F32
    )
    partial = partial.reshape(ctx_size, tp_size, quarter, columns)
    summed = lax.psum_scatter(partial.astype(BF16), "tp", scatter_dimension=1, tiled=True)
    return summed.reshape(1, ctx_size, 1, quarter, columns)


def solution(mesh):
    sizes = dict(mesh.shape)
    on_line = sizes["tp"] == 4 and sizes["ctx"] == 2 and sizes["pipe"] == 4
    return jax.shard_map(
        shards_line if on_line else shards_any,
        mesh=mesh,
        in_specs=(
            P(("pipe", "ctx"), "tp", None),
            P(("pipe", "ctx"), "tp", None),
            P(("pipe", "ctx"), "tp", None),
            P(("pipe", "ctx")),
            P("tp", "ctx"),
        ),
        out_specs=P("pipe", None, "tp", None, "ctx"),
        check_vma=False,
    )
```

time: 69.8 us -> 58.4 us (0.84)
  the two profiles are of different devices: /device:TPU:18 before, /device:TPU:0 now
where the time goes in v3:
time: 58.4 us; the launch traced here: 58.3 us
  starting transfers between devices  25.8 us (44%)
  Pallas kernels  17.3 us (30%)
  waiting for transfers between devices  13.6 us (23%)
  other arithmetic  1.27 us (2%)
    ppermute x6, starting transfers between devices, swap(): return lax.ppermute(value, 'tp', OUTER)  17.7 us
    ppermute x6, waiting for transfers between devices, swap(): return lax.ppermute(value, 'tp', OUTER)  9.61 us
    pallas_call x1, Pallas kernels, load(): pl.pallas_call(functools.partial(load_kernel, heads), out_shape=[pltpu.VM...  6.2 us
    pallas_call x2, Pallas kernels, attention_call(): pl.pallas_call(functools.partial(kernel, window, heads), out_shape=outs,...  5.63 us
    ppermute x7, starting transfers between devices, pair(): return lax.ppermute(value, ('pipe', 'ctx'), [(i, i ^ m) for i in range(8)])  5.63 us
    pallas_call x2, Pallas kernels, project_call(): pl.pallas_call(functools.partial(project_kernel, len(parts)), out_shape=o...  4.69 us
    ppermute x2, waiting for transfers between devices, trade(): return lax.ppermute(value, 'ctx', [(0, 1), (1, 0)])  3.12 us
    ppermute x2, starting transfers between devices, trade(): return lax.ppermute(value, 'ctx', [(0, 1), (1, 0)])  2.23 us
  transfers between devices with their start and end apart: 19, of which 7 were waited for; matrix products, arithmetic and copies ran while one was open for 1% of the time, Pallas kernels for 22%

profile of v3, /device:TPU:0, one launch (start us, length us, event | category | flops | bytes accessed | tf_op | source)
XLA Modules:
  0.0 58.3 jit_solution(10211006267856076286)
XLA Ops:
  0.0 0.8 %shard_map.56.refs_0_ = bf16[272,128]{1,0:T(8,128)(2,1)S(1)} custom-call(bf16[128,128]{1,0:T(8,128)(2,1)} %bitcast.13, bf16[128,128]{1,0:T(8,128)(2,1)} %bitcast.14, s32[1,128]{1,0:T(1,128)} %bitcast.15), custom_call_target="tpu_custom_call" | custom-call | tf_op jit(solution)/shard_map/pallas_call | solution.py:46
  0.8 3.0 %collective-permute-start = (bf16[272,128]{1,0:T(8,128)(2,1)S(1)}, bf16[272,128]{1,0:T(8,128)(2,1)S(1)}, u32[]{:S(2)}, u32[]{:S(2)}) collective-permute-start(bf16[272,128]{1,0:T(8,128)(2,1)S(1)} %shard_map.56.refs_0_), channel_id=1, source_target_pairs={{0,16},{4,20},{8,24},{12,28},{16,0},{20,4},{24,8},{28,12},{1,17},{... | collective-permute-start | bytes 208904 | tf_op jit(solution)/shard_map/ppermute | solution.py:285
  3.8 1.5 %collective-permute-start.1 = (bf16[272,128]{1,0:T(8,128)(2,1)S(1)}, bf16[272,128]{1,0:T(8,128)(2,1)S(1)}, u32[]{:S(2)}, u32[]{:S(2)}) collective-permute-start(bf16[272,128]{1,0:T(8,128)(2,1)S(1)} %shard_map.56.refs_0_), channel_id=1, source_target_pairs={{0,20},{4,16},{8,28},{12,24},{16,4},{20,0},{24,12},{28,8},{1,21},{... | collective-permute-start | bytes 208904 | tf_op jit(solution)/shard_map/ppermute | solution.py:285
  5.4 6.2 %shard_map.55 = (bf16[2048,4096]{1,0:T(8,128)(2,1)S(1)}, bf16[1024,128]{1,0:T(8,128)(2,1)S(1)}, bf16[1024,128]{1,0:T(8,128)(2,1)S(1)}) custom-call(bf16[2048,4096]{1,0:T(8,128)(2,1)} %weight_ref, bf16[2048,128]{1,0:T(8,128)(2,1)} %bitcast.12), custom_call_target="tpu_custom_call" | custom-call | bytes 33554432 | tf_op jit(solution)/shard_map/pallas_call | solution.py:255
  11.6 0.6 collective-permute-start.4
  12.3 0.4 collective-permute-start.6
  12.7 0.4 collective-permute-done.4.refs_3_
  13.1 0.4 collective-permute-done.5.refs_6_
  13.6 3.8 %shard_map.57 = (bf16[64,2048]{1,0:T(8,128)(2,1)S(1)}, bf16[32,4096]{1,0:T(8,128)(2,1)S(1)}, bf16[32,4096]{1,0:T(8,128)(2,1)S(1)}) custom-call(bf16[1024,128]{1,0:T(8,128)(2,1)S(1)} %get-tuple-element.27.query_ref, bf16[2048,4096]{1,0:T(8,128)(2,1)S(1)} %get-tuple-element.29.weight_ref.refs_2_.refs_1_, bf16[272,128]{1,0:T(8,128)(2,1)S(1)} %shard_map.56.refs_0_, ...), custom_call_target="tpu_custom_call" | custom-call | flops 1409286144 | bytes 1048576 | tf_op jit(solution)/shard_map/pallas_call | solution.py:184
  17.4 2.1 %collective-permute-start.13 = (bf16[64,2048]{1,0:T(8,128)(2,1)S(1)}, bf16[64,2048]{1,0:T(8,128)(2,1)S(1)}, u32[]{:S(2)}, u32[]{:S(2)}) collective-permute-start(bf16[64,2048]{1,0:T(8,128)(2,1)S(1)} %get-tuple-element.42), channel_id=1, source_target_pairs={{0,4},{4,0},{1,5},{5,1},{2,6},{6,2},{3,7},{7,3},{8,12},{12,8},{9,1... | collective-permute-start | bytes 786440 | tf_op jit(solution)/shard_map/ppermute | solution.py:297
  19.5 1.6 %collective-permute-start.8 = (bf16[32,4096]{1,0:T(8,128)(2,1)S(1)}, bf16[32,4096]{1,0:T(8,128)(2,1)S(1)}, u32[]{:S(2)}, u32[]{:S(2)}) collective-permute-start(bf16[32,4096]{1,0:T(8,128)(2,1)S(1)} %get-tuple-element.38), channel_id=1, source_target_pairs={{0,1},{1,0},{2,3},{3,2},{4,5},{5,4},{6,7},{7,6},{8,9},{9,8},{10,11... | collective-permute-start | bytes 786440 | tf_op jit(solution)/shard_map/ppermute | solution.py:271
  21.1 0.4 collective-permute-start.11
  21.5 1.8 %shard_map.58.refs_0_ = bf16[64,2048]{1,0:T(8,128)(2,1)S(1)} custom-call(bf16[1024,128]{1,0:T(8,128)(2,1)S(1)} %get-tuple-element.34.query_ref, bf16[272,128]{1,0:T(8,128)(2,1)S(1)} %shard_map.56.refs_0_, bf16[272,128]{1,0:T(8,128)(2,1)S(1)} %collective-permute-done.2.refs_1_, bf16[272,128]{1,0:T(8,128)(2,1)S(1)} %collective-permute-done.3.refs_2_, ...), custom_call_target="tpu_custom_call" | custom-call | flops 335544320 | bytes 1048576 | tf_op jit(solution)/shard_map/pallas_call | solution.py:184
  23.5 3.1 %collective-permute-done.13.refs_0_ = bf16[64,2048]{1,0:T(8,128)(2,1)S(1)} collective-permute-done((bf16[64,2048]{1,0:T(8,128)(2,1)S(1)}, bf16[64,2048]{1,0:T(8,128)(2,1)S(1)}, u32[]{:S(2)}, u32[]{:S(2)}) %collective-permute-start.13) | collective-permute-done | bytes 262176 | tf_op jit(solution)/shard_map/ppermute | solution.py:297
  26.6 2.4 %shard_map.60 = (bf16[32,4096]{1,0:T(8,128)(2,1)S(1)}, bf16[32,4096]{1,0:T(8,128)(2,1)S(1)}) custom-call(bf16[64,2048]{1,0:T(8,128)(2,1)S(1)} %collective-permute-done.13.refs_0_, bf16[2048,4096]{1,0:T(8,128)(2,1)S(1)} %get-tuple-element.29.weight_ref.refs_2_.refs_1_), custom_call_target="tpu_custom_call" | custom-call | flops 1073741824 | bytes 16777216 | tf_op jit(solution)/shard_map/pallas_call | solution.py:209
  29.0 2.1 %collective-permute-start.14 = (bf16[32,4096]{1,0:T(8,128)(2,1)S(1)}, bf16[32,4096]{1,0:T(8,128)(2,1)S(1)}, u32[]{:S(2)}, u32[]{:S(2)}) collective-permute-start(bf16[32,4096]{1,0:T(8,128)(2,1)S(1)} %get-tuple-element.43), channel_id=1, source_target_pairs={{0,1},{1,0},{2,3},{3,2},{4,5},{5,4},{6,7},{7,6},{8,9},{9,8},{10,11... | collective-permute-start | bytes 786440 | tf_op jit(solution)/shard_map/ppermute | solution.py:271
  31.3 3.0 %collective-permute-done.11 = bf16[32,4096]{1,0:T(8,128)(2,1)S(1)} collective-permute-done((bf16[32,4096]{1,0:T(8,128)(2,1)S(1)}, bf16[32,4096]{1,0:T(8,128)(2,1)S(1)}, u32[]{:S(2)}, u32[]{:S(2)}) %collective-permute-start.11) | collective-permute-done | bytes 262176 | tf_op jit(solution)/shard_map/ppermute | solution.py:271
  34.4 3.1 %collective-permute-start.17 = (bf16[32,4096]{1,0:T(8,128)(2,1)S(1)}, bf16[32,4096]{1,0:T(8,128)(2,1)S(1)}, u32[]{:S(2)}, u32[]{:S(2)}) collective-permute-start(bf16[32,4096]{1,0:T(8,128)(2,1)S(1)} %get-tuple-element.44), channel_id=1, source_target_pairs={{0,1},{1,0},{2,3},{3,2},{4,5},{5,4},{6,7},{7,6},{8,9},{9,8},{10,11... | collective-permute-start | bytes 786440 | tf_op jit(solution)/shard_map/ppermute | solution.py:271
  37.6 2.3 %shard_map.59 = (bf16[32,4096]{1,0:T(8,128)(2,1)S(1)}, bf16[32,4096]{1,0:T(8,128)(2,1)S(1)}, bf16[32,4096]{1,0:T(8,128)(2,1)S(1)}, bf16[32,4096]{1,0:T(8,128)(2,1)S(1)}) custom-call(bf16[64,2048]{1,0:T(8,128)(2,1)S(1)} %shard_map.58.refs_0_, bf16[64,2048]{1,0:T(8,128)(2,1)S(1)} %collective-permute-done.7.refs_1_, ...), custom_call_target="tpu_custom_call" | custom-call | flops 2147483648 | bytes 16777216 | tf_op jit(solution)/shard_map/pallas_call | solution.py:209
  40.1 3.2 %collective-permute-start.10 = (bf16[32,4096]{1,0:T(8,128)(2,1)S(1)}, bf16[32,4096]{1,0:T(8,128)(2,1)S(1)}, u32[]{:S(2)}, u32[]{:S(2)}) collective-permute-start(bf16[32,4096]{1,0:T(8,128)(2,1)S(1)} %select_add_fusion.3), channel_id=1, source_target_pairs={{0,1},{1,0},{2,3},{3,2},{4,5},{5,4},{6,7},{7,6},{8,9},{9,8},{10,11... | collective-permute-start | bytes 786440 | tf_op jit(solution)/shard_map/ppermute | solution.py:271
  43.3 2.2 %collective-permute-done.17 = bf16[32,4096]{1,0:T(8,128)(2,1)S(1)} collective-permute-done((bf16[32,4096]{1,0:T(8,128)(2,1)S(1)}, bf16[32,4096]{1,0:T(8,128)(2,1)S(1)}, u32[]{:S(2)}, u32[]{:S(2)}) %collective-permute-start.17) | collective-permute-done | bytes 262176 | tf_op jit(solution)/shard_map/ppermute | solution.py:271
  45.7 7.2 %collective-permute-start.16 = (bf16[32,4096]{1,0:T(8,128)(2,1)S(1)}, bf16[32,4096]{1,0:T(8,128)(2,1)S(1)}, u32[]{:S(2)}, u32[]{:S(2)}) collective-permute-start(bf16[32,4096]{1,0:T(8,128)(2,1)S(1)} %select_add_fusion.1), channel_id=1, source_target_pairs={{0,1},{1,0},{2,3},{3,2},{4,5},{5,4},{6,7},{7,6},{8,9},{9,8},{10,11... | collective-permute-start | bytes 786440 | tf_op jit(solution)/shard_map/ppermute | solution.py:271
  53.0 4.3 %collective-permute-done.16 = bf16[32,4096]{1,0:T(8,128)(2,1)S(1)} collective-permute-done((bf16[32,4096]{1,0:T(8,128)(2,1)S(1)}, bf16[32,4096]{1,0:T(8,128)(2,1)S(1)}, u32[]{:S(2)}, u32[]{:S(2)}) %collective-permute-start.16) | collective-permute-done | bytes 262176 | tf_op jit(solution)/shard_map/ppermute | solution.py:271
  57.4 0.8 %maximum_bitcast_fusion = bf16[1,2,1,32,4096]{4,3,2,1,0:T(8,128)(2,1)} fusion(bf16[1,32,4096]{2,1,0:T(8,128)(2,1)S(1)} %select_bitcast_fusion, bf16[1,32,4096]{2,1,0:T(8,128)(2,1)S(1)} %get-tuple-element.45), kind=kLoop, calls=%fused_computation | loop fusion | flops 262144 | bytes 1048576 | tf_op jit(solution)/shard_map/reshape | solution.py:318
  (29 shorter events, 1.2 us)
Async XLA Ops:
  0.8 10.8 %collective-permute-start = (bf16[272,128]{1,0:T(8,128)(2,1)S(1)}, bf16[272,128]{1,0:T(8,128)(2,1)S(1)}, u32[]{:S(2)}, u32[]{:S(2)}) collective-permute-start(bf16[272,128]{1,0:T(8,128)(2,1)S(1)} %shard_map.56.refs_0_), channel_id=1, source_target_pairs={{0,16},{4,20},{8,24},{12,28},{16,0},{20,4},{24,8},{28,12},{1,17},{... | collective-permute-start | bytes 208904 | tf_op jit(solution)/shard_map/ppermute | solution.py:285
  3.8 7.8 %collective-permute-start.1 = (bf16[272,128]{1,0:T(8,128)(2,1)S(1)}, bf16[272,128]{1,0:T(8,128)(2,1)S(1)}, u32[]{:S(2)}, u32[]{:S(2)}) collective-permute-start(bf16[272,128]{1,0:T(8,128)(2,1)S(1)} %shard_map.56.refs_0_), channel_id=1, source_target_pairs={{0,20},{4,16},{8,28},{12,24},{16,4},{20,0},{24,12},{28,8},{1,21},{... | collective-permute-start | bytes 208904 | tf_op jit(solution)/shard_map/ppermute | solution.py:285
  5.3 6.3 %collective-permute-start.2 = (bf16[272,128]{1,0:T(8,128)(2,1)S(1)}, bf16[272,128]{1,0:T(8,128)(2,1)S(1)}, u32[]{:S(2)}, u32[]{:S(2)}) collective-permute-start(bf16[272,128]{1,0:T(8,128)(2,1)S(1)} %shard_map.56.refs_0_), channel_id=1, source_target_pairs={{0,4},{4,0},{8,12},{12,8},{16,20},{20,16},{24,28},{28,24},{1,5},{5... | collective-permute-start | bytes 208904 | tf_op jit(solution)/shard_map/ppermute | solution.py:285
  5.4 7.3 %collective-permute-start.3 = (bf16[272,128]{1,0:T(8,128)(2,1)S(1)}, bf16[272,128]{1,0:T(8,128)(2,1)S(1)}, u32[]{:S(2)}, u32[]{:S(2)}) collective-permute-start(bf16[272,128]{1,0:T(8,128)(2,1)S(1)} %shard_map.56.refs_0_), channel_id=1, source_target_pairs={{0,8},{4,12},{8,0},{12,4},{16,24},{20,28},{24,16},{28,20},{1,9},{5... | collective-permute-start | bytes 208904 | tf_op jit(solution)/shard_map/ppermute | solution.py:285
  11.6 1.5 %collective-permute-start.4 = (bf16[272,128]{1,0:T(8,128)(2,1)S(1)}, bf16[272,128]{1,0:T(8,128)(2,1)S(1)}, u32[]{:S(2)}, u32[]{:S(2)}) collective-permute-start(bf16[272,128]{1,0:T(8,128)(2,1)S(1)} %collective-permute-done.2.refs_1_), channel_id=1, source_target_pairs={{0,8},{4,12},{8,0},{12,4},{16,24},{20,28},{24,16},{28,20},{1,9},{5... | collective-permute-start | bytes 208904 | tf_op jit(solution)/shard_map/ppermute | solution.py:285
  12.2 1.3 %collective-permute-start.5 = (bf16[272,128]{1,0:T(8,128)(2,1)S(1)}, bf16[272,128]{1,0:T(8,128)(2,1)S(1)}, u32[]{:S(2)}, u32[]{:S(2)}) collective-permute-start(bf16[272,128]{1,0:T(8,128)(2,1)S(1)} %collective-permute-done.refs_4_), channel_id=1, source_target_pairs={{0,8},{4,12},{8,0},{12,4},{16,24},{20,28},{24,16},{28,20},{1,9},{5... | collective-permute-start | bytes 208904 | tf_op jit(solution)/shard_map/ppermute | solution.py:285
  12.3 1.3 %collective-permute-start.6 = (bf16[272,128]{1,0:T(8,128)(2,1)S(1)}, bf16[272,128]{1,0:T(8,128)(2,1)S(1)}, u32[]{:S(2)}, u32[]{:S(2)}) collective-permute-start(bf16[272,128]{1,0:T(8,128)(2,1)S(1)} %collective-permute-done.1.refs_5_), channel_id=1, source_target_pairs={{0,8},{4,12},{8,0},{12,4},{16,24},{20,28},{24,16},{28,20},{1,9},{5... | collective-permute-start | bytes 208904 | tf_op jit(solution)/shard_map/ppermute | solution.py:285
  17.4 9.2 %collective-permute-start.13 = (bf16[64,2048]{1,0:T(8,128)(2,1)S(1)}, bf16[64,2048]{1,0:T(8,128)(2,1)S(1)}, u32[]{:S(2)}, u32[]{:S(2)}) collective-permute-start(bf16[64,2048]{1,0:T(8,128)(2,1)S(1)} %get-tuple-element.42), channel_id=1, source_target_pairs={{0,4},{4,0},{1,5},{5,1},{2,6},{6,2},{3,7},{7,3},{8,12},{12,8},{9,1... | collective-permute-start | bytes 786440 | tf_op jit(solution)/shard_map/ppermute | solution.py:297
  19.5 11.6 %collective-permute-start.8 = (bf16[32,4096]{1,0:T(8,128)(2,1)S(1)}, bf16[32,4096]{1,0:T(8,128)(2,1)S(1)}, u32[]{:S(2)}, u32[]{:S(2)}) collective-permute-start(bf16[32,4096]{1,0:T(8,128)(2,1)S(1)} %get-tuple-element.38), channel_id=1, source_target_pairs={{0,1},{1,0},{2,3},{3,2},{4,5},{5,4},{6,7},{7,6},{8,9},{9,8},{10,11... | collective-permute-start | bytes 786440 | tf_op jit(solution)/shard_map/ppermute | solution.py:271
  21.1 13.2 %collective-permute-start.11 = (bf16[32,4096]{1,0:T(8,128)(2,1)S(1)}, bf16[32,4096]{1,0:T(8,128)(2,1)S(1)}, u32[]{:S(2)}, u32[]{:S(2)}) collective-permute-start(bf16[32,4096]{1,0:T(8,128)(2,1)S(1)} %get-tuple-element.39), channel_id=1, source_target_pairs={{0,1},{1,0},{2,3},{3,2},{4,5},{5,4},{6,7},{7,6},{8,9},{9,8},{10,11... | collective-permute-start | bytes 786440 | tf_op jit(solution)/shard_map/ppermute | solution.py:271
  23.3 14.2 %collective-permute-start.7 = (bf16[64,2048]{1,0:T(8,128)(2,1)S(1)}, bf16[64,2048]{1,0:T(8,128)(2,1)S(1)}, u32[]{:S(2)}, u32[]{:S(2)}) collective-permute-start(bf16[64,2048]{1,0:T(8,128)(2,1)S(1)} %shard_map.58.refs_0_), channel_id=1, source_target_pairs={{0,4},{4,0},{1,5},{5,1},{2,6},{6,2},{3,7},{7,3},{8,12},{12,8},{9,1... | collective-permute-start | bytes 786440 | tf_op jit(solution)/shard_map/ppermute | solution.py:297
  29.0 11.0 %collective-permute-start.14 = (bf16[32,4096]{1,0:T(8,128)(2,1)S(1)}, bf16[32,4096]{1,0:T(8,128)(2,1)S(1)}, u32[]{:S(2)}, u32[]{:S(2)}) collective-permute-start(bf16[32,4096]{1,0:T(8,128)(2,1)S(1)} %get-tuple-element.43), channel_id=1, source_target_pairs={{0,1},{1,0},{2,3},{3,2},{4,5},{5,4},{6,7},{7,6},{8,9},{9,8},{10,11... | collective-permute-start | bytes 786440 | tf_op jit(solution)/shard_map/ppermute | solution.py:271
  31.2 8.9 %collective-permute-start.9 = (bf16[32,4096]{1,0:T(8,128)(2,1)S(1)}, bf16[32,4096]{1,0:T(8,128)(2,1)S(1)}, u32[]{:S(2)}, u32[]{:S(2)}) collective-permute-start(bf16[32,4096]{1,0:T(8,128)(2,1)S(1)} %add.30), channel_id=1, source_target_pairs={{0,8},{1,2},{2,1},{3,11},{4,12},{5,6},{6,5},{7,15},{8,0},{9,10},{1... | collective-permute-start | bytes 786440 | tf_op jit(solution)/shard_map/ppermute | solution.py:275
  34.4 18.6 %collective-permute-start.12 = (bf16[32,4096]{1,0:T(8,128)(2,1)S(1)}, bf16[32,4096]{1,0:T(8,128)(2,1)S(1)}, u32[]{:S(2)}, u32[]{:S(2)}) collective-permute-start(bf16[32,4096]{1,0:T(8,128)(2,1)S(1)} %add.33), channel_id=1, source_target_pairs={{0,8},{1,2},{2,1},{3,11},{4,12},{5,6},{6,5},{7,15},{8,0},{9,10},{1... | collective-permute-start | bytes 786440 | tf_op jit(solution)/shard_map/ppermute | solution.py:275
  34.4 11.1 %collective-permute-start.17 = (bf16[32,4096]{1,0:T(8,128)(2,1)S(1)}, bf16[32,4096]{1,0:T(8,128)(2,1)S(1)}, u32[]{:S(2)}, u32[]{:S(2)}) collective-permute-start(bf16[32,4096]{1,0:T(8,128)(2,1)S(1)} %get-tuple-element.44), channel_id=1, source_target_pairs={{0,1},{1,0},{2,3},{3,2},{4,5},{5,4},{6,7},{7,6},{8,9},{9,8},{10,11... | collective-permute-start | bytes 786440 | tf_op jit(solution)/shard_map/ppermute | solution.py:271
  40.0 5.7 %collective-permute-start.15 = (bf16[32,4096]{1,0:T(8,128)(2,1)S(1)}, bf16[32,4096]{1,0:T(8,128)(2,1)S(1)}, u32[]{:S(2)}, u32[]{:S(2)}) collective-permute-start(bf16[32,4096]{1,0:T(8,128)(2,1)S(1)} %add.35), channel_id=1, source_target_pairs={{0,8},{1,2},{2,1},{3,11},{4,12},{5,6},{6,5},{7,15},{8,0},{9,10},{1... | collective-permute-start | bytes 786440 | tf_op jit(solution)/shard_map/ppermute | solution.py:275
  40.1 12.8 %collective-permute-start.10 = (bf16[32,4096]{1,0:T(8,128)(2,1)S(1)}, bf16[32,4096]{1,0:T(8,128)(2,1)S(1)}, u32[]{:S(2)}, u32[]{:S(2)}) collective-permute-start(bf16[32,4096]{1,0:T(8,128)(2,1)S(1)} %select_add_fusion.3), channel_id=1, source_target_pairs={{0,1},{1,0},{2,3},{3,2},{4,5},{5,4},{6,7},{7,6},{8,9},{9,8},{10,11... | collective-permute-start | bytes 786440 | tf_op jit(solution)/shard_map/ppermute | solution.py:271
  45.6 7.4 %collective-permute-start.18 = (bf16[32,4096]{1,0:T(8,128)(2,1)S(1)}, bf16[32,4096]{1,0:T(8,128)(2,1)S(1)}, u32[]{:S(2)}, u32[]{:S(2)}) collective-permute-start(bf16[32,4096]{1,0:T(8,128)(2,1)S(1)} %add.38), channel_id=1, source_target_pairs={{0,8},{1,2},{2,1},{3,11},{4,12},{5,6},{6,5},{7,15},{8,0},{9,10},{1... | collective-permute-start | bytes 786440 | tf_op jit(solution)/shard_map/ppermute | solution.py:275
  45.7 11.6 %collective-permute-start.16 = (bf16[32,4096]{1,0:T(8,128)(2,1)S(1)}, bf16[32,4096]{1,0:T(8,128)(2,1)S(1)}, u32[]{:S(2)}, u32[]{:S(2)}) collective-permute-start(bf16[32,4096]{1,0:T(8,128)(2,1)S(1)} %select_add_fusion.1), channel_id=1, source_target_pairs={{0,1},{1,0},{2,3},{3,2},{4,5},{5,4},{6,7},{7,6},{8,9},{9,8},{10,11... | collective-permute-start | bytes 786440 | tf_op jit(solution)/shard_map/ppermute | solution.py:271

commit v4 on v3

--- a/solution.py
+++ b/solution.py
@@ -130,12 +130,12 @@
             result[:, h * width : (h + 1) * width] = done
 
 
-def project(rows, weight, outs):
-    tile = weight.shape[1] // 4
-    for i in range(4):
-        at = slice(i * tile, (i + 1) * tile)
-        product = jnp.dot(rows, weight[:, at], preferred_element_type=F32).astype(BF16)
-        top = 0
+def project(rows, weight, outs, left):
+    tile = outs[0].shape[1] // 4
+    for i in range(weight.shape[1] // tile):
+        part = weight[:, i * tile : (i + 1) * tile]
+        product = jnp.dot(rows, part, preferred_element_type=F32).astype(BF16)
+        at, top = slice(left + i * tile, left + (i + 1) * tile), 0
         for out in outs:
             out[:, at] = product[top : top + out.shape[0]]
             top += out.shape[0]
@@ -145,11 +145,19 @@
     return jnp.concatenate([rows, jnp.zeros_like(rows)], axis=0)
 
 
-def far_kernel(window, heads, query_ref, weight_ref, *refs):
-    blocks, (rows_out, first, second), scratch = refs[:8], refs[8:11], refs[11:]
+def far_kernel(window, heads, query_ref, wide_ref, weight_ref, *refs):
+    blocks, (rows_out, first, second, rest_ref) = refs[:8], refs[8:12]
+    scratch, sems = refs[12:-1], refs[-1]
+    copies = pieces(weight_ref, rest_ref, wide_ref.shape[1], WEIGHT_CUTS, sems)
+    for copy in copies:
+        copy.start()
     shards = leaving(lax.axis_index("tp"))[:2]
     attend(window, heads, shards, query_ref, blocks, scratch, rows_out)
-    project(filled(rows_out[...]), weight_ref, (first, second))
+    rows = filled(rows_out[...])
+    project(rows, wide_ref, (first, second), 0)
+    for copy in copies:
+        copy.wait()
+    project(rows, rest_ref, (first, second), wide_ref.shape[1])
 
 
 def near_kernel(window, heads, query_ref, *refs):
@@ -175,10 +183,12 @@
     given, specs = [query], [vmem]
     kernel = near_kernel
     if weight is not None:
-        depth, columns = weight.shape
+        (depth, columns), loaded = weight[1].shape, weight[0].shape[1]
         outs += [jax.ShapeDtypeStruct((half // 2, columns), BF16)] * 2
-        given.append(pltpu.with_memory_space_constraint(weight, pltpu.VMEM))
-        specs.append(vmem)
+        outs.append(pltpu.VMEM((depth, columns - loaded), BF16))
+        given += [weight[0], pin(weight[1])]
+        specs += [vmem, pl.BlockSpec(memory_space=pltpu.HBM)]
+        scratch.append(pltpu.SemaphoreType.DMA((WEIGHT_CUTS,)))
         flops += 2 * half * depth * columns
         kernel = far_kernel
     return pl.pallas_call(
@@ -195,21 +205,23 @@
 
 
 def project_kernel(count, *refs):
-    weight_ref = refs[count]
     rows = [ref[...] for ref in refs[:count]]
     rows = filled(rows[0]) if count == 1 else jnp.concatenate(rows, axis=0)
-    project(rows, weight_ref, refs[count + 1 :])
-
-
-def project_call(parts, weight):
-    depth, columns = weight.shape
+    wide_ref, rest_ref, *outs = refs[count:]
+    project(rows, wide_ref, outs, 0)
+    project(rows, rest_ref, outs, wide_ref.shape[1])
+
+
+def project_call(parts, weights):
+    depth = parts[0].shape[1]
+    columns = weights[0].shape[1] + weights[1].shape[1]
     half = parts[0].shape[0]
     vmem = pl.BlockSpec(memory_space=pltpu.VMEM)
     outs = [jax.ShapeDtypeStruct((half // 2, columns), BF16)] * (2 * len(parts))
     return pl.pallas_call(
         functools.partial(project_kernel, len(parts)),
         out_shape=outs,
-        in_specs=[vmem] * (len(parts) + 1),
+        in_specs=[vmem] * (len(parts) + 2),
         out_specs=[vmem] * len(outs),
         compiler_params=pltpu.CompilerParams(vmem_limit_bytes=24 * MIB),
         cost_estimate=pl.CostEstimate(
@@ -217,11 +229,23 @@
             bytes_accessed=2 * depth * columns,
             transcendentals=0,
         ),
-    )(*parts, pltpu.with_memory_space_constraint(weight, pltpu.VMEM))
+    )(*parts, *weights)
+
+
+def pieces(weight_ref, part_ref, left, count, sems):
+    depth, columns = part_ref.shape
+    rows = depth // count
+    return [
+        pltpu.make_async_copy(
+            weight_ref.at[pl.ds(i * rows, rows), pl.ds(left, columns)],
+            part_ref.at[pl.ds(i * rows, rows)],
+            sems.at[i],
+        )
+        for i in range(count)
+    ]
 
 
 def load_kernel(heads, weight_ref, query_ref, out_ref, far_ref, near_ref, query_in, wide, sems):
-    depth = weight_ref.shape[0] // WEIGHT_CUTS
     size = query_ref.shape[0] // 4
     half = 2 * size // heads
     copies = [
@@ -232,9 +256,7 @@
         )
         for i, shard in enumerate(leaving(lax.axis_index("tp")))
     ]
-    for i in range(WEIGHT_CUTS):
-        at = pl.ds(i * depth, depth)
-        copies.append(pltpu.make_async_copy(weight_ref.at[at], out_ref.at[at], sems.at[4 + i]))
+    copies += pieces(weight_ref, out_ref, 0, WEIGHT_CUTS, sems.at[pl.ds(4, WEIGHT_CUTS)])
     for copy in copies:
         copy.start()
     for copy in copies[:4]:
@@ -250,11 +272,12 @@
 
 def load(weight, query):
     rows, heads, width = query.shape
+    depth, columns = weight.shape
     hbm, vmem = pl.BlockSpec(memory_space=pltpu.HBM), pl.BlockSpec(memory_space=pltpu.VMEM)
     part = pltpu.VMEM((rows // 2 * heads, width), BF16)
     return pl.pallas_call(
         functools.partial(load_kernel, heads),
-        out_shape=[pltpu.VMEM(weight.shape, weight.dtype), part, part],
+        out_shape=[pltpu.VMEM((depth, columns * 3 // 4), BF16), part, part],
         in_specs=[hbm, hbm],
         out_specs=[vmem] * 3,
         scratch_shapes=[
@@ -299,14 +322,18 @@
     def passed(value):
         return jnp.where(inside, value, jnp.zeros_like(value))
 
-    far_rows, first, second = attention_call(far_query, blocks, window, weight)
+    far_rows, first, second, rest = attention_call(
+        far_query, blocks, window, (weight, out_weight)
+    )
+    weights = (weight, rest)
     near_query, far_rows = after((near_query, far_rows))
     (near_rows,) = attention_call(near_query, blocks, window)
     other_far, other_near = trade(far_rows), trade(near_rows)
-    late_first, late_second = project_call([other_far], weight)
-    third, kept, late_third, late_kept = project_call([near_rows, other_near], weight)
-
-    far = swap_inner(first + swap(first))
+    first_sum = first + swap(first)
+    far = swap_inner(first_sum)
+    late_first, late_second = project_call([other_far], weights)
+    other_near, far = after((other_near, far))
+    third, kept, late_third, late_kept = project_call([near_rows, other_near], weights)
     near = swap_inner(second + swap(second))
     late_far = swap_inner(late_first + swap(late_first))
     late_near = swap_inner(late_second + swap(late_second))

time: 58.4 us -> 55.2 us (0.945)
  starting transfers between devices: 25.8 us -> 23.9 us
  Pallas kernels: 17.3 us -> 16.4 us
    ppermute x6, starting transfers between devices: 17.7 us -> 16.3 us  [swap(): return lax.ppermute(value, 'tp', OUTER)]
    ppermute x2, waiting for transfers between devices: 3.12 us -> 1.88 us  [trade(): return lax.ppermute(value, 'ctx', [(0, 1), (1, 0)])]
    pallas_call x1, Pallas kernels: 6.2 us -> 4.98 us  [load(): pl.pallas_call(functools.partial(load_kernel, heads), out_shape=[pltpu.VM...]
    ppermute x6, waiting for transfers between devices: 9.61 us -> 10.5 us  [swap(): return lax.ppermute(value, 'tp', OUTER)]
  transfers between devices with their start and end apart: 19 -> 19, of which waited for: 7 -> 8; matrix products, arithmetic and copies ran while one was open for 1% -> 1% of each run, Pallas kernels for 22% -> 21%
where the time goes in v4:
time: 55.2 us; the launch traced here: 55 us
  starting transfers between devices  23.9 us (43%)
  Pallas kernels  16.4 us (30%)
  waiting for transfers between devices  13.3 us (24%)
  other arithmetic  1.27 us (2%)
    ppermute x6, starting transfers between devices, swap(): return lax.ppermute(value, 'tp', OUTER)  16.3 us
    ppermute x6, waiting for transfers between devices, swap(): return lax.ppermute(value, 'tp', OUTER)  10.5 us
    pallas_call x2, Pallas kernels, attention_call(): pl.pallas_call(functools.partial(kernel, window, heads), out_shape=outs,...  5.86 us
    ppermute x7, starting transfers between devices, pair(): return lax.ppermute(value, ('pipe', 'ctx'), [(i, i ^ m) for i in range(8)])  5.63 us
    pallas_call x1, Pallas kernels, load(): pl.pallas_call(functools.partial(load_kernel, heads), out_shape=[pltpu.VM...  4.98 us
    pallas_call x2, Pallas kernels, project_call(): pl.pallas_call(functools.partial(project_kernel, len(parts)), out_shape=o...  4.69 us
    ppermute x2, waiting for transfers between devices, trade(): return lax.ppermute(value, 'ctx', [(0, 1), (1, 0)])  1.88 us
    ppermute x2, starting transfers between devices, trade(): return lax.ppermute(value, 'ctx', [(0, 1), (1, 0)])  1.73 us
  transfers between devices with their start and end apart: 19, of which 8 were waited for; matrix products, arithmetic and copies ran while one was open for 1% of the time, Pallas kernels for 21%

profile of v4, /device:TPU:0, one launch (start us, length us, event | category | flops | bytes accessed | tf_op | source)
XLA Modules:
  0.0 55.0 jit_solution(17618283733960230001)
XLA Ops:
  0.0 0.8 %shard_map.56.refs_0_ = bf16[272,128]{1,0:T(8,128)(2,1)S(1)} custom-call(bf16[128,128]{1,0:T(8,128)(2,1)} %bitcast.13, bf16[128,128]{1,0:T(8,128)(2,1)} %bitcast.14, s32[1,128]{1,0:T(1,128)} %bitcast.15), custom_call_target="tpu_custom_call" | custom-call | tf_op jit(solution)/shard_map/pallas_call | solution.py:46
  0.8 3.0 %collective-permute-start = (bf16[272,128]{1,0:T(8,128)(2,1)S(1)}, bf16[272,128]{1,0:T(8,128)(2,1)S(1)}, u32[]{:S(2)}, u32[]{:S(2)}) collective-permute-start(bf16[272,128]{1,0:T(8,128)(2,1)S(1)} %shard_map.56.refs_0_), channel_id=1, source_target_pairs={{0,16},{4,20},{8,24},{12,28},{16,0},{20,4},{24,8},{28,12},{1,17},{... | collective-permute-start | bytes 208904 | tf_op jit(solution)/shard_map/ppermute | solution.py:308
  3.8 1.5 %collective-permute-start.1 = (bf16[272,128]{1,0:T(8,128)(2,1)S(1)}, bf16[272,128]{1,0:T(8,128)(2,1)S(1)}, u32[]{:S(2)}, u32[]{:S(2)}) collective-permute-start(bf16[272,128]{1,0:T(8,128)(2,1)S(1)} %shard_map.56.refs_0_), channel_id=1, source_target_pairs={{0,20},{4,16},{8,28},{12,24},{16,4},{20,0},{24,12},{28,8},{1,21},{... | collective-permute-start | bytes 208904 | tf_op jit(solution)/shard_map/ppermute | solution.py:308
  5.4 5.0 %shard_map.55 = (bf16[2048,3072]{1,0:T(8,128)(2,1)S(1)}, bf16[1024,128]{1,0:T(8,128)(2,1)S(1)}, bf16[1024,128]{1,0:T(8,128)(2,1)S(1)}) custom-call(bf16[2048,4096]{1,0:T(8,128)(2,1)} %weight_ref.2, bf16[2048,128]{1,0:T(8,128)(2,1)} %bitcast.12), custom_call_target="tpu_custom_call" | custom-call | bytes 33554432 | tf_op jit(solution)/shard_map/pallas_call | solution.py:278
  10.4 0.6 %collective-permute-start.4 = (bf16[272,128]{1,0:T(8,128)(2,1)S(1)}, bf16[272,128]{1,0:T(8,128)(2,1)S(1)}, u32[]{:S(2)}, u32[]{:S(2)}) collective-permute-start(bf16[272,128]{1,0:T(8,128)(2,1)S(1)} %collective-permute-done.2.refs_1_), channel_id=1, source_target_pairs={{0,8},{4,12},{8,0},{12,4},{16,24},{20,28},{24,16},{28,20},{1,9},{5... | collective-permute-start | bytes 208904 | tf_op jit(solution)/shard_map/ppermute | solution.py:308
  11.0 0.4 collective-permute-start.6
  11.5 0.4 collective-permute-done.4.refs_3_
  12.4 4.1 %shard_map.57 = (bf16[64,2048]{1,0:T(8,128)(2,1)S(1)}, bf16[32,4096]{1,0:T(8,128)(2,1)S(1)}, bf16[32,4096]{1,0:T(8,128)(2,1)S(1)}, bf16[2048,1024]{1,0:T(8,128)(2,1)S(1)}) custom-call(bf16[1024,128]{1,0:T(8,128)(2,1)S(1)} %get-tuple-element.30.query_ref, bf16[2048,3072]{1,0:T(8,128)(2,1)S(1)} %get-tuple-element.32.wide_ref.refs_2_.refs_1_, ...), custom_call_target="tpu_custom_call" | custom-call | flops 1409286144 | bytes 1048576 | tf_op jit(solution)/shard_map/pallas_call | solution.py:194
  16.5 2.1 %collective-permute-start.8 = (bf16[32,4096]{1,0:T(8,128)(2,1)S(1)}, bf16[32,4096]{1,0:T(8,128)(2,1)S(1)}, u32[]{:S(2)}, u32[]{:S(2)}) collective-permute-start(bf16[32,4096]{1,0:T(8,128)(2,1)S(1)} %get-tuple-element.38), channel_id=1, source_target_pairs={{0,1},{1,0},{2,3},{3,2},{4,5},{5,4},{6,7},{7,6},{8,9},{9,8},{10,11... | collective-permute-start | bytes 786440 | tf_op jit(solution)/shard_map/ppermute | solution.py:294
  18.6 1.5 %collective-permute-start.13 = (bf16[64,2048]{1,0:T(8,128)(2,1)S(1)}, bf16[64,2048]{1,0:T(8,128)(2,1)S(1)}, u32[]{:S(2)}, u32[]{:S(2)}) collective-permute-start(bf16[64,2048]{1,0:T(8,128)(2,1)S(1)} %get-tuple-element.48), channel_id=1, source_target_pairs={{0,4},{4,0},{1,5},{5,1},{2,6},{6,2},{3,7},{7,3},{8,12},{12,8},{9,1... | collective-permute-start | bytes 786440 | tf_op jit(solution)/shard_map/ppermute | solution.py:320
  20.1 0.4 collective-permute-start.11
  20.6 1.8 %shard_map.58.refs_0_ = bf16[64,2048]{1,0:T(8,128)(2,1)S(1)} custom-call(bf16[1024,128]{1,0:T(8,128)(2,1)S(1)} %get-tuple-element.37.query_ref, bf16[272,128]{1,0:T(8,128)(2,1)S(1)} %shard_map.56.refs_0_, bf16[272,128]{1,0:T(8,128)(2,1)S(1)} %collective-permute-done.2.refs_1_, bf16[272,128]{1,0:T(8,128)(2,1)S(1)} %collective-permute-done.3.refs_2_, ...), custom_call_target="tpu_custom_call" | custom-call | flops 335544320 | bytes 1048576 | tf_op jit(solution)/shard_map/pallas_call | solution.py:194
  22.6 3.2 %collective-permute-done.8 = bf16[32,4096]{1,0:T(8,128)(2,1)S(1)} collective-permute-done((bf16[32,4096]{1,0:T(8,128)(2,1)S(1)}, bf16[32,4096]{1,0:T(8,128)(2,1)S(1)}, u32[]{:S(2)}, u32[]{:S(2)}) %collective-permute-start.8) | collective-permute-done | bytes 262176 | tf_op jit(solution)/shard_map/ppermute | solution.py:294
  25.9 1.9 %collective-permute-done.13.refs_0_ = bf16[64,2048]{1,0:T(8,128)(2,1)S(1)} collective-permute-done((bf16[64,2048]{1,0:T(8,128)(2,1)S(1)}, bf16[64,2048]{1,0:T(8,128)(2,1)S(1)}, u32[]{:S(2)}, u32[]{:S(2)}) %collective-permute-start.13) | collective-permute-done | bytes 262176 | tf_op jit(solution)/shard_map/ppermute | solution.py:320
  27.7 2.3 %shard_map.60 = (bf16[32,4096]{1,0:T(8,128)(2,1)S(1)}, bf16[32,4096]{1,0:T(8,128)(2,1)S(1)}) custom-call(bf16[64,2048]{1,0:T(8,128)(2,1)S(1)} %collective-permute-done.13.refs_0_, bf16[2048,3072]{1,0:T(8,128)(2,1)S(1)} %get-tuple-element.32.wide_ref.refs_2_.refs_1_, bf16[2048,1024]{1,0:T(8,128)(2,1)S(1)} %get-tuple-element.40.refs_3_.refs_2_), custom_call_target="tpu_custom_call" | custom-call | flops 1073741824 | bytes 16777216 | tf_op jit(solution)/shard_map/pallas_call | solution.py:221
  30.1 1.7 %collective-permute-start.14 = (bf16[32,4096]{1,0:T(8,128)(2,1)S(1)}, bf16[32,4096]{1,0:T(8,128)(2,1)S(1)}, u32[]{:S(2)}, u32[]{:S(2)}) collective-permute-start(bf16[32,4096]{1,0:T(8,128)(2,1)S(1)} %get-tuple-element.49), channel_id=1, source_target_pairs={{0,1},{1,0},{2,3},{3,2},{4,5},{5,4},{6,7},{7,6},{8,9},{9,8},{10,11... | collective-permute-start | bytes 786440 | tf_op jit(solution)/shard_map/ppermute | solution.py:294
  32.0 2.5 %collective-permute-start.17 = (bf16[32,4096]{1,0:T(8,128)(2,1)S(1)}, bf16[32,4096]{1,0:T(8,128)(2,1)S(1)}, u32[]{:S(2)}, u32[]{:S(2)}) collective-permute-start(bf16[32,4096]{1,0:T(8,128)(2,1)S(1)} %get-tuple-element.50), channel_id=1, source_target_pairs={{0,1},{1,0},{2,3},{3,2},{4,5},{5,4},{6,7},{7,6},{8,9},{9,8},{10,11... | collective-permute-start | bytes 786440 | tf_op jit(solution)/shard_map/ppermute | solution.py:294
  34.5 2.3 %shard_map.59 = (bf16[32,4096]{1,0:T(8,128)(2,1)S(1)}, bf16[32,4096]{1,0:T(8,128)(2,1)S(1)}, bf16[32,4096]{1,0:T(8,128)(2,1)S(1)}, bf16[32,4096]{1,0:T(8,128)(2,1)S(1)}) custom-call(bf16[64,2048]{1,0:T(8,128)(2,1)S(1)} %shard_map.58.refs_0_, bf16[64,2048]{1,0:T(8,128)(2,1)S(1)} %collective-permute-done.7.refs_1_, ...), custom_call_target="tpu_custom_call" | custom-call | flops 2147483648 | bytes 16777216 | tf_op jit(solution)/shard_map/pallas_call | solution.py:221
  36.8 2.1 %collective-permute-done.14 = bf16[32,4096]{1,0:T(8,128)(2,1)S(1)} collective-permute-done((bf16[32,4096]{1,0:T(8,128)(2,1)S(1)}, bf16[32,4096]{1,0:T(8,128)(2,1)S(1)}, u32[]{:S(2)}, u32[]{:S(2)}) %collective-permute-start.14) | collective-permute-done | bytes 262176 | tf_op jit(solution)/shard_map/ppermute | solution.py:294
  39.1 3.7 %collective-permute-start.10 = (bf16[32,4096]{1,0:T(8,128)(2,1)S(1)}, bf16[32,4096]{1,0:T(8,128)(2,1)S(1)}, u32[]{:S(2)}, u32[]{:S(2)}) collective-permute-start(bf16[32,4096]{1,0:T(8,128)(2,1)S(1)} %select_add_fusion.3), channel_id=1, source_target_pairs={{0,1},{1,0},{2,3},{3,2},{4,5},{5,4},{6,7},{7,6},{8,9},{9,8},{10,11... | collective-permute-start | bytes 786440 | tf_op jit(solution)/shard_map/ppermute | solution.py:294
  42.8 0.9 %collective-permute-done.17 = bf16[32,4096]{1,0:T(8,128)(2,1)S(1)} collective-permute-done((bf16[32,4096]{1,0:T(8,128)(2,1)S(1)}, bf16[32,4096]{1,0:T(8,128)(2,1)S(1)}, u32[]{:S(2)}, u32[]{:S(2)}) %collective-permute-start.17) | collective-permute-done | bytes 262176 | tf_op jit(solution)/shard_map/ppermute | solution.py:294
  43.9 5.8 %collective-permute-start.16 = (bf16[32,4096]{1,0:T(8,128)(2,1)S(1)}, bf16[32,4096]{1,0:T(8,128)(2,1)S(1)}, u32[]{:S(2)}, u32[]{:S(2)}) collective-permute-start(bf16[32,4096]{1,0:T(8,128)(2,1)S(1)} %select_add_fusion.1), channel_id=1, source_target_pairs={{0,1},{1,0},{2,3},{3,2},{4,5},{5,4},{6,7},{7,6},{8,9},{9,8},{10,11... | collective-permute-start | bytes 786440 | tf_op jit(solution)/shard_map/ppermute | solution.py:294
  49.7 4.3 %collective-permute-done.16 = bf16[32,4096]{1,0:T(8,128)(2,1)S(1)} collective-permute-done((bf16[32,4096]{1,0:T(8,128)(2,1)S(1)}, bf16[32,4096]{1,0:T(8,128)(2,1)S(1)}, u32[]{:S(2)}, u32[]{:S(2)}) %collective-permute-start.16) | collective-permute-done | bytes 262176 | tf_op jit(solution)/shard_map/ppermute | solution.py:294
  54.2 0.8 %maximum_bitcast_fusion = bf16[1,2,1,32,4096]{4,3,2,1,0:T(8,128)(2,1)} fusion(bf16[1,32,4096]{2,1,0:T(8,128)(2,1)S(1)} %select_bitcast_fusion, bf16[1,32,4096]{2,1,0:T(8,128)(2,1)S(1)} %get-tuple-element.51), kind=kLoop, calls=%fused_computation | loop fusion | flops 262144 | bytes 1048576 | tf_op jit(solution)/shard_map/reshape | solution.py:345
  (29 shorter events, 1.6 us)
Async XLA Ops:
  0.8 9.5 %collective-permute-start = (bf16[272,128]{1,0:T(8,128)(2,1)S(1)}, bf16[272,128]{1,0:T(8,128)(2,1)S(1)}, u32[]{:S(2)}, u32[]{:S(2)}) collective-permute-start(bf16[272,128]{1,0:T(8,128)(2,1)S(1)} %shard_map.56.refs_0_), channel_id=1, source_target_pairs={{0,16},{4,20},{8,24},{12,28},{16,0},{20,4},{24,8},{28,12},{1,17},{... | collective-permute-start | bytes 208904 | tf_op jit(solution)/shard_map/ppermute | solution.py:308
  3.8 6.6 %collective-permute-start.1 = (bf16[272,128]{1,0:T(8,128)(2,1)S(1)}, bf16[272,128]{1,0:T(8,128)(2,1)S(1)}, u32[]{:S(2)}, u32[]{:S(2)}) collective-permute-start(bf16[272,128]{1,0:T(8,128)(2,1)S(1)} %shard_map.56.refs_0_), channel_id=1, source_target_pairs={{0,20},{4,16},{8,28},{12,24},{16,4},{20,0},{24,12},{28,8},{1,21},{... | collective-permute-start | bytes 208904 | tf_op jit(solution)/shard_map/ppermute | solution.py:308
  5.3 5.1 %collective-permute-start.2 = (bf16[272,128]{1,0:T(8,128)(2,1)S(1)}, bf16[272,128]{1,0:T(8,128)(2,1)S(1)}, u32[]{:S(2)}, u32[]{:S(2)}) collective-permute-start(bf16[272,128]{1,0:T(8,128)(2,1)S(1)} %shard_map.56.refs_0_), channel_id=1, source_target_pairs={{0,4},{4,0},{8,12},{12,8},{16,20},{20,16},{24,28},{28,24},{1,5},{5... | collective-permute-start | bytes 208904 | tf_op jit(solution)/shard_map/ppermute | solution.py:308
  5.4 6.1 %collective-permute-start.3 = (bf16[272,128]{1,0:T(8,128)(2,1)S(1)}, bf16[272,128]{1,0:T(8,128)(2,1)S(1)}, u32[]{:S(2)}, u32[]{:S(2)}) collective-permute-start(bf16[272,128]{1,0:T(8,128)(2,1)S(1)} %shard_map.56.refs_0_), channel_id=1, source_target_pairs={{0,8},{4,12},{8,0},{12,4},{16,24},{20,28},{24,16},{28,20},{1,9},{5... | collective-permute-start | bytes 208904 | tf_op jit(solution)/shard_map/ppermute | solution.py:308
  10.4 1.5 %collective-permute-start.4 = (bf16[272,128]{1,0:T(8,128)(2,1)S(1)}, bf16[272,128]{1,0:T(8,128)(2,1)S(1)}, u32[]{:S(2)}, u32[]{:S(2)}) collective-permute-start(bf16[272,128]{1,0:T(8,128)(2,1)S(1)} %collective-permute-done.2.refs_1_), channel_id=1, source_target_pairs={{0,8},{4,12},{8,0},{12,4},{16,24},{20,28},{24,16},{28,20},{1,9},{5... | collective-permute-start | bytes 208904 | tf_op jit(solution)/shard_map/ppermute | solution.py:308
  11.0 1.3 %collective-permute-start.5 = (bf16[272,128]{1,0:T(8,128)(2,1)S(1)}, bf16[272,128]{1,0:T(8,128)(2,1)S(1)}, u32[]{:S(2)}, u32[]{:S(2)}) collective-permute-start(bf16[272,128]{1,0:T(8,128)(2,1)S(1)} %collective-permute-done.refs_4_), channel_id=1, source_target_pairs={{0,8},{4,12},{8,0},{12,4},{16,24},{20,28},{24,16},{28,20},{1,9},{5... | collective-permute-start | bytes 208904 | tf_op jit(solution)/shard_map/ppermute | solution.py:308
  11.0 1.3 %collective-permute-start.6 = (bf16[272,128]{1,0:T(8,128)(2,1)S(1)}, bf16[272,128]{1,0:T(8,128)(2,1)S(1)}, u32[]{:S(2)}, u32[]{:S(2)}) collective-permute-start(bf16[272,128]{1,0:T(8,128)(2,1)S(1)} %collective-permute-done.1.refs_5_), channel_id=1, source_target_pairs={{0,8},{4,12},{8,0},{12,4},{16,24},{20,28},{24,16},{28,20},{1,9},{5... | collective-permute-start | bytes 208904 | tf_op jit(solution)/shard_map/ppermute | solution.py:308
  16.5 9.3 %collective-permute-start.8 = (bf16[32,4096]{1,0:T(8,128)(2,1)S(1)}, bf16[32,4096]{1,0:T(8,128)(2,1)S(1)}, u32[]{:S(2)}, u32[]{:S(2)}) collective-permute-start(bf16[32,4096]{1,0:T(8,128)(2,1)S(1)} %get-tuple-element.38), channel_id=1, source_target_pairs={{0,1},{1,0},{2,3},{3,2},{4,5},{5,4},{6,7},{7,6},{8,9},{9,8},{10,11... | collective-permute-start | bytes 786440 | tf_op jit(solution)/shard_map/ppermute | solution.py:294
  18.6 9.2 %collective-permute-start.13 = (bf16[64,2048]{1,0:T(8,128)(2,1)S(1)}, bf16[64,2048]{1,0:T(8,128)(2,1)S(1)}, u32[]{:S(2)}, u32[]{:S(2)}) collective-permute-start(bf16[64,2048]{1,0:T(8,128)(2,1)S(1)} %get-tuple-element.48), channel_id=1, source_target_pairs={{0,4},{4,0},{1,5},{5,1},{2,6},{6,2},{3,7},{7,3},{8,12},{12,8},{9,1... | collective-permute-start | bytes 786440 | tf_op jit(solution)/shard_map/ppermute | solution.py:320
  20.1 11.7 %collective-permute-start.11 = (bf16[32,4096]{1,0:T(8,128)(2,1)S(1)}, bf16[32,4096]{1,0:T(8,128)(2,1)S(1)}, u32[]{:S(2)}, u32[]{:S(2)}) collective-permute-start(bf16[32,4096]{1,0:T(8,128)(2,1)S(1)} %get-tuple-element.45), channel_id=1, source_target_pairs={{0,1},{1,0},{2,3},{3,2},{4,5},{5,4},{6,7},{7,6},{8,9},{9,8},{10,11... | collective-permute-start | bytes 786440 | tf_op jit(solution)/shard_map/ppermute | solution.py:294
  22.4 12.1 %collective-permute-start.7 = (bf16[64,2048]{1,0:T(8,128)(2,1)S(1)}, bf16[64,2048]{1,0:T(8,128)(2,1)S(1)}, u32[]{:S(2)}, u32[]{:S(2)}) collective-permute-start(bf16[64,2048]{1,0:T(8,128)(2,1)S(1)} %shard_map.58.refs_0_), channel_id=1, source_target_pairs={{0,4},{4,0},{1,5},{5,1},{2,6},{6,2},{3,7},{7,3},{8,12},{12,8},{9,1... | collective-permute-start | bytes 786440 | tf_op jit(solution)/shard_map/ppermute | solution.py:320
  25.8 8.7 %collective-permute-start.9 = (bf16[32,4096]{1,0:T(8,128)(2,1)S(1)}, bf16[32,4096]{1,0:T(8,128)(2,1)S(1)}, u32[]{:S(2)}, u32[]{:S(2)}) collective-permute-start(bf16[32,4096]{1,0:T(8,128)(2,1)S(1)} %add.30), channel_id=1, source_target_pairs={{0,8},{1,2},{2,1},{3,11},{4,12},{5,6},{6,5},{7,15},{8,0},{9,10},{1... | collective-permute-start | bytes 786440 | tf_op jit(solution)/shard_map/ppermute | solution.py:298
  30.1 8.8 %collective-permute-start.14 = (bf16[32,4096]{1,0:T(8,128)(2,1)S(1)}, bf16[32,4096]{1,0:T(8,128)(2,1)S(1)}, u32[]{:S(2)}, u32[]{:S(2)}) collective-permute-start(bf16[32,4096]{1,0:T(8,128)(2,1)S(1)} %get-tuple-element.49), channel_id=1, source_target_pairs={{0,1},{1,0},{2,3},{3,2},{4,5},{5,4},{6,7},{7,6},{8,9},{9,8},{10,11... | collective-permute-start | bytes 786440 | tf_op jit(solution)/shard_map/ppermute | solution.py:294
  31.9 17.8 %collective-permute-start.12 = (bf16[32,4096]{1,0:T(8,128)(2,1)S(1)}, bf16[32,4096]{1,0:T(8,128)(2,1)S(1)}, u32[]{:S(2)}, u32[]{:S(2)}) collective-permute-start(bf16[32,4096]{1,0:T(8,128)(2,1)S(1)} %add.33), channel_id=1, source_target_pairs={{0,8},{1,2},{2,1},{3,11},{4,12},{5,6},{6,5},{7,15},{8,0},{9,10},{1... | collective-permute-start | bytes 786440 | tf_op jit(solution)/shard_map/ppermute | solution.py:298
  32.0 11.7 %collective-permute-start.17 = (bf16[32,4096]{1,0:T(8,128)(2,1)S(1)}, bf16[32,4096]{1,0:T(8,128)(2,1)S(1)}, u32[]{:S(2)}, u32[]{:S(2)}) collective-permute-start(bf16[32,4096]{1,0:T(8,128)(2,1)S(1)} %get-tuple-element.50), channel_id=1, source_target_pairs={{0,1},{1,0},{2,3},{3,2},{4,5},{5,4},{6,7},{7,6},{8,9},{9,8},{10,11... | collective-permute-start | bytes 786440 | tf_op jit(solution)/shard_map/ppermute | solution.py:294
  39.0 4.9 %collective-permute-start.15 = (bf16[32,4096]{1,0:T(8,128)(2,1)S(1)}, bf16[32,4096]{1,0:T(8,128)(2,1)S(1)}, u32[]{:S(2)}, u32[]{:S(2)}) collective-permute-start(bf16[32,4096]{1,0:T(8,128)(2,1)S(1)} %add.35), channel_id=1, source_target_pairs={{0,8},{1,2},{2,1},{3,11},{4,12},{5,6},{6,5},{7,15},{8,0},{9,10},{1... | collective-permute-start | bytes 786440 | tf_op jit(solution)/shard_map/ppermute | solution.py:298
  39.1 10.6 %collective-permute-start.10 = (bf16[32,4096]{1,0:T(8,128)(2,1)S(1)}, bf16[32,4096]{1,0:T(8,128)(2,1)S(1)}, u32[]{:S(2)}, u32[]{:S(2)}) collective-permute-start(bf16[32,4096]{1,0:T(8,128)(2,1)S(1)} %select_add_fusion.3), channel_id=1, source_target_pairs={{0,1},{1,0},{2,3},{3,2},{4,5},{5,4},{6,7},{7,6},{8,9},{9,8},{10,11... | collective-permute-start | bytes 786440 | tf_op jit(solution)/shard_map/ppermute | solution.py:294
  43.8 5.9 %collective-permute-start.18 = (bf16[32,4096]{1,0:T(8,128)(2,1)S(1)}, bf16[32,4096]{1,0:T(8,128)(2,1)S(1)}, u32[]{:S(2)}, u32[]{:S(2)}) collective-permute-start(bf16[32,4096]{1,0:T(8,128)(2,1)S(1)} %add.38), channel_id=1, source_target_pairs={{0,8},{1,2},{2,1},{3,11},{4,12},{5,6},{6,5},{7,15},{8,0},{9,10},{1... | collective-permute-start | bytes 786440 | tf_op jit(solution)/shard_map/ppermute | solution.py:298
  43.9 10.2 %collective-permute-start.16 = (bf16[32,4096]{1,0:T(8,128)(2,1)S(1)}, bf16[32,4096]{1,0:T(8,128)(2,1)S(1)}, u32[]{:S(2)}, u32[]{:S(2)}) collective-permute-start(bf16[32,4096]{1,0:T(8,128)(2,1)S(1)} %select_add_fusion.1), channel_id=1, source_target_pairs={{0,1},{1,0},{2,3},{3,2},{4,5},{5,4},{6,7},{7,6},{8,9},{9,8},{10,11... | collective-permute-start | bytes 786440 | tf_op jit(solution)/shard_map/ppermute | solution.py:294

commit v5 on v4

--- a/solution.py
+++ b/solution.py
@@ -131,7 +131,7 @@
 
 
 def project(rows, weight, outs, left):
-    tile = outs[0].shape[1] // 4
+    tile = 1024 if weight.shape[1] % 1024 == 0 else weight.shape[1]
     for i in range(weight.shape[1] // tile):
         part = weight[:, i * tile : (i + 1) * tile]
         product = jnp.dot(rows, part, preferred_element_type=F32).astype(BF16)
@@ -145,19 +145,48 @@
     return jnp.concatenate([rows, jnp.zeros_like(rows)], axis=0)
 
 
-def far_kernel(window, heads, query_ref, wide_ref, weight_ref, *refs):
-    blocks, (rows_out, first, second, rest_ref) = refs[:8], refs[8:12]
-    scratch, sems = refs[12:-1], refs[-1]
-    copies = pieces(weight_ref, rest_ref, wide_ref.shape[1], WEIGHT_CUTS, sems)
+def far_kernel(window, heads, query_ref, loaded_ref, weight_ref, *refs):
+    blocks, (rows_out, early, part_ref) = refs[:8], refs[8:11]
+    scratch, sems = refs[11:-1], refs[-1]
+    copies = pieces(weight_ref, part_ref, loaded_ref.shape[1], WEIGHT_CUTS, sems)
     for copy in copies:
         copy.start()
     shards = leaving(lax.axis_index("tp"))[:2]
     attend(window, heads, shards, query_ref, blocks, scratch, rows_out)
-    rows = filled(rows_out[...])
-    project(rows, wide_ref, (first, second), 0)
+    project(filled(rows_out[...]), loaded_ref, (early,), 0)
     for copy in copies:
         copy.wait()
-    project(rows, rest_ref, (first, second), wide_ref.shape[1])
+
+
+def rest_kernel(left, rows_ref, loaded_ref, weight_ref, early, part_ref, sems):
+    copies = pieces(weight_ref, part_ref, left, WEIGHT_CUTS, sems)
+    for copy in copies:
+        copy.start()
+    rows = filled(rows_ref[...])
+    project(rows, loaded_ref, (early,), 0)
+    for copy in copies:
+        copy.wait()
+    project(rows, part_ref, (early,), loaded_ref.shape[1])
+
+
+def rest_call(rows, loaded, weight):
+    (half, depth), columns = rows.shape, weight.shape[1]
+    vmem = pl.BlockSpec(memory_space=pltpu.VMEM)
+    width = columns // 4
+    return pl.pallas_call(
+        functools.partial(rest_kernel, columns - width),
+        out_shape=[
+            jax.ShapeDtypeStruct((half, 2 * width), BF16),
+            pltpu.VMEM((depth, width), BF16),
+        ],
+        in_specs=[vmem, vmem, pl.BlockSpec(memory_space=pltpu.HBM)],
+        out_specs=[vmem, vmem],
+        scratch_shapes=[pltpu.SemaphoreType.DMA((WEIGHT_CUTS,))],
+        compiler_params=pltpu.CompilerParams(vmem_limit_bytes=24 * MIB),
+        cost_estimate=pl.CostEstimate(
+            flops=2 * half * depth * columns // 2, bytes_accessed=depth * columns, transcendentals=0
+        ),
+    )(rows, loaded, pin(weight))
 
 
 def near_kernel(window, heads, query_ref, *refs):
@@ -184,12 +213,12 @@
     kernel = near_kernel
     if weight is not None:
         (depth, columns), loaded = weight[1].shape, weight[0].shape[1]
-        outs += [jax.ShapeDtypeStruct((half // 2, columns), BF16)] * 2
-        outs.append(pltpu.VMEM((depth, columns - loaded), BF16))
+        outs.append(jax.ShapeDtypeStruct((half, loaded), BF16))
+        outs.append(pltpu.VMEM((depth, columns // 4), BF16))
         given += [weight[0], pin(weight[1])]
         specs += [vmem, pl.BlockSpec(memory_space=pltpu.HBM)]
         scratch.append(pltpu.SemaphoreType.DMA((WEIGHT_CUTS,)))
-        flops += 2 * half * depth * columns
+        flops += 2 * half * depth * loaded
         kernel = far_kernel
     return pl.pallas_call(
         functools.partial(kernel, window, heads),
@@ -207,21 +236,22 @@
 def project_kernel(count, *refs):
     rows = [ref[...] for ref in refs[:count]]
     rows = filled(rows[0]) if count == 1 else jnp.concatenate(rows, axis=0)
-    wide_ref, rest_ref, *outs = refs[count:]
-    project(rows, wide_ref, outs, 0)
-    project(rows, rest_ref, outs, wide_ref.shape[1])
+    left = 0
+    for weight in refs[count : count + 3]:
+        project(rows, weight, refs[count + 3 :], left)
+        left += weight.shape[1]
 
 
 def project_call(parts, weights):
     depth = parts[0].shape[1]
-    columns = weights[0].shape[1] + weights[1].shape[1]
+    columns = sum(weight.shape[1] for weight in weights)
     half = parts[0].shape[0]
     vmem = pl.BlockSpec(memory_space=pltpu.VMEM)
     outs = [jax.ShapeDtypeStruct((half // 2, columns), BF16)] * (2 * len(parts))
     return pl.pallas_call(
         functools.partial(project_kernel, len(parts)),
         out_shape=outs,
-        in_specs=[vmem] * (len(parts) + 2),
+        in_specs=[vmem] * (len(parts) + 3),
         out_specs=[vmem] * len(outs),
         compiler_params=pltpu.CompilerParams(vmem_limit_bytes=24 * MIB),
         cost_estimate=pl.CostEstimate(
@@ -277,7 +307,7 @@
     part = pltpu.VMEM((rows // 2 * heads, width), BF16)
     return pl.pallas_call(
         functools.partial(load_kernel, heads),
-        out_shape=[pltpu.VMEM((depth, columns * 3 // 4), BF16), part, part],
+        out_shape=[pltpu.VMEM((depth, columns // 2), BF16), part, part],
         in_specs=[hbm, hbm],
         out_specs=[vmem] * 3,
         scratch_shapes=[
@@ -322,24 +352,27 @@
     def passed(value):
         return jnp.where(inside, value, jnp.zeros_like(value))
 
-    far_rows, first, second, rest = attention_call(
-        far_query, blocks, window, (weight, out_weight)
-    )
-    weights = (weight, rest)
-    near_query, far_rows = after((near_query, far_rows))
+    far_rows, early, part = attention_call(far_query, blocks, window, (weight, out_weight))
+    early_in = swap(early)
+    other_far = trade(far_rows)
+    early_rest, last = rest_call(far_rows, part, out_weight)
+    weights = (weight, part, last)
+    near_query, early_rest = after((near_query, early_rest))
     (near_rows,) = attention_call(near_query, blocks, window)
-    other_far, other_near = trade(far_rows), trade(near_rows)
-    first_sum = first + swap(first)
-    far = swap_inner(first_sum)
+    other_near = trade(near_rows)
+
+    passed_on = swap_inner(early + early_in)
     late_first, late_second = project_call([other_far], weights)
-    other_near, far = after((other_near, far))
+    other_near, passed_on = after((other_near, passed_on))
     third, kept, late_third, late_kept = project_call([near_rows, other_near], weights)
-    near = swap_inner(second + swap(second))
-    late_far = swap_inner(late_first + swap(late_first))
+    passed_rest = swap_inner(early_rest + swap(early_rest))
+    late_in, third = after((swap(late_first), third))
+    late_far = swap_inner(late_first + late_in)
     late_near = swap_inner(late_second + swap(late_second))
-    own = kept + swap(third + passed(far)) + passed(near)
+    both = passed(jnp.concatenate([passed_on, passed_rest], axis=1))
+    quarter = rows // 4
+    own = kept + swap(third + both[:quarter]) + both[quarter:]
     other = late_kept + swap(late_third + passed(late_far)) + passed(late_near)
-    quarter = rows // 4
     at_first = lax.axis_index("ctx") == 0
     both = jnp.stack([jnp.where(at_first, own, other), jnp.where(at_first, other, own)])
     return both.reshape(1, 2, 1, rows // 4, columns)

time: 55.2 us -> 53.1 us (0.962)
  waiting for transfers between devices: 13.3 us -> 11.7 us
  starting transfers between devices: 23.9 us -> 22.6 us
  Pallas kernels: 16.4 us -> 17 us
    pallas_call x0 -> x1, Pallas kernels: none -> 3.11 us  [rest_call(): pl.pallas_call(functools.partial(rest_kernel, columns - width), out_shape...]
    ppermute x2, waiting for transfers between devices: 1.88 us -> 0.5 us  [trade(): return lax.ppermute(value, 'ctx', [(0, 1), (1, 0)])]
    ppermute x6, waiting for transfers between devices: 10.5 us -> 9.15 us  [swap(): return lax.ppermute(value, 'tp', OUTER)]
    pallas_call x2, Pallas kernels: 5.86 us -> 4.61 us  [attention_call(): pl.pallas_call(functools.partial(kernel, window, heads), out_shape=outs,...]
    pallas_call x1, Pallas kernels: 4.98 us -> 3.81 us  [load(): pl.pallas_call(functools.partial(load_kernel, heads), out_shape=[pltpu.VM...]
    ppermute x7, waiting for transfers between devices: 0.91 us -> 2.07 us  [pair(): return lax.ppermute(value, ('pipe', 'ctx'), [(i, i ^ m) for i in range(8)])]
    ppermute x6, starting transfers between devices: 16.3 us -> 15.2 us  [swap(): return lax.ppermute(value, 'tp', OUTER)]
    ppermute x7, starting transfers between devices: 5.63 us -> 5.06 us  [pair(): return lax.ppermute(value, ('pipe', 'ctx'), [(i, i ^ m) for i in range(8)])]
  transfers between devices with their start and end apart: 19 -> 19, of which waited for: 8 -> 9; matrix products, arithmetic and copies ran while one was open for 1% -> 1% of each run, Pallas kernels for 21% -> 25%
where the time goes in v5:
time: 53.1 us; the launch traced here: 52.9 us
  starting transfers between devices  22.6 us (43%)
  Pallas kernels  17 us (32%)
  waiting for transfers between devices  11.7 us (22%)
  other arithmetic  1.38 us (3%)
    ppermute x6, starting transfers between devices, swap(): return lax.ppermute(value, 'tp', OUTER)  15.2 us
    ppermute x6, waiting for transfers between devices, swap(): return lax.ppermute(value, 'tp', OUTER)  9.15 us
    ppermute x7, starting transfers between devices, pair(): return lax.ppermute(value, ('pipe', 'ctx'), [(i, i ^ m) for i in range(8)])  5.06 us
    pallas_call x2, Pallas kernels, project_call(): pl.pallas_call(functools.partial(project_kernel, len(parts)), out_shape=o...  4.69 us
    pallas_call x2, Pallas kernels, attention_call(): pl.pallas_call(functools.partial(kernel, window, heads), out_shape=outs,...  4.61 us
    pallas_call x1, Pallas kernels, load(): pl.pallas_call(functools.partial(load_kernel, heads), out_shape=[pltpu.VM...  3.81 us
    pallas_call x1, Pallas kernels, rest_call(): pl.pallas_call(functools.partial(rest_kernel, columns - width), out_shape...  3.11 us
    ppermute x2, starting transfers between devices, trade(): return lax.ppermute(value, 'ctx', [(0, 1), (1, 0)])  2.09 us
  transfers between devices with their start and end apart: 19, of which 9 were waited for; matrix products, arithmetic and copies ran while one was open for 1% of the time, Pallas kernels for 25%

profile of v5, /device:TPU:0, one launch (start us, length us, event | category | flops | bytes accessed | tf_op | source)
XLA Modules:
  0.0 52.9 jit_solution(1485576296069981659)
XLA Ops:
  0.0 0.8 %shard_map.56.refs_0_ = bf16[272,128]{1,0:T(8,128)(2,1)S(1)} custom-call(bf16[128,128]{1,0:T(8,128)(2,1)} %bitcast.13, bf16[128,128]{1,0:T(8,128)(2,1)} %bitcast.14, s32[1,128]{1,0:T(1,128)} %bitcast.15), custom_call_target="tpu_custom_call" | custom-call | tf_op jit(solution)/shard_map/pallas_call | solution.py:46
  0.8 3.0 %collective-permute-start = (bf16[272,128]{1,0:T(8,128)(2,1)S(1)}, bf16[272,128]{1,0:T(8,128)(2,1)S(1)}, u32[]{:S(2)}, u32[]{:S(2)}) collective-permute-start(bf16[272,128]{1,0:T(8,128)(2,1)S(1)} %shard_map.56.refs_0_), channel_id=1, source_target_pairs={{0,16},{4,20},{8,24},{12,28},{16,0},{20,4},{24,8},{28,12},{1,17},{... | collective-permute-start | bytes 208904 | tf_op jit(solution)/shard_map/ppermute | solution.py:338
  3.8 1.5 %collective-permute-start.1 = (bf16[272,128]{1,0:T(8,128)(2,1)S(1)}, bf16[272,128]{1,0:T(8,128)(2,1)S(1)}, u32[]{:S(2)}, u32[]{:S(2)}) collective-permute-start(bf16[272,128]{1,0:T(8,128)(2,1)S(1)} %shard_map.56.refs_0_), channel_id=1, source_target_pairs={{0,20},{4,16},{8,28},{12,24},{16,4},{20,0},{24,12},{28,8},{1,21},{... | collective-permute-start | bytes 208904 | tf_op jit(solution)/shard_map/ppermute | solution.py:338
  5.4 3.8 %shard_map.55 = (bf16[2048,2048]{1,0:T(8,128)(2,1)S(1)}, bf16[1024,128]{1,0:T(8,128)(2,1)S(1)}, bf16[1024,128]{1,0:T(8,128)(2,1)S(1)}) custom-call(bf16[2048,4096]{1,0:T(8,128)(2,1)} %weight_ref.4, bf16[2048,128]{1,0:T(8,128)(2,1)} %bitcast.12), custom_call_target="tpu_custom_call" | custom-call | bytes 33554432 | tf_op jit(solution)/shard_map/pallas_call | solution.py:308
  9.2 0.8 %collective-permute-done.2.refs_1_ = bf16[272,128]{1,0:T(8,128)(2,1)S(1)} collective-permute-done((bf16[272,128]{1,0:T(8,128)(2,1)S(1)}, bf16[272,128]{1,0:T(8,128)(2,1)S(1)}, u32[]{:S(2)}, u32[]{:S(2)}) %collective-permute-start.2) | collective-permute-done | bytes 69664 | tf_op jit(solution)/shard_map/ppermute | solution.py:338
  10.0 0.5 collective-permute-start.5
  10.5 0.7 %collective-permute-done.4.refs_3_ = bf16[272,128]{1,0:T(8,128)(2,1)S(1)} collective-permute-done((bf16[272,128]{1,0:T(8,128)(2,1)S(1)}, bf16[272,128]{1,0:T(8,128)(2,1)S(1)}, u32[]{:S(2)}, u32[]{:S(2)}) %collective-permute-start.4) | collective-permute-done | bytes 69664 | tf_op jit(solution)/shard_map/ppermute | solution.py:338
  11.8 2.8 %shard_map.57 = (bf16[64,2048]{1,0:T(8,128)(2,1)S(1)}, bf16[64,2048]{1,0:T(8,128)(2,1)S(1)}, bf16[2048,1024]{1,0:T(8,128)(2,1)S(1)}) custom-call(bf16[1024,128]{1,0:T(8,128)(2,1)S(1)} %get-tuple-element.33.query_ref, bf16[2048,2048]{1,0:T(8,128)(2,1)S(1)} %get-tuple-element.35.loaded_ref.refs_2_.refs_1_, bf16[2048,4096]{1,0:T(8,128)(2,1)} %weight_ref.4, ...), custom_call_target="tpu_custom_call" | custom-call | flops 872415232 | bytes 1048576 | tf_op jit(solution)/shard_map/pallas_call | solution.py:223
  14.6 1.6 %collective-permute-start.8 = (bf16[64,2048]{1,0:T(8,128)(2,1)S(1)}, bf16[64,2048]{1,0:T(8,128)(2,1)S(1)}, u32[]{:S(2)}, u32[]{:S(2)}) collective-permute-start(bf16[64,2048]{1,0:T(8,128)(2,1)S(1)} %get-tuple-element.43), channel_id=1, source_target_pairs={{0,1},{1,0},{2,3},{3,2},{4,5},{5,4},{6,7},{7,6},{8,9},{9,8},{10,11... | collective-permute-start | bytes 786440 | tf_op jit(solution)/shard_map/ppermute | solution.py:324
  16.2 1.4 %collective-permute-start.10 = (bf16[64,2048]{1,0:T(8,128)(2,1)S(1)}, bf16[64,2048]{1,0:T(8,128)(2,1)S(1)}, u32[]{:S(2)}, u32[]{:S(2)}) collective-permute-start(bf16[64,2048]{1,0:T(8,128)(2,1)S(1)} %get-tuple-element.39.rows_ref), channel_id=1, source_target_pairs={{0,4},{4,0},{1,5},{5,1},{2,6},{6,2},{3,7},{7,3},{8,12},{12,8},{9,1... | collective-permute-start | bytes 786440 | tf_op jit(solution)/shard_map/ppermute | solution.py:350
  17.7 3.1 %shard_map.58 = (bf16[64,2048]{1,0:T(8,128)(2,1)S(1)}, bf16[2048,1024]{1,0:T(8,128)(2,1)S(1)}) custom-call(bf16[64,2048]{1,0:T(8,128)(2,1)S(1)} %get-tuple-element.39.rows_ref, bf16[2048,1024]{1,0:T(8,128)(2,1)S(1)} %get-tuple-element.40.loaded_ref.refs_3_.refs_2_, bf16[2048,4096]{1,0:T(8,128)(2,1)} %weight_ref.4), custom_call_target="tpu_custom_call" | custom-call | flops 536870912 | bytes 8388608 | tf_op jit(solution)/shard_map/pallas_call | solution.py:176
  20.8 0.5 collective-permute-start.12
  21.3 1.8 %shard_map.59.refs_0_ = bf16[64,2048]{1,0:T(8,128)(2,1)S(1)} custom-call(bf16[1024,128]{1,0:T(8,128)(2,1)S(1)} %get-tuple-element.42.query_ref, bf16[272,128]{1,0:T(8,128)(2,1)S(1)} %shard_map.56.refs_0_, bf16[272,128]{1,0:T(8,128)(2,1)S(1)} %collective-permute-done.2.refs_1_, bf16[272,128]{1,0:T(8,128)(2,1)S(1)} %collective-permute-done.3.refs_2_, ...), custom_call_target="tpu_custom_call" | custom-call | flops 335544320 | bytes 1048576 | tf_op jit(solution)/shard_map/pallas_call | solution.py:223
  23.1 0.7 %collective-permute-start.7 = (bf16[64,2048]{1,0:T(8,128)(2,1)S(1)}, bf16[64,2048]{1,0:T(8,128)(2,1)S(1)}, u32[]{:S(2)}, u32[]{:S(2)}) collective-permute-start(bf16[64,2048]{1,0:T(8,128)(2,1)S(1)} %shard_map.59.refs_0_), channel_id=1, source_target_pairs={{0,4},{4,0},{1,5},{5,1},{2,6},{6,2},{3,7},{7,3},{8,12},{12,8},{9,1... | collective-permute-start | bytes 786440 | tf_op jit(solution)/shard_map/ppermute | solution.py:350
  24.4 2.3 %shard_map.61 = (bf16[32,4096]{1,0:T(8,128)(2,1)S(1)}, bf16[32,4096]{1,0:T(8,128)(2,1)S(1)}) custom-call(bf16[64,2048]{1,0:T(8,128)(2,1)S(1)} %collective-permute-done.10.refs_0_, bf16[2048,2048]{1,0:T(8,128)(2,1)S(1)} %get-tuple-element.35.loaded_ref.refs_2_.refs_1_, bf16[2048,1024]{1,0:T(8,128)(2,1)S(1)} %get-tuple-element.40.loaded_ref.refs_3_.refs_2_, ...), custom_call_target="tpu_custom_call" | custom-call | flops 1073741824 | bytes 16777216 | tf_op jit(solution)/shard_map/pallas_call | solution.py:251
  26.8 2.7 %collective-permute-start.11 = (bf16[32,4096]{1,0:T(8,128)(2,1)S(1)}, bf16[32,4096]{1,0:T(8,128)(2,1)S(1)}, u32[]{:S(2)}, u32[]{:S(2)}) collective-permute-start(bf16[32,4096]{1,0:T(8,128)(2,1)S(1)} %get-tuple-element.47), channel_id=1, source_target_pairs={{0,1},{1,0},{2,3},{3,2},{4,5},{5,4},{6,7},{7,6},{8,9},{9,8},{10,11... | collective-permute-start | bytes 786440 | tf_op jit(solution)/shard_map/ppermute | solution.py:324
  29.6 2.5 %collective-permute-start.17 = (bf16[32,4096]{1,0:T(8,128)(2,1)S(1)}, bf16[32,4096]{1,0:T(8,128)(2,1)S(1)}, u32[]{:S(2)}, u32[]{:S(2)}) collective-permute-start(bf16[32,4096]{1,0:T(8,128)(2,1)S(1)} %get-tuple-element.56), channel_id=1, source_target_pairs={{0,1},{1,0},{2,3},{3,2},{4,5},{5,4},{6,7},{7,6},{8,9},{9,8},{10,11... | collective-permute-start | bytes 786440 | tf_op jit(solution)/shard_map/ppermute | solution.py:324
  32.1 2.3 %shard_map.60 = (bf16[32,4096]{1,0:T(8,128)(2,1)S(1)}, bf16[32,4096]{1,0:T(8,128)(2,1)S(1)}, bf16[32,4096]{1,0:T(8,128)(2,1)S(1)}, bf16[32,4096]{1,0:T(8,128)(2,1)S(1)}) custom-call(bf16[64,2048]{1,0:T(8,128)(2,1)S(1)} %shard_map.59.refs_0_, bf16[64,2048]{1,0:T(8,128)(2,1)S(1)} %collective-permute-done.7.refs_1_, ...), custom_call_target="tpu_custom_call" | custom-call | flops 2147483648 | bytes 16777216 | tf_op jit(solution)/shard_map/pallas_call | solution.py:251
  34.5 2.2 %collective-permute-done.11 = bf16[32,4096]{1,0:T(8,128)(2,1)S(1)} collective-permute-done((bf16[32,4096]{1,0:T(8,128)(2,1)S(1)}, bf16[32,4096]{1,0:T(8,128)(2,1)S(1)}, u32[]{:S(2)}, u32[]{:S(2)}) %collective-permute-start.11) | collective-permute-done | bytes 262176 | tf_op jit(solution)/shard_map/ppermute | solution.py:324
  37.0 2.5 %collective-permute-start.14 = (bf16[32,4096]{1,0:T(8,128)(2,1)S(1)}, bf16[32,4096]{1,0:T(8,128)(2,1)S(1)}, u32[]{:S(2)}, u32[]{:S(2)}) collective-permute-start(bf16[32,4096]{1,0:T(8,128)(2,1)S(1)} %slice_add_fusion.1), channel_id=1, source_target_pairs={{0,1},{1,0},{2,3},{3,2},{4,5},{5,4},{6,7},{7,6},{8,9},{9,8},{10,11... | collective-permute-start | bytes 786440 | tf_op jit(solution)/shard_map/ppermute | solution.py:324
  39.5 1.8 %collective-permute-done.17 = bf16[32,4096]{1,0:T(8,128)(2,1)S(1)} collective-permute-done((bf16[32,4096]{1,0:T(8,128)(2,1)S(1)}, bf16[32,4096]{1,0:T(8,128)(2,1)S(1)}, u32[]{:S(2)}, u32[]{:S(2)}) %collective-permute-start.17) | collective-permute-done | bytes 262176 | tf_op jit(solution)/shard_map/ppermute | solution.py:324
  41.5 5.3 %collective-permute-start.16 = (bf16[32,4096]{1,0:T(8,128)(2,1)S(1)}, bf16[32,4096]{1,0:T(8,128)(2,1)S(1)}, u32[]{:S(2)}, u32[]{:S(2)}) collective-permute-start(bf16[32,4096]{1,0:T(8,128)(2,1)S(1)} %select_add_fusion.1), channel_id=1, source_target_pairs={{0,1},{1,0},{2,3},{3,2},{4,5},{5,4},{6,7},{7,6},{8,9},{9,8},{10,11... | collective-permute-start | bytes 786440 | tf_op jit(solution)/shard_map/ppermute | solution.py:324
  47.0 4.9 %collective-permute-done.16 = bf16[32,4096]{1,0:T(8,128)(2,1)S(1)} collective-permute-done((bf16[32,4096]{1,0:T(8,128)(2,1)S(1)}, bf16[32,4096]{1,0:T(8,128)(2,1)S(1)}, u32[]{:S(2)}, u32[]{:S(2)}) %collective-permute-start.16) | collective-permute-done | bytes 262176 | tf_op jit(solution)/shard_map/ppermute | solution.py:324
  52.1 0.8 %maximum_bitcast_fusion = bf16[1,2,1,32,4096]{4,3,2,1,0:T(8,128)(2,1)} fusion(bf16[1,32,4096]{2,1,0:T(8,128)(2,1)S(1)} %select_bitcast_fusion, bf16[1,32,4096]{2,1,0:T(8,128)(2,1)S(1)} %get-tuple-element.57), kind=kLoop, calls=%fused_computation.1 | loop fusion | flops 262144 | bytes 1048576 | tf_op jit(solution)/shard_map/reshape | solution.py:378
  (31 shorter events, 2.0 us)
Async XLA Ops:
  0.8 8.4 %collective-permute-start = (bf16[272,128]{1,0:T(8,128)(2,1)S(1)}, bf16[272,128]{1,0:T(8,128)(2,1)S(1)}, u32[]{:S(2)}, u32[]{:S(2)}) collective-permute-start(bf16[272,128]{1,0:T(8,128)(2,1)S(1)} %shard_map.56.refs_0_), channel_id=1, source_target_pairs={{0,16},{4,20},{8,24},{12,28},{16,0},{20,4},{24,8},{28,12},{1,17},{... | collective-permute-start | bytes 208904 | tf_op jit(solution)/shard_map/ppermute | solution.py:338
  3.8 5.4 %collective-permute-start.1 = (bf16[272,128]{1,0:T(8,128)(2,1)S(1)}, bf16[272,128]{1,0:T(8,128)(2,1)S(1)}, u32[]{:S(2)}, u32[]{:S(2)}) collective-permute-start(bf16[272,128]{1,0:T(8,128)(2,1)S(1)} %shard_map.56.refs_0_), channel_id=1, source_target_pairs={{0,20},{4,16},{8,28},{12,24},{16,4},{20,0},{24,12},{28,8},{1,21},{... | collective-permute-start | bytes 208904 | tf_op jit(solution)/shard_map/ppermute | solution.py:338
  5.3 4.7 %collective-permute-start.2 = (bf16[272,128]{1,0:T(8,128)(2,1)S(1)}, bf16[272,128]{1,0:T(8,128)(2,1)S(1)}, u32[]{:S(2)}, u32[]{:S(2)}) collective-permute-start(bf16[272,128]{1,0:T(8,128)(2,1)S(1)} %shard_map.56.refs_0_), channel_id=1, source_target_pairs={{0,4},{4,0},{8,12},{12,8},{16,20},{20,16},{24,28},{28,24},{1,5},{5... | collective-permute-start | bytes 208904 | tf_op jit(solution)/shard_map/ppermute | solution.py:338
  5.4 5.2 %collective-permute-start.3 = (bf16[272,128]{1,0:T(8,128)(2,1)S(1)}, bf16[272,128]{1,0:T(8,128)(2,1)S(1)}, u32[]{:S(2)}, u32[]{:S(2)}) collective-permute-start(bf16[272,128]{1,0:T(8,128)(2,1)S(1)} %shard_map.56.refs_0_), channel_id=1, source_target_pairs={{0,8},{4,12},{8,0},{12,4},{16,24},{20,28},{24,16},{28,20},{1,9},{5... | collective-permute-start | bytes 208904 | tf_op jit(solution)/shard_map/ppermute | solution.py:338
  10.0 1.3 %collective-permute-start.4 = (bf16[272,128]{1,0:T(8,128)(2,1)S(1)}, bf16[272,128]{1,0:T(8,128)(2,1)S(1)}, u32[]{:S(2)}, u32[]{:S(2)}) collective-permute-start(bf16[272,128]{1,0:T(8,128)(2,1)S(1)} %collective-permute-done.2.refs_1_), channel_id=1, source_target_pairs={{0,8},{4,12},{8,0},{12,4},{16,24},{20,28},{24,16},{28,20},{1,9},{5... | collective-permute-start | bytes 208904 | tf_op jit(solution)/shard_map/ppermute | solution.py:338
  10.0 1.4 %collective-permute-start.5 = (bf16[272,128]{1,0:T(8,128)(2,1)S(1)}, bf16[272,128]{1,0:T(8,128)(2,1)S(1)}, u32[]{:S(2)}, u32[]{:S(2)}) collective-permute-start(bf16[272,128]{1,0:T(8,128)(2,1)S(1)} %collective-permute-done.refs_4_), channel_id=1, source_target_pairs={{0,8},{4,12},{8,0},{12,4},{16,24},{20,28},{24,16},{28,20},{1,9},{5... | collective-permute-start | bytes 208904 | tf_op jit(solution)/shard_map/ppermute | solution.py:338
  10.5 1.3 %collective-permute-start.6 = (bf16[272,128]{1,0:T(8,128)(2,1)S(1)}, bf16[272,128]{1,0:T(8,128)(2,1)S(1)}, u32[]{:S(2)}, u32[]{:S(2)}) collective-permute-start(bf16[272,128]{1,0:T(8,128)(2,1)S(1)} %collective-permute-done.1.refs_5_), channel_id=1, source_target_pairs={{0,8},{4,12},{8,0},{12,4},{16,24},{20,28},{24,16},{28,20},{1,9},{5... | collective-permute-start | bytes 208904 | tf_op jit(solution)/shard_map/ppermute | solution.py:338
  14.6 9.2 %collective-permute-start.8 = (bf16[64,2048]{1,0:T(8,128)(2,1)S(1)}, bf16[64,2048]{1,0:T(8,128)(2,1)S(1)}, u32[]{:S(2)}, u32[]{:S(2)}) collective-permute-start(bf16[64,2048]{1,0:T(8,128)(2,1)S(1)} %get-tuple-element.43), channel_id=1, source_target_pairs={{0,1},{1,0},{2,3},{3,2},{4,5},{5,4},{6,7},{7,6},{8,9},{9,8},{10,11... | collective-permute-start | bytes 786440 | tf_op jit(solution)/shard_map/ppermute | solution.py:324
  16.2 8.2 %collective-permute-start.10 = (bf16[64,2048]{1,0:T(8,128)(2,1)S(1)}, bf16[64,2048]{1,0:T(8,128)(2,1)S(1)}, u32[]{:S(2)}, u32[]{:S(2)}) collective-permute-start(bf16[64,2048]{1,0:T(8,128)(2,1)S(1)} %get-tuple-element.39.rows_ref), channel_id=1, source_target_pairs={{0,4},{4,0},{1,5},{5,1},{2,6},{6,2},{3,7},{7,3},{8,12},{12,8},{9,1... | collective-permute-start | bytes 786440 | tf_op jit(solution)/shard_map/ppermute | solution.py:350
  20.8 8.7 %collective-permute-start.12 = (bf16[64,2048]{1,0:T(8,128)(2,1)S(1)}, bf16[64,2048]{1,0:T(8,128)(2,1)S(1)}, u32[]{:S(2)}, u32[]{:S(2)}) collective-permute-start(bf16[64,2048]{1,0:T(8,128)(2,1)S(1)} %get-tuple-element.52), channel_id=1, source_target_pairs={{0,1},{1,0},{2,3},{3,2},{4,5},{5,4},{6,7},{7,6},{8,9},{9,8},{10,11... | collective-permute-start | bytes 786440 | tf_op jit(solution)/shard_map/ppermute | solution.py:324
  23.1 9.0 %collective-permute-start.7 = (bf16[64,2048]{1,0:T(8,128)(2,1)S(1)}, bf16[64,2048]{1,0:T(8,128)(2,1)S(1)}, u32[]{:S(2)}, u32[]{:S(2)}) collective-permute-start(bf16[64,2048]{1,0:T(8,128)(2,1)S(1)} %shard_map.59.refs_0_), channel_id=1, source_target_pairs={{0,4},{4,0},{1,5},{5,1},{2,6},{6,2},{3,7},{7,3},{8,12},{12,8},{9,1... | collective-permute-start | bytes 786440 | tf_op jit(solution)/shard_map/ppermute | solution.py:350
  23.8 8.3 %collective-permute-start.9 = (bf16[64,2048]{1,0:T(8,128)(2,1)S(1)}, bf16[64,2048]{1,0:T(8,128)(2,1)S(1)}, u32[]{:S(2)}, u32[]{:S(2)}) collective-permute-start(bf16[64,2048]{1,0:T(8,128)(2,1)S(1)} %add.30), channel_id=1, source_target_pairs={{0,8},{1,2},{2,1},{3,11},{4,12},{5,6},{6,5},{7,15},{8,0},{9,10},{1... | collective-permute-start | bytes 786440 | tf_op jit(solution)/shard_map/ppermute | solution.py:328
  26.8 9.9 %collective-permute-start.11 = (bf16[32,4096]{1,0:T(8,128)(2,1)S(1)}, bf16[32,4096]{1,0:T(8,128)(2,1)S(1)}, u32[]{:S(2)}, u32[]{:S(2)}) collective-permute-start(bf16[32,4096]{1,0:T(8,128)(2,1)S(1)} %get-tuple-element.47), channel_id=1, source_target_pairs={{0,1},{1,0},{2,3},{3,2},{4,5},{5,4},{6,7},{7,6},{8,9},{9,8},{10,11... | collective-permute-start | bytes 786440 | tf_op jit(solution)/shard_map/ppermute | solution.py:324
  29.6 7.3 %collective-permute-start.13 = (bf16[64,2048]{1,0:T(8,128)(2,1)S(1)}, bf16[64,2048]{1,0:T(8,128)(2,1)S(1)}, u32[]{:S(2)}, u32[]{:S(2)}) collective-permute-start(bf16[64,2048]{1,0:T(8,128)(2,1)S(1)} %add.31), channel_id=1, source_target_pairs={{0,8},{1,2},{2,1},{3,11},{4,12},{5,6},{6,5},{7,15},{8,0},{9,10},{1... | collective-permute-start | bytes 786440 | tf_op jit(solution)/shard_map/ppermute | solution.py:328
  29.6 11.7 %collective-permute-start.17 = (bf16[32,4096]{1,0:T(8,128)(2,1)S(1)}, bf16[32,4096]{1,0:T(8,128)(2,1)S(1)}, u32[]{:S(2)}, u32[]{:S(2)}) collective-permute-start(bf16[32,4096]{1,0:T(8,128)(2,1)S(1)} %get-tuple-element.56), channel_id=1, source_target_pairs={{0,1},{1,0},{2,3},{3,2},{4,5},{5,4},{6,7},{7,6},{8,9},{9,8},{10,11... | collective-permute-start | bytes 786440 | tf_op jit(solution)/shard_map/ppermute | solution.py:324
  36.8 4.7 %collective-permute-start.15 = (bf16[32,4096]{1,0:T(8,128)(2,1)S(1)}, bf16[32,4096]{1,0:T(8,128)(2,1)S(1)}, u32[]{:S(2)}, u32[]{:S(2)}) collective-permute-start(bf16[32,4096]{1,0:T(8,128)(2,1)S(1)} %add.35), channel_id=1, source_target_pairs={{0,8},{1,2},{2,1},{3,11},{4,12},{5,6},{6,5},{7,15},{8,0},{9,10},{1... | collective-permute-start | bytes 786440 | tf_op jit(solution)/shard_map/ppermute | solution.py:328
  37.0 10.0 %collective-permute-start.14 = (bf16[32,4096]{1,0:T(8,128)(2,1)S(1)}, bf16[32,4096]{1,0:T(8,128)(2,1)S(1)}, u32[]{:S(2)}, u32[]{:S(2)}) collective-permute-start(bf16[32,4096]{1,0:T(8,128)(2,1)S(1)} %slice_add_fusion.1), channel_id=1, source_target_pairs={{0,1},{1,0},{2,3},{3,2},{4,5},{5,4},{6,7},{7,6},{8,9},{9,8},{10,11... | collective-permute-start | bytes 786440 | tf_op jit(solution)/shard_map/ppermute | solution.py:324
  41.4 5.6 %collective-permute-start.18 = (bf16[32,4096]{1,0:T(8,128)(2,1)S(1)}, bf16[32,4096]{1,0:T(8,128)(2,1)S(1)}, u32[]{:S(2)}, u32[]{:S(2)}) collective-permute-start(bf16[32,4096]{1,0:T(8,128)(2,1)S(1)} %add.38), channel_id=1, source_target_pairs={{0,8},{1,2},{2,1},{3,11},{4,12},{5,6},{6,5},{7,15},{8,0},{9,10},{1... | collective-permute-start | bytes 786440 | tf_op jit(solution)/shard_map/ppermute | solution.py:328
  41.5 10.4 %collective-permute-start.16 = (bf16[32,4096]{1,0:T(8,128)(2,1)S(1)}, bf16[32,4096]{1,0:T(8,128)(2,1)S(1)}, u32[]{:S(2)}, u32[]{:S(2)}) collective-permute-start(bf16[32,4096]{1,0:T(8,128)(2,1)S(1)} %select_add_fusion.1), channel_id=1, source_target_pairs={{0,1},{1,0},{2,3},{3,2},{4,5},{5,4},{6,7},{7,6},{8,9},{9,8},{10,11... | collective-permute-start | bytes 786440 | tf_op jit(solution)/shard_map/ppermute | solution.py:324

commit v6 on v5

--- a/solution.py
+++ b/solution.py
@@ -12,7 +12,7 @@
 LOG2E = 1.4426950408889634
 MIB = 1 << 20
 
-WEIGHT_CUTS = 4
+WEIGHT_CUTS = 2
 OUTER = ((0, 1), (1, 0), (2, 3), (3, 2))
 INNER = tuple(
     (p * 8 + c * 4 + t, p * 8 + c * 4 + 3 - t if t in (1, 2) else (p ^ 1) * 8 + c * 4 + t)
@@ -80,9 +80,15 @@
     half = 2 * quarter
     mine = lax.axis_index(("pipe", "ctx"))
 
-    keys[...] = jnp.zeros_like(keys)
-    values[...] = jnp.zeros_like(values)
-    marks[...] = jnp.full_like(marks, -1.0)
+    for s in range(window - 1):
+
+        @pl.when(mine + s < window - 1)
+        def _(s=s):
+            at = slice(s * rows, (s + 1) * rows)
+            keys[at] = jnp.zeros((rows, width), BF16)
+            values[at, :] = jnp.zeros((rows, width), BF16)
+            marks[s] = jnp.full((8, rows), -1.0, F32)
+
     for m in range(8):
         slot = (mine ^ m) - mine + window - 1
 
@@ -324,6 +330,10 @@
     return lax.ppermute(value, "tp", OUTER)
 
 
+def send(value):
+    return lax.ppermute(value, "tp", ((0, 1), (3, 2)))
+
+
 def swap_inner(value):
     return lax.ppermute(value, ("pipe", "ctx", "tp"), INNER)
 
@@ -331,7 +341,7 @@
 def shards_line(query_rows, key_rows, value_rows, doc_ids, out_weight):
     rows, heads, width = query_rows.shape
     columns = out_weight.shape[1]
-    window = 5
+    window = (lax.axis_size("pipe") * lax.axis_size("ctx")) // 2 + 1
     packed = pack(key_rows, value_rows, doc_ids)
 
     def pair(value, m):
@@ -343,7 +353,9 @@
     line = lax.axis_index("tp")
     weight_here, inside = after((out_weight, (line == 1) | (line == 2)))
     weight, far_query, near_query = load(weight_here, query_rows)
-    by_x, by_both, by_y, weight = after((by_x, by_both, by_y, weight))
+    by_both, weight = after((by_both, weight))
+    by_x, weight = after((by_x, weight))
+    by_y, weight = after((by_y, weight))
     blocks = [packed, by_y, by_core, pair(by_y, 2), by_x, by_both, pair(by_x, 2), pair(by_both, 2)]
 
     def trade(value):
@@ -353,26 +365,31 @@
         return jnp.where(inside, value, jnp.zeros_like(value))
 
     far_rows, early, part = attention_call(far_query, blocks, window, (weight, out_weight))
+    early_rest, last = rest_call(far_rows, part, out_weight)
+    weights = (weight, part, last)
     early_in = swap(early)
     other_far = trade(far_rows)
-    early_rest, last = rest_call(far_rows, part, out_weight)
-    weights = (weight, part, last)
-    near_query, early_rest = after((near_query, early_rest))
+    passed_on = swap_inner(early + early_in)
+    rest_in = swap(early_rest)
+    late_first, late_second = project_call([other_far], weights)
+    first_in = swap(late_first)
+    second_in = send(late_second)
+    passed_rest = swap_inner(early_rest + rest_in)
+    late_near = swap_inner(late_second + second_in)
+    near_query, _ = after((near_query, early_rest))
+    quarter = rows // 4
+    both = passed(jnp.concatenate([passed_on, passed_rest], axis=1))
     (near_rows,) = attention_call(near_query, blocks, window)
     other_near = trade(near_rows)
-
-    passed_on = swap_inner(early + early_in)
-    late_first, late_second = project_call([other_far], weights)
-    other_near, passed_on = after((other_near, passed_on))
+    other_near, _ = after((other_near, passed_on))
     third, kept, late_third, late_kept = project_call([near_rows, other_near], weights)
-    passed_rest = swap_inner(early_rest + swap(early_rest))
-    late_in, third = after((swap(late_first), third))
-    late_far = swap_inner(late_first + late_in)
-    late_near = swap_inner(late_second + swap(late_second))
-    both = passed(jnp.concatenate([passed_on, passed_rest], axis=1))
-    quarter = rows // 4
-    own = kept + swap(third + both[:quarter]) + both[quarter:]
-    other = late_kept + swap(late_third + passed(late_far)) + passed(late_near)
+    first_in, _ = after((first_in, third))
+    late_far = swap_inner(late_first + first_in)
+    last_in = swap(late_third + passed(late_far))
+    other = late_kept + last_in + passed(late_near)
+    third_in = swap(third + both[:quarter])
+    third_in, _ = after((third_in, last_in))
+    own = kept + third_in + both[quarter:]
     at_first = lax.axis_index("ctx") == 0
     both = jnp.stack([jnp.where(at_first, own, other), jnp.where(at_first, other, own)])
     return both.reshape(1, 2, 1, rows // 4, columns)

time: 53.1 us -> 52.3 us (0.985)
  waiting for transfers between devices: 11.7 us -> 9.72 us
  starting transfers between devices: 22.6 us -> 24.1 us
    ppermute x0 -> x1, starting transfers between devices: none -> 4.87 us  [send(): return lax.ppermute(value, 'tp', ((0, 1), (3, 2)))]
    ppermute x6 -> x5, starting transfers between devices: 15.2 us -> 11.8 us  [swap(): return lax.ppermute(value, 'tp', OUTER)]
    ppermute x6 -> x5, waiting for transfers between devices: 9.15 us -> 7.11 us  [swap(): return lax.ppermute(value, 'tp', OUTER)]
    ppermute x2, waiting for transfers between devices: 0.5 us -> 1.16 us  [trade(): return lax.ppermute(value, 'ctx', [(0, 1), (1, 0)])]
    ppermute x7, waiting for transfers between devices: 2.07 us -> 1.44 us  [pair(): return lax.ppermute(value, ('pipe', 'ctx'), [(i, i ^ m) for i in range(8)])]
  transfers between devices with their start and end apart: 19 -> 19, of which waited for: 9 -> 7; matrix products, arithmetic and copies ran while one was open for 1% -> 1% of each run, Pallas kernels for 25% -> 25%
where the time goes in v6:
time: 52.3 us; the launch traced here: 52.1 us
  starting transfers between devices  24.1 us (46%)
  Pallas kernels  16.7 us (32%)
  waiting for transfers between devices  9.72 us (19%)
  other arithmetic  1.38 us (3%)
    ppermute x5, starting transfers between devices, swap(): return lax.ppermute(value, 'tp', OUTER)  11.8 us
    ppermute x5, waiting for transfers between devices, swap(): return lax.ppermute(value, 'tp', OUTER)  7.11 us
    ppermute x7, starting transfers between devices, pair(): return lax.ppermute(value, ('pipe', 'ctx'), [(i, i ^ m) for i in range(8)])  5.32 us
    ppermute x1, starting transfers between devices, send(): return lax.ppermute(value, 'tp', ((0, 1), (3, 2)))  4.87 us
    pallas_call x2, Pallas kernels, project_call(): pl.pallas_call(functools.partial(project_kernel, len(parts)), out_shape=o...  4.69 us
    pallas_call x2, Pallas kernels, attention_call(): pl.pallas_call(functools.partial(kernel, window, heads), out_shape=outs,...  4.39 us
    pallas_call x1, Pallas kernels, load(): pl.pallas_call(functools.partial(load_kernel, heads), out_shape=[pltpu.VM...  3.79 us
    pallas_call x1, Pallas kernels, rest_call(): pl.pallas_call(functools.partial(rest_kernel, columns - width), out_shape...  3 us
  transfers between devices with their start and end apart: 19, of which 7 were waited for; matrix products, arithmetic and copies ran while one was open for 1% of the time, Pallas kernels for 25%

profile of v6, /device:TPU:0, one launch (start us, length us, event | category | flops | bytes accessed | tf_op | source)
XLA Modules:
  0.0 52.1 jit_solution(6855763618486717960)
XLA Ops:
  0.0 0.8 %shard_map.56.refs_0_ = bf16[272,128]{1,0:T(8,128)(2,1)S(1)} custom-call(bf16[128,128]{1,0:T(8,128)(2,1)} %bitcast.13, bf16[128,128]{1,0:T(8,128)(2,1)} %bitcast.14, s32[1,128]{1,0:T(1,128)} %bitcast.15), custom_call_target="tpu_custom_call" | custom-call | tf_op jit(solution)/shard_map/pallas_call | solution.py:46
  0.8 4.0 %collective-permute-start.2 = (bf16[272,128]{1,0:T(8,128)(2,1)S(1)}, bf16[272,128]{1,0:T(8,128)(2,1)S(1)}, u32[]{:S(2)}, u32[]{:S(2)}) collective-permute-start(bf16[272,128]{1,0:T(8,128)(2,1)S(1)} %shard_map.56.refs_0_), channel_id=1, source_target_pairs={{0,20},{4,16},{8,28},{12,24},{16,4},{20,0},{24,12},{28,8},{1,21},{... | collective-permute-start | bytes 208904 | tf_op jit(solution)/shard_map/ppermute | solution.py:348
  4.8 0.5 %collective-permute-start.1 = (bf16[272,128]{1,0:T(8,128)(2,1)S(1)}, bf16[272,128]{1,0:T(8,128)(2,1)S(1)}, u32[]{:S(2)}, u32[]{:S(2)}) collective-permute-start(bf16[272,128]{1,0:T(8,128)(2,1)S(1)} %shard_map.56.refs_0_), channel_id=1, source_target_pairs={{0,16},{4,20},{8,24},{12,28},{16,0},{20,4},{24,8},{28,12},{1,17},{... | collective-permute-start | bytes 208904 | tf_op jit(solution)/shard_map/ppermute | solution.py:348
  5.4 3.8 %shard_map.55 = (bf16[2048,2048]{1,0:T(8,128)(2,1)S(1)}, bf16[1024,128]{1,0:T(8,128)(2,1)S(1)}, bf16[1024,128]{1,0:T(8,128)(2,1)S(1)}) custom-call(bf16[2048,4096]{1,0:T(8,128)(2,1)} %weight_ref.4, bf16[2048,128]{1,0:T(8,128)(2,1)} %bitcast.12), custom_call_target="tpu_custom_call" | custom-call | bytes 33554432 | tf_op jit(solution)/shard_map/pallas_call | solution.py:314
  9.2 0.4 collective-permute-done.refs_1_
  10.3 0.5 %collective-permute-done.4.refs_3_ = bf16[272,128]{1,0:T(8,128)(2,1)S(1)} collective-permute-done((bf16[272,128]{1,0:T(8,128)(2,1)S(1)}, bf16[272,128]{1,0:T(8,128)(2,1)S(1)}, u32[]{:S(2)}, u32[]{:S(2)}) %collective-permute-start.4) | collective-permute-done | bytes 69664 | tf_op jit(solution)/shard_map/ppermute | solution.py:348
  11.1 0.3 collective-permute-done.6.refs_7_
  11.4 2.8 %shard_map.57 = (bf16[64,2048]{1,0:T(8,128)(2,1)S(1)}, bf16[64,2048]{1,0:T(8,128)(2,1)S(1)}, bf16[2048,1024]{1,0:T(8,128)(2,1)S(1)}) custom-call(bf16[1024,128]{1,0:T(8,128)(2,1)S(1)} %get-tuple-element.33.query_ref, bf16[2048,2048]{1,0:T(8,128)(2,1)S(1)} %get-tuple-element.37.loaded_ref.refs_2_.refs_1_, bf16[2048,4096]{1,0:T(8,128)(2,1)} %weight_ref.4, ...), custom_call_target="tpu_custom_call" | custom-call | flops 872415232 | bytes 1048576 | tf_op jit(solution)/shard_map/pallas_call | solution.py:229
  14.2 1.9 %collective-permute-start.8 = (bf16[64,2048]{1,0:T(8,128)(2,1)S(1)}, bf16[64,2048]{1,0:T(8,128)(2,1)S(1)}, u32[]{:S(2)}, u32[]{:S(2)}) collective-permute-start(bf16[64,2048]{1,0:T(8,128)(2,1)S(1)} %get-tuple-element.45), channel_id=1, source_target_pairs={{0,1},{1,0},{2,3},{3,2},{4,5},{5,4},{6,7},{7,6},{8,9},{9,8},{10,11... | collective-permute-start | bytes 786440 | tf_op jit(solution)/shard_map/ppermute | solution.py:330
  16.1 1.5 %collective-permute-start.13 = (bf16[64,2048]{1,0:T(8,128)(2,1)S(1)}, bf16[64,2048]{1,0:T(8,128)(2,1)S(1)}, u32[]{:S(2)}, u32[]{:S(2)}) collective-permute-start(bf16[64,2048]{1,0:T(8,128)(2,1)S(1)} %get-tuple-element.41.rows_ref), channel_id=1, source_target_pairs={{0,4},{4,0},{1,5},{5,1},{2,6},{6,2},{3,7},{7,3},{8,12},{12,8},{9,1... | collective-permute-start | bytes 786440 | tf_op jit(solution)/shard_map/ppermute | solution.py:362
  17.6 3.0 %shard_map.58 = (bf16[64,2048]{1,0:T(8,128)(2,1)S(1)}, bf16[2048,1024]{1,0:T(8,128)(2,1)S(1)}) custom-call(bf16[64,2048]{1,0:T(8,128)(2,1)S(1)} %get-tuple-element.41.rows_ref, bf16[2048,1024]{1,0:T(8,128)(2,1)S(1)} %get-tuple-element.42.loaded_ref.refs_3_.refs_2_, bf16[2048,4096]{1,0:T(8,128)(2,1)} %weight_ref.4), custom_call_target="tpu_custom_call" | custom-call | flops 536870912 | bytes 8388608 | tf_op jit(solution)/shard_map/pallas_call | solution.py:182
  20.6 0.5 collective-permute-start.10
  21.1 1.6 %shard_map.59.refs_0_ = bf16[64,2048]{1,0:T(8,128)(2,1)S(1)} custom-call(bf16[1024,128]{1,0:T(8,128)(2,1)S(1)} %get-tuple-element.44.query_ref, bf16[272,128]{1,0:T(8,128)(2,1)S(1)} %shard_map.56.refs_0_, bf16[272,128]{1,0:T(8,128)(2,1)S(1)} %collective-permute-done.refs_1_, bf16[272,128]{1,0:T(8,128)(2,1)S(1)} %collective-permute-done.3.refs_2_, ...), custom_call_target="tpu_custom_call" | custom-call | flops 335544320 | bytes 1048576 | tf_op jit(solution)/shard_map/pallas_call | solution.py:229
  22.7 0.3 collective-permute-start.7
  23.2 1.2 %collective-permute-done.13.refs_0_ = bf16[64,2048]{1,0:T(8,128)(2,1)S(1)} collective-permute-done((bf16[64,2048]{1,0:T(8,128)(2,1)S(1)}, bf16[64,2048]{1,0:T(8,128)(2,1)S(1)}, u32[]{:S(2)}, u32[]{:S(2)}) %collective-permute-start.13) | collective-permute-done | bytes 262176 | tf_op jit(solution)/shard_map/ppermute | solution.py:362
  24.4 2.4 %shard_map.61 = (bf16[32,4096]{1,0:T(8,128)(2,1)S(1)}, bf16[32,4096]{1,0:T(8,128)(2,1)S(1)}) custom-call(bf16[64,2048]{1,0:T(8,128)(2,1)S(1)} %collective-permute-done.13.refs_0_, bf16[2048,2048]{1,0:T(8,128)(2,1)S(1)} %get-tuple-element.37.loaded_ref.refs_2_.refs_1_, bf16[2048,1024]{1,0:T(8,128)(2,1)S(1)} %get-tuple-element.42.loaded_ref.refs_3_.refs_2_, ...), custom_call_target="tpu_custom_call" | custom-call | flops 1073741824 | bytes 16777216 | tf_op jit(solution)/shard_map/pallas_call | solution.py:257
  26.7 2.3 %collective-permute-start.14 = (bf16[32,4096]{1,0:T(8,128)(2,1)S(1)}, bf16[32,4096]{1,0:T(8,128)(2,1)S(1)}, u32[]{:S(2)}, u32[]{:S(2)}) collective-permute-start(bf16[32,4096]{1,0:T(8,128)(2,1)S(1)} %get-tuple-element.52), channel_id=1, source_target_pairs={{0,1},{1,0},{2,3},{3,2},{4,5},{5,4},{6,7},{7,6},{8,9},{9,8},{10,11... | collective-permute-start | bytes 786440 | tf_op jit(solution)/shard_map/ppermute | solution.py:330
  29.2 4.9 %collective-permute-start.17 = (bf16[32,4096]{1,0:T(8,128)(2,1)S(1)}, bf16[32,4096]{1,0:T(8,128)(2,1)S(1)}, u32[]{:S(2)}, u32[]{:S(2)}) collective-permute-start(bf16[32,4096]{1,0:T(8,128)(2,1)S(1)} %get-tuple-element.56), channel_id=1, source_target_pairs={{0,1},{3,2},{4,5},{7,6},{8,9},{11,10},{12,13},{15,14},{16,17},{19,... | collective-permute-start | bytes 786440 | tf_op jit(solution)/shard_map/ppermute | solution.py:334
  34.1 2.3 %shard_map.60 = (bf16[32,4096]{1,0:T(8,128)(2,1)S(1)}, bf16[32,4096]{1,0:T(8,128)(2,1)S(1)}, bf16[32,4096]{1,0:T(8,128)(2,1)S(1)}, bf16[32,4096]{1,0:T(8,128)(2,1)S(1)}) custom-call(bf16[64,2048]{1,0:T(8,128)(2,1)S(1)} %shard_map.59.refs_0_, bf16[64,2048]{1,0:T(8,128)(2,1)S(1)} %collective-permute-done.7.refs_1_, ...), custom_call_target="tpu_custom_call" | custom-call | flops 2147483648 | bytes 16777216 | tf_op jit(solution)/shard_map/pallas_call | solution.py:257
  36.7 2.7 %collective-permute-start.12 = (bf16[32,4096]{1,0:T(8,128)(2,1)S(1)}, bf16[32,4096]{1,0:T(8,128)(2,1)S(1)}, u32[]{:S(2)}, u32[]{:S(2)}) collective-permute-start(bf16[32,4096]{1,0:T(8,128)(2,1)S(1)} %slice_add_fusion.1), channel_id=1, source_target_pairs={{0,1},{1,0},{2,3},{3,2},{4,5},{5,4},{6,7},{7,6},{8,9},{9,8},{10,11... | collective-permute-start | bytes 786440 | tf_op jit(solution)/shard_map/ppermute | solution.py:330
  39.5 4.4 %collective-permute-start.16 = (bf16[32,4096]{1,0:T(8,128)(2,1)S(1)}, bf16[32,4096]{1,0:T(8,128)(2,1)S(1)}, u32[]{:S(2)}, u32[]{:S(2)}) collective-permute-start(bf16[32,4096]{1,0:T(8,128)(2,1)S(1)} %select_add_fusion.1), channel_id=1, source_target_pairs={{0,1},{1,0},{2,3},{3,2},{4,5},{5,4},{6,7},{7,6},{8,9},{9,8},{10,11... | collective-permute-start | bytes 786440 | tf_op jit(solution)/shard_map/ppermute | solution.py:330
  44.0 2.6 %collective-permute-done.12 = bf16[32,4096]{1,0:T(8,128)(2,1)S(1)} collective-permute-done((bf16[32,4096]{1,0:T(8,128)(2,1)S(1)}, bf16[32,4096]{1,0:T(8,128)(2,1)S(1)}, u32[]{:S(2)}, u32[]{:S(2)}) %collective-permute-start.12) | collective-permute-done | bytes 262176 | tf_op jit(solution)/shard_map/ppermute | solution.py:330
  46.7 4.5 %collective-permute-done.16 = bf16[32,4096]{1,0:T(8,128)(2,1)S(1)} collective-permute-done((bf16[32,4096]{1,0:T(8,128)(2,1)S(1)}, bf16[32,4096]{1,0:T(8,128)(2,1)S(1)}, u32[]{:S(2)}, u32[]{:S(2)}) %collective-permute-start.16) | collective-permute-done | bytes 262176 | tf_op jit(solution)/shard_map/ppermute | solution.py:330
  51.3 0.8 %maximum_bitcast_fusion = bf16[1,2,1,32,4096]{4,3,2,1,0:T(8,128)(2,1)} fusion(bf16[1,32,4096]{2,1,0:T(8,128)(2,1)S(1)} %select_bitcast_fusion, bf16[1,32,4096]{2,1,0:T(8,128)(2,1)S(1)} %get-tuple-element.57), kind=kLoop, calls=%fused_computation.1 | loop fusion | flops 262144 | bytes 1048576 | tf_op jit(solution)/shard_map/reshape | solution.py:395
  (31 shorter events, 1.9 us)
Async XLA Ops:
  0.8 8.4 %collective-permute-start.2 = (bf16[272,128]{1,0:T(8,128)(2,1)S(1)}, bf16[272,128]{1,0:T(8,128)(2,1)S(1)}, u32[]{:S(2)}, u32[]{:S(2)}) collective-permute-start(bf16[272,128]{1,0:T(8,128)(2,1)S(1)} %shard_map.56.refs_0_), channel_id=1, source_target_pairs={{0,20},{4,16},{8,28},{12,24},{16,4},{20,0},{24,12},{28,8},{1,21},{... | collective-permute-start | bytes 208904 | tf_op jit(solution)/shard_map/ppermute | solution.py:348
  4.8 4.5 %collective-permute-start.1 = (bf16[272,128]{1,0:T(8,128)(2,1)S(1)}, bf16[272,128]{1,0:T(8,128)(2,1)S(1)}, u32[]{:S(2)}, u32[]{:S(2)}) collective-permute-start(bf16[272,128]{1,0:T(8,128)(2,1)S(1)} %shard_map.56.refs_0_), channel_id=1, source_target_pairs={{0,16},{4,20},{8,24},{12,28},{16,0},{20,4},{24,8},{28,12},{1,17},{... | collective-permute-start | bytes 208904 | tf_op jit(solution)/shard_map/ppermute | solution.py:348
  5.3 4.3 %collective-permute-start = (bf16[272,128]{1,0:T(8,128)(2,1)S(1)}, bf16[272,128]{1,0:T(8,128)(2,1)S(1)}, u32[]{:S(2)}, u32[]{:S(2)}) collective-permute-start(bf16[272,128]{1,0:T(8,128)(2,1)S(1)} %shard_map.56.refs_0_), channel_id=1, source_target_pairs={{0,4},{4,0},{8,12},{12,8},{16,20},{20,16},{24,28},{28,24},{1,5},{5... | collective-permute-start | bytes 208904 | tf_op jit(solution)/shard_map/ppermute | solution.py:348
  5.4 4.9 %collective-permute-start.3 = (bf16[272,128]{1,0:T(8,128)(2,1)S(1)}, bf16[272,128]{1,0:T(8,128)(2,1)S(1)}, u32[]{:S(2)}, u32[]{:S(2)}) collective-permute-start(bf16[272,128]{1,0:T(8,128)(2,1)S(1)} %shard_map.56.refs_0_), channel_id=1, source_target_pairs={{0,8},{4,12},{8,0},{12,4},{16,24},{20,28},{24,16},{28,20},{1,9},{5... | collective-permute-start | bytes 208904 | tf_op jit(solution)/shard_map/ppermute | solution.py:348
  9.6 1.3 %collective-permute-start.4 = (bf16[272,128]{1,0:T(8,128)(2,1)S(1)}, bf16[272,128]{1,0:T(8,128)(2,1)S(1)}, u32[]{:S(2)}, u32[]{:S(2)}) collective-permute-start(bf16[272,128]{1,0:T(8,128)(2,1)S(1)} %collective-permute-done.refs_1_), channel_id=1, source_target_pairs={{0,8},{4,12},{8,0},{12,4},{16,24},{20,28},{24,16},{28,20},{1,9},{5... | collective-permute-start | bytes 208904 | tf_op jit(solution)/shard_map/ppermute | solution.py:348
  9.8 1.3 %collective-permute-start.5 = (bf16[272,128]{1,0:T(8,128)(2,1)S(1)}, bf16[272,128]{1,0:T(8,128)(2,1)S(1)}, u32[]{:S(2)}, u32[]{:S(2)}) collective-permute-start(bf16[272,128]{1,0:T(8,128)(2,1)S(1)} %collective-permute-done.1.refs_4_), channel_id=1, source_target_pairs={{0,8},{4,12},{8,0},{12,4},{16,24},{20,28},{24,16},{28,20},{1,9},{5... | collective-permute-start | bytes 208904 | tf_op jit(solution)/shard_map/ppermute | solution.py:348
  10.1 1.3 %collective-permute-start.6 = (bf16[272,128]{1,0:T(8,128)(2,1)S(1)}, bf16[272,128]{1,0:T(8,128)(2,1)S(1)}, u32[]{:S(2)}, u32[]{:S(2)}) collective-permute-start(bf16[272,128]{1,0:T(8,128)(2,1)S(1)} %collective-permute-done.2.refs_5_), channel_id=1, source_target_pairs={{0,8},{4,12},{8,0},{12,4},{16,24},{20,28},{24,16},{28,20},{1,9},{5... | collective-permute-start | bytes 208904 | tf_op jit(solution)/shard_map/ppermute | solution.py:348
  14.2 8.9 %collective-permute-start.8 = (bf16[64,2048]{1,0:T(8,128)(2,1)S(1)}, bf16[64,2048]{1,0:T(8,128)(2,1)S(1)}, u32[]{:S(2)}, u32[]{:S(2)}) collective-permute-start(bf16[64,2048]{1,0:T(8,128)(2,1)S(1)} %get-tuple-element.45), channel_id=1, source_target_pairs={{0,1},{1,0},{2,3},{3,2},{4,5},{5,4},{6,7},{7,6},{8,9},{9,8},{10,11... | collective-permute-start | bytes 786440 | tf_op jit(solution)/shard_map/ppermute | solution.py:330
  16.1 8.3 %collective-permute-start.13 = (bf16[64,2048]{1,0:T(8,128)(2,1)S(1)}, bf16[64,2048]{1,0:T(8,128)(2,1)S(1)}, u32[]{:S(2)}, u32[]{:S(2)}) collective-permute-start(bf16[64,2048]{1,0:T(8,128)(2,1)S(1)} %get-tuple-element.41.rows_ref), channel_id=1, source_target_pairs={{0,4},{4,0},{1,5},{5,1},{2,6},{6,2},{3,7},{7,3},{8,12},{12,8},{9,1... | collective-permute-start | bytes 786440 | tf_op jit(solution)/shard_map/ppermute | solution.py:362
  20.6 8.4 %collective-permute-start.10 = (bf16[64,2048]{1,0:T(8,128)(2,1)S(1)}, bf16[64,2048]{1,0:T(8,128)(2,1)S(1)}, u32[]{:S(2)}, u32[]{:S(2)}) collective-permute-start(bf16[64,2048]{1,0:T(8,128)(2,1)S(1)} %get-tuple-element.43), channel_id=1, source_target_pairs={{0,1},{1,0},{2,3},{3,2},{4,5},{5,4},{6,7},{7,6},{8,9},{9,8},{10,11... | collective-permute-start | bytes 786440 | tf_op jit(solution)/shard_map/ppermute | solution.py:330
  22.7 11.3 %collective-permute-start.7 = (bf16[64,2048]{1,0:T(8,128)(2,1)S(1)}, bf16[64,2048]{1,0:T(8,128)(2,1)S(1)}, u32[]{:S(2)}, u32[]{:S(2)}) collective-permute-start(bf16[64,2048]{1,0:T(8,128)(2,1)S(1)} %shard_map.59.refs_0_), channel_id=1, source_target_pairs={{0,4},{4,0},{1,5},{5,1},{2,6},{6,2},{3,7},{7,3},{8,12},{12,8},{9,1... | collective-permute-start | bytes 786440 | tf_op jit(solution)/shard_map/ppermute | solution.py:362
  23.1 10.9 %collective-permute-start.9 = (bf16[64,2048]{1,0:T(8,128)(2,1)S(1)}, bf16[64,2048]{1,0:T(8,128)(2,1)S(1)}, u32[]{:S(2)}, u32[]{:S(2)}) collective-permute-start(bf16[64,2048]{1,0:T(8,128)(2,1)S(1)} %add.30), channel_id=1, source_target_pairs={{0,8},{1,2},{2,1},{3,11},{4,12},{5,6},{6,5},{7,15},{8,0},{9,10},{1... | collective-permute-start | bytes 786440 | tf_op jit(solution)/shard_map/ppermute | solution.py:338
  26.7 9.7 %collective-permute-start.14 = (bf16[32,4096]{1,0:T(8,128)(2,1)S(1)}, bf16[32,4096]{1,0:T(8,128)(2,1)S(1)}, u32[]{:S(2)}, u32[]{:S(2)}) collective-permute-start(bf16[32,4096]{1,0:T(8,128)(2,1)S(1)} %get-tuple-element.52), channel_id=1, source_target_pairs={{0,1},{1,0},{2,3},{3,2},{4,5},{5,4},{6,7},{7,6},{8,9},{9,8},{10,11... | collective-permute-start | bytes 786440 | tf_op jit(solution)/shard_map/ppermute | solution.py:330
  29.1 7.5 %collective-permute-start.11 = (bf16[64,2048]{1,0:T(8,128)(2,1)S(1)}, bf16[64,2048]{1,0:T(8,128)(2,1)S(1)}, u32[]{:S(2)}, u32[]{:S(2)}) collective-permute-start(bf16[64,2048]{1,0:T(8,128)(2,1)S(1)} %add.31), channel_id=1, source_target_pairs={{0,8},{1,2},{2,1},{3,11},{4,12},{5,6},{6,5},{7,15},{8,0},{9,10},{1... | collective-permute-start | bytes 786440 | tf_op jit(solution)/shard_map/ppermute | solution.py:338
  29.2 14.7 %collective-permute-start.17 = (bf16[32,4096]{1,0:T(8,128)(2,1)S(1)}, bf16[32,4096]{1,0:T(8,128)(2,1)S(1)}, u32[]{:S(2)}, u32[]{:S(2)}) collective-permute-start(bf16[32,4096]{1,0:T(8,128)(2,1)S(1)} %get-tuple-element.56), channel_id=1, source_target_pairs={{0,1},{3,2},{4,5},{7,6},{8,9},{11,10},{12,13},{15,14},{16,17},{19,... | collective-permute-start | bytes 786440 | tf_op jit(solution)/shard_map/ppermute | solution.py:334
  36.5 3.0 %collective-permute-start.15 = (bf16[32,4096]{1,0:T(8,128)(2,1)S(1)}, bf16[32,4096]{1,0:T(8,128)(2,1)S(1)}, u32[]{:S(2)}, u32[]{:S(2)}) collective-permute-start(bf16[32,4096]{1,0:T(8,128)(2,1)S(1)} %add.33), channel_id=1, source_target_pairs={{0,8},{1,2},{2,1},{3,11},{4,12},{5,6},{6,5},{7,15},{8,0},{9,10},{1... | collective-permute-start | bytes 786440 | tf_op jit(solution)/shard_map/ppermute | solution.py:338
  36.7 9.9 %collective-permute-start.12 = (bf16[32,4096]{1,0:T(8,128)(2,1)S(1)}, bf16[32,4096]{1,0:T(8,128)(2,1)S(1)}, u32[]{:S(2)}, u32[]{:S(2)}) collective-permute-start(bf16[32,4096]{1,0:T(8,128)(2,1)S(1)} %slice_add_fusion.1), channel_id=1, source_target_pairs={{0,1},{1,0},{2,3},{3,2},{4,5},{5,4},{6,7},{7,6},{8,9},{9,8},{10,11... | collective-permute-start | bytes 786440 | tf_op jit(solution)/shard_map/ppermute | solution.py:330
  39.5 11.6 %collective-permute-start.16 = (bf16[32,4096]{1,0:T(8,128)(2,1)S(1)}, bf16[32,4096]{1,0:T(8,128)(2,1)S(1)}, u32[]{:S(2)}, u32[]{:S(2)}) collective-permute-start(bf16[32,4096]{1,0:T(8,128)(2,1)S(1)} %select_add_fusion.1), channel_id=1, source_target_pairs={{0,1},{1,0},{2,3},{3,2},{4,5},{5,4},{6,7},{7,6},{8,9},{9,8},{10,11... | collective-permute-start | bytes 786440 | tf_op jit(solution)/shard_map/ppermute | solution.py:330
  43.9 7.2 %collective-permute-start.18 = (bf16[32,4096]{1,0:T(8,128)(2,1)S(1)}, bf16[32,4096]{1,0:T(8,128)(2,1)S(1)}, u32[]{:S(2)}, u32[]{:S(2)}) collective-permute-start(bf16[32,4096]{1,0:T(8,128)(2,1)S(1)} %add.38), channel_id=1, source_target_pairs={{0,8},{1,2},{2,1},{3,11},{4,12},{5,6},{6,5},{7,15},{8,0},{9,10},{1... | collective-permute-start | bytes 786440 | tf_op jit(solution)/shard_map/ppermute | solution.py:338

commit v7 on v6

--- a/solution.py
+++ b/solution.py
@@ -12,7 +12,7 @@
 LOG2E = 1.4426950408889634
 MIB = 1 << 20
 
-WEIGHT_CUTS = 2
+WEIGHT_CUTS = 1
 OUTER = ((0, 1), (1, 0), (2, 3), (3, 2))
 INNER = tuple(
     (p * 8 + c * 4 + t, p * 8 + c * 4 + 3 - t if t in (1, 2) else (p ^ 1) * 8 + c * 4 + t)
@@ -297,7 +297,7 @@
         copy.start()
     for copy in copies[:4]:
         copy.wait()
-    wide[...] = query_in[...].astype(F32)
+    wide[: query_in.shape[0]] = query_in[...].astype(F32)
     for part, ref in enumerate((far_ref, near_ref)):
         for h in range(heads):
             start = part * half * heads + h
@@ -318,7 +318,7 @@
         out_specs=[vmem] * 3,
         scratch_shapes=[
             pltpu.VMEM((rows * heads, width), BF16),
-            pltpu.VMEM((rows * heads, width), F32),
+            pltpu.VMEM((rows * heads + heads, width), F32),
             pltpu.SemaphoreType.DMA((4 + WEIGHT_CUTS,)),
         ],
         compiler_params=pltpu.CompilerParams(vmem_limit_bytes=24 * MIB),

time: 52.3 us -> 52.3 us (level)
  no operation moved by 1% of the time
where the time goes in v7:
time: 52.3 us; the launch traced here: 52 us
  starting transfers between devices  24 us (46%)
  Pallas kernels  16.6 us (32%)
  waiting for transfers between devices  9.85 us (19%)
  other arithmetic  1.38 us (3%)
    ppermute x5, starting transfers between devices, swap(): return lax.ppermute(value, 'tp', OUTER)  11.7 us
    ppermute x5, waiting for transfers between devices, swap(): return lax.ppermute(value, 'tp', OUTER)  7.13 us
    ppermute x7, starting transfers between devices, pair(): return lax.ppermute(value, ('pipe', 'ctx'), [(i, i ^ m) for i in range(8)])  5.24 us
    ppermute x1, starting transfers between devices, send(): return lax.ppermute(value, 'tp', ((0, 1), (3, 2)))  4.92 us
    pallas_call x2, Pallas kernels, project_call(): pl.pallas_call(functools.partial(project_kernel, len(parts)), out_shape=o...  4.7 us
    pallas_call x2, Pallas kernels, attention_call(): pl.pallas_call(functools.partial(kernel, window, heads), out_shape=outs,...  4.38 us
    pallas_call x1, Pallas kernels, load(): pl.pallas_call(functools.partial(load_kernel, heads), out_shape=[pltpu.VM...  3.71 us
    pallas_call x1, Pallas kernels, rest_call(): pl.pallas_call(functools.partial(rest_kernel, columns - width), out_shape...  2.95 us
  transfers between devices with their start and end apart: 19, of which 7 were waited for; matrix products, arithmetic and copies ran while one was open for 1% of the time, Pallas kernels for 25%

profile of v7, /device:TPU:0, one launch (start us, length us, event | category | flops | bytes accessed | tf_op | source)
XLA Modules:
  0.0 52.0 jit_solution(17501668908127856035)
XLA Ops:
  0.0 0.8 %shard_map.56.refs_0_ = bf16[272,128]{1,0:T(8,128)(2,1)S(1)} custom-call(bf16[128,128]{1,0:T(8,128)(2,1)} %bitcast.13, bf16[128,128]{1,0:T(8,128)(2,1)} %bitcast.14, s32[1,128]{1,0:T(1,128)} %bitcast.15), custom_call_target="tpu_custom_call" | custom-call | tf_op jit(solution)/shard_map/pallas_call | solution.py:46
  0.8 4.0 %collective-permute-start.2 = (bf16[272,128]{1,0:T(8,128)(2,1)S(1)}, bf16[272,128]{1,0:T(8,128)(2,1)S(1)}, u32[]{:S(2)}, u32[]{:S(2)}) collective-permute-start(bf16[272,128]{1,0:T(8,128)(2,1)S(1)} %shard_map.56.refs_0_), channel_id=1, source_target_pairs={{0,20},{4,16},{8,28},{12,24},{16,4},{20,0},{24,12},{28,8},{1,21},{... | collective-permute-start | bytes 208904 | tf_op jit(solution)/shard_map/ppermute | solution.py:348
  4.8 0.5 %collective-permute-start.1 = (bf16[272,128]{1,0:T(8,128)(2,1)S(1)}, bf16[272,128]{1,0:T(8,128)(2,1)S(1)}, u32[]{:S(2)}, u32[]{:S(2)}) collective-permute-start(bf16[272,128]{1,0:T(8,128)(2,1)S(1)} %shard_map.56.refs_0_), channel_id=1, source_target_pairs={{0,16},{4,20},{8,24},{12,28},{16,0},{20,4},{24,8},{28,12},{1,17},{... | collective-permute-start | bytes 208904 | tf_op jit(solution)/shard_map/ppermute | solution.py:348
  5.4 3.7 %shard_map.55 = (bf16[2048,2048]{1,0:T(8,128)(2,1)S(1)}, bf16[1024,128]{1,0:T(8,128)(2,1)S(1)}, bf16[1024,128]{1,0:T(8,128)(2,1)S(1)}) custom-call(bf16[2048,4096]{1,0:T(8,128)(2,1)} %weight_ref.4, bf16[2048,128]{1,0:T(8,128)(2,1)} %bitcast.12), custom_call_target="tpu_custom_call" | custom-call | bytes 33554432 | tf_op jit(solution)/shard_map/pallas_call | solution.py:314
  9.2 0.5 collective-permute-done.refs_1_
  9.8 0.4 collective-permute-start.5
  10.3 0.6 %collective-permute-done.4.refs_3_ = bf16[272,128]{1,0:T(8,128)(2,1)S(1)} collective-permute-done((bf16[272,128]{1,0:T(8,128)(2,1)S(1)}, bf16[272,128]{1,0:T(8,128)(2,1)S(1)}, u32[]{:S(2)}, u32[]{:S(2)}) %collective-permute-start.4) | collective-permute-done | bytes 69664 | tf_op jit(solution)/shard_map/ppermute | solution.py:348
  11.4 2.8 %shard_map.57 = (bf16[64,2048]{1,0:T(8,128)(2,1)S(1)}, bf16[64,2048]{1,0:T(8,128)(2,1)S(1)}, bf16[2048,1024]{1,0:T(8,128)(2,1)S(1)}) custom-call(bf16[1024,128]{1,0:T(8,128)(2,1)S(1)} %get-tuple-element.33.query_ref, bf16[2048,2048]{1,0:T(8,128)(2,1)S(1)} %get-tuple-element.37.loaded_ref.refs_2_.refs_1_, bf16[2048,4096]{1,0:T(8,128)(2,1)} %weight_ref.4, ...), custom_call_target="tpu_custom_call" | custom-call | flops 872415232 | bytes 1048576 | tf_op jit(solution)/shard_map/pallas_call | solution.py:229
  14.2 1.8 %collective-permute-start.8 = (bf16[64,2048]{1,0:T(8,128)(2,1)S(1)}, bf16[64,2048]{1,0:T(8,128)(2,1)S(1)}, u32[]{:S(2)}, u32[]{:S(2)}) collective-permute-start(bf16[64,2048]{1,0:T(8,128)(2,1)S(1)} %get-tuple-element.45), channel_id=1, source_target_pairs={{0,1},{1,0},{2,3},{3,2},{4,5},{5,4},{6,7},{7,6},{8,9},{9,8},{10,11... | collective-permute-start | bytes 786440 | tf_op jit(solution)/shard_map/ppermute | solution.py:330
  16.0 1.5 %collective-permute-start.13 = (bf16[64,2048]{1,0:T(8,128)(2,1)S(1)}, bf16[64,2048]{1,0:T(8,128)(2,1)S(1)}, u32[]{:S(2)}, u32[]{:S(2)}) collective-permute-start(bf16[64,2048]{1,0:T(8,128)(2,1)S(1)} %get-tuple-element.41.rows_ref), channel_id=1, source_target_pairs={{0,4},{4,0},{1,5},{5,1},{2,6},{6,2},{3,7},{7,3},{8,12},{12,8},{9,1... | collective-permute-start | bytes 786440 | tf_op jit(solution)/shard_map/ppermute | solution.py:362
  17.5 3.0 %shard_map.58 = (bf16[64,2048]{1,0:T(8,128)(2,1)S(1)}, bf16[2048,1024]{1,0:T(8,128)(2,1)S(1)}) custom-call(bf16[64,2048]{1,0:T(8,128)(2,1)S(1)} %get-tuple-element.41.rows_ref, bf16[2048,1024]{1,0:T(8,128)(2,1)S(1)} %get-tuple-element.42.loaded_ref.refs_3_.refs_2_, bf16[2048,4096]{1,0:T(8,128)(2,1)} %weight_ref.4), custom_call_target="tpu_custom_call" | custom-call | flops 536870912 | bytes 8388608 | tf_op jit(solution)/shard_map/pallas_call | solution.py:182
  20.5 0.5 collective-permute-start.10
  21.0 1.6 %shard_map.59.refs_0_ = bf16[64,2048]{1,0:T(8,128)(2,1)S(1)} custom-call(bf16[1024,128]{1,0:T(8,128)(2,1)S(1)} %get-tuple-element.44.query_ref, bf16[272,128]{1,0:T(8,128)(2,1)S(1)} %shard_map.56.refs_0_, bf16[272,128]{1,0:T(8,128)(2,1)S(1)} %collective-permute-done.refs_1_, bf16[272,128]{1,0:T(8,128)(2,1)S(1)} %collective-permute-done.3.refs_2_, ...), custom_call_target="tpu_custom_call" | custom-call | flops 335544320 | bytes 1048576 | tf_op jit(solution)/shard_map/pallas_call | solution.py:229
  22.6 0.4 collective-permute-start.7
  23.2 1.1 %collective-permute-done.13.refs_0_ = bf16[64,2048]{1,0:T(8,128)(2,1)S(1)} collective-permute-done((bf16[64,2048]{1,0:T(8,128)(2,1)S(1)}, bf16[64,2048]{1,0:T(8,128)(2,1)S(1)}, u32[]{:S(2)}, u32[]{:S(2)}) %collective-permute-start.13) | collective-permute-done | bytes 262176 | tf_op jit(solution)/shard_map/ppermute | solution.py:362
  24.3 2.4 %shard_map.61 = (bf16[32,4096]{1,0:T(8,128)(2,1)S(1)}, bf16[32,4096]{1,0:T(8,128)(2,1)S(1)}) custom-call(bf16[64,2048]{1,0:T(8,128)(2,1)S(1)} %collective-permute-done.13.refs_0_, bf16[2048,2048]{1,0:T(8,128)(2,1)S(1)} %get-tuple-element.37.loaded_ref.refs_2_.refs_1_, bf16[2048,1024]{1,0:T(8,128)(2,1)S(1)} %get-tuple-element.42.loaded_ref.refs_3_.refs_2_, ...), custom_call_target="tpu_custom_call" | custom-call | flops 1073741824 | bytes 16777216 | tf_op jit(solution)/shard_map/pallas_call | solution.py:257
  26.6 2.3 %collective-permute-start.14 = (bf16[32,4096]{1,0:T(8,128)(2,1)S(1)}, bf16[32,4096]{1,0:T(8,128)(2,1)S(1)}, u32[]{:S(2)}, u32[]{:S(2)}) collective-permute-start(bf16[32,4096]{1,0:T(8,128)(2,1)S(1)} %get-tuple-element.52), channel_id=1, source_target_pairs={{0,1},{1,0},{2,3},{3,2},{4,5},{5,4},{6,7},{7,6},{8,9},{9,8},{10,11... | collective-permute-start | bytes 786440 | tf_op jit(solution)/shard_map/ppermute | solution.py:330
  29.0 4.9 %collective-permute-start.17 = (bf16[32,4096]{1,0:T(8,128)(2,1)S(1)}, bf16[32,4096]{1,0:T(8,128)(2,1)S(1)}, u32[]{:S(2)}, u32[]{:S(2)}) collective-permute-start(bf16[32,4096]{1,0:T(8,128)(2,1)S(1)} %get-tuple-element.56), channel_id=1, source_target_pairs={{0,1},{3,2},{4,5},{7,6},{8,9},{11,10},{12,13},{15,14},{16,17},{19,... | collective-permute-start | bytes 786440 | tf_op jit(solution)/shard_map/ppermute | solution.py:334
  34.0 2.3 %shard_map.60 = (bf16[32,4096]{1,0:T(8,128)(2,1)S(1)}, bf16[32,4096]{1,0:T(8,128)(2,1)S(1)}, bf16[32,4096]{1,0:T(8,128)(2,1)S(1)}, bf16[32,4096]{1,0:T(8,128)(2,1)S(1)}) custom-call(bf16[64,2048]{1,0:T(8,128)(2,1)S(1)} %shard_map.59.refs_0_, bf16[64,2048]{1,0:T(8,128)(2,1)S(1)} %collective-permute-done.7.refs_1_, ...), custom_call_target="tpu_custom_call" | custom-call | flops 2147483648 | bytes 16777216 | tf_op jit(solution)/shard_map/pallas_call | solution.py:257
  36.7 2.7 %collective-permute-start.12 = (bf16[32,4096]{1,0:T(8,128)(2,1)S(1)}, bf16[32,4096]{1,0:T(8,128)(2,1)S(1)}, u32[]{:S(2)}, u32[]{:S(2)}) collective-permute-start(bf16[32,4096]{1,0:T(8,128)(2,1)S(1)} %slice_add_fusion.1), channel_id=1, source_target_pairs={{0,1},{1,0},{2,3},{3,2},{4,5},{5,4},{6,7},{7,6},{8,9},{9,8},{10,11... | collective-permute-start | bytes 786440 | tf_op jit(solution)/shard_map/ppermute | solution.py:330
  39.4 4.3 %collective-permute-start.16 = (bf16[32,4096]{1,0:T(8,128)(2,1)S(1)}, bf16[32,4096]{1,0:T(8,128)(2,1)S(1)}, u32[]{:S(2)}, u32[]{:S(2)}) collective-permute-start(bf16[32,4096]{1,0:T(8,128)(2,1)S(1)} %select_add_fusion.1), channel_id=1, source_target_pairs={{0,1},{1,0},{2,3},{3,2},{4,5},{5,4},{6,7},{7,6},{8,9},{9,8},{10,11... | collective-permute-start | bytes 786440 | tf_op jit(solution)/shard_map/ppermute | solution.py:330
  43.9 2.6 %collective-permute-done.12 = bf16[32,4096]{1,0:T(8,128)(2,1)S(1)} collective-permute-done((bf16[32,4096]{1,0:T(8,128)(2,1)S(1)}, bf16[32,4096]{1,0:T(8,128)(2,1)S(1)}, u32[]{:S(2)}, u32[]{:S(2)}) %collective-permute-start.12) | collective-permute-done | bytes 262176 | tf_op jit(solution)/shard_map/ppermute | solution.py:330
  46.6 4.5 %collective-permute-done.16 = bf16[32,4096]{1,0:T(8,128)(2,1)S(1)} collective-permute-done((bf16[32,4096]{1,0:T(8,128)(2,1)S(1)}, bf16[32,4096]{1,0:T(8,128)(2,1)S(1)}, u32[]{:S(2)}, u32[]{:S(2)}) %collective-permute-start.16) | collective-permute-done | bytes 262176 | tf_op jit(solution)/shard_map/ppermute | solution.py:330
  51.2 0.8 %maximum_bitcast_fusion = bf16[1,2,1,32,4096]{4,3,2,1,0:T(8,128)(2,1)} fusion(bf16[1,32,4096]{2,1,0:T(8,128)(2,1)S(1)} %select_bitcast_fusion, bf16[1,32,4096]{2,1,0:T(8,128)(2,1)S(1)} %get-tuple-element.57), kind=kLoop, calls=%fused_computation.1 | loop fusion | flops 262144 | bytes 1048576 | tf_op jit(solution)/shard_map/reshape | solution.py:395
  (31 shorter events, 1.7 us)
Async XLA Ops:
  0.8 8.3 %collective-permute-start.2 = (bf16[272,128]{1,0:T(8,128)(2,1)S(1)}, bf16[272,128]{1,0:T(8,128)(2,1)S(1)}, u32[]{:S(2)}, u32[]{:S(2)}) collective-permute-start(bf16[272,128]{1,0:T(8,128)(2,1)S(1)} %shard_map.56.refs_0_), channel_id=1, source_target_pairs={{0,20},{4,16},{8,28},{12,24},{16,4},{20,0},{24,12},{28,8},{1,21},{... | collective-permute-start | bytes 208904 | tf_op jit(solution)/shard_map/ppermute | solution.py:348
  4.8 4.4 %collective-permute-start.1 = (bf16[272,128]{1,0:T(8,128)(2,1)S(1)}, bf16[272,128]{1,0:T(8,128)(2,1)S(1)}, u32[]{:S(2)}, u32[]{:S(2)}) collective-permute-start(bf16[272,128]{1,0:T(8,128)(2,1)S(1)} %shard_map.56.refs_0_), channel_id=1, source_target_pairs={{0,16},{4,20},{8,24},{12,28},{16,0},{20,4},{24,8},{28,12},{1,17},{... | collective-permute-start | bytes 208904 | tf_op jit(solution)/shard_map/ppermute | solution.py:348
  5.3 4.3 %collective-permute-start = (bf16[272,128]{1,0:T(8,128)(2,1)S(1)}, bf16[272,128]{1,0:T(8,128)(2,1)S(1)}, u32[]{:S(2)}, u32[]{:S(2)}) collective-permute-start(bf16[272,128]{1,0:T(8,128)(2,1)S(1)} %shard_map.56.refs_0_), channel_id=1, source_target_pairs={{0,4},{4,0},{8,12},{12,8},{16,20},{20,16},{24,28},{28,24},{1,5},{5... | collective-permute-start | bytes 208904 | tf_op jit(solution)/shard_map/ppermute | solution.py:348
  5.4 4.8 %collective-permute-start.3 = (bf16[272,128]{1,0:T(8,128)(2,1)S(1)}, bf16[272,128]{1,0:T(8,128)(2,1)S(1)}, u32[]{:S(2)}, u32[]{:S(2)}) collective-permute-start(bf16[272,128]{1,0:T(8,128)(2,1)S(1)} %shard_map.56.refs_0_), channel_id=1, source_target_pairs={{0,8},{4,12},{8,0},{12,4},{16,24},{20,28},{24,16},{28,20},{1,9},{5... | collective-permute-start | bytes 208904 | tf_op jit(solution)/shard_map/ppermute | solution.py:348
  9.6 1.3 %collective-permute-start.4 = (bf16[272,128]{1,0:T(8,128)(2,1)S(1)}, bf16[272,128]{1,0:T(8,128)(2,1)S(1)}, u32[]{:S(2)}, u32[]{:S(2)}) collective-permute-start(bf16[272,128]{1,0:T(8,128)(2,1)S(1)} %collective-permute-done.refs_1_), channel_id=1, source_target_pairs={{0,8},{4,12},{8,0},{12,4},{16,24},{20,28},{24,16},{28,20},{1,9},{5... | collective-permute-start | bytes 208904 | tf_op jit(solution)/shard_map/ppermute | solution.py:348
  9.8 1.3 %collective-permute-start.5 = (bf16[272,128]{1,0:T(8,128)(2,1)S(1)}, bf16[272,128]{1,0:T(8,128)(2,1)S(1)}, u32[]{:S(2)}, u32[]{:S(2)}) collective-permute-start(bf16[272,128]{1,0:T(8,128)(2,1)S(1)} %collective-permute-done.1.refs_4_), channel_id=1, source_target_pairs={{0,8},{4,12},{8,0},{12,4},{16,24},{20,28},{24,16},{28,20},{1,9},{5... | collective-permute-start | bytes 208904 | tf_op jit(solution)/shard_map/ppermute | solution.py:348
  10.1 1.3 %collective-permute-start.6 = (bf16[272,128]{1,0:T(8,128)(2,1)S(1)}, bf16[272,128]{1,0:T(8,128)(2,1)S(1)}, u32[]{:S(2)}, u32[]{:S(2)}) collective-permute-start(bf16[272,128]{1,0:T(8,128)(2,1)S(1)} %collective-permute-done.2.refs_5_), channel_id=1, source_target_pairs={{0,8},{4,12},{8,0},{12,4},{16,24},{20,28},{24,16},{28,20},{1,9},{5... | collective-permute-start | bytes 208904 | tf_op jit(solution)/shard_map/ppermute | solution.py:348
  14.2 8.8 %collective-permute-start.8 = (bf16[64,2048]{1,0:T(8,128)(2,1)S(1)}, bf16[64,2048]{1,0:T(8,128)(2,1)S(1)}, u32[]{:S(2)}, u32[]{:S(2)}) collective-permute-start(bf16[64,2048]{1,0:T(8,128)(2,1)S(1)} %get-tuple-element.45), channel_id=1, source_target_pairs={{0,1},{1,0},{2,3},{3,2},{4,5},{5,4},{6,7},{7,6},{8,9},{9,8},{10,11... | collective-permute-start | bytes 786440 | tf_op jit(solution)/shard_map/ppermute | solution.py:330
  16.0 8.3 %collective-permute-start.13 = (bf16[64,2048]{1,0:T(8,128)(2,1)S(1)}, bf16[64,2048]{1,0:T(8,128)(2,1)S(1)}, u32[]{:S(2)}, u32[]{:S(2)}) collective-permute-start(bf16[64,2048]{1,0:T(8,128)(2,1)S(1)} %get-tuple-element.41.rows_ref), channel_id=1, source_target_pairs={{0,4},{4,0},{1,5},{5,1},{2,6},{6,2},{3,7},{7,3},{8,12},{12,8},{9,1... | collective-permute-start | bytes 786440 | tf_op jit(solution)/shard_map/ppermute | solution.py:362
  20.5 8.4 %collective-permute-start.10 = (bf16[64,2048]{1,0:T(8,128)(2,1)S(1)}, bf16[64,2048]{1,0:T(8,128)(2,1)S(1)}, u32[]{:S(2)}, u32[]{:S(2)}) collective-permute-start(bf16[64,2048]{1,0:T(8,128)(2,1)S(1)} %get-tuple-element.43), channel_id=1, source_target_pairs={{0,1},{1,0},{2,3},{3,2},{4,5},{5,4},{6,7},{7,6},{8,9},{9,8},{10,11... | collective-permute-start | bytes 786440 | tf_op jit(solution)/shard_map/ppermute | solution.py:330
  22.6 11.4 %collective-permute-start.7 = (bf16[64,2048]{1,0:T(8,128)(2,1)S(1)}, bf16[64,2048]{1,0:T(8,128)(2,1)S(1)}, u32[]{:S(2)}, u32[]{:S(2)}) collective-permute-start(bf16[64,2048]{1,0:T(8,128)(2,1)S(1)} %shard_map.59.refs_0_), channel_id=1, source_target_pairs={{0,4},{4,0},{1,5},{5,1},{2,6},{6,2},{3,7},{7,3},{8,12},{12,8},{9,1... | collective-permute-start | bytes 786440 | tf_op jit(solution)/shard_map/ppermute | solution.py:362
  23.1 10.9 %collective-permute-start.9 = (bf16[64,2048]{1,0:T(8,128)(2,1)S(1)}, bf16[64,2048]{1,0:T(8,128)(2,1)S(1)}, u32[]{:S(2)}, u32[]{:S(2)}) collective-permute-start(bf16[64,2048]{1,0:T(8,128)(2,1)S(1)} %add.30), channel_id=1, source_target_pairs={{0,8},{1,2},{2,1},{3,11},{4,12},{5,6},{6,5},{7,15},{8,0},{9,10},{1... | collective-permute-start | bytes 786440 | tf_op jit(solution)/shard_map/ppermute | solution.py:338
  26.6 9.7 %collective-permute-start.14 = (bf16[32,4096]{1,0:T(8,128)(2,1)S(1)}, bf16[32,4096]{1,0:T(8,128)(2,1)S(1)}, u32[]{:S(2)}, u32[]{:S(2)}) collective-permute-start(bf16[32,4096]{1,0:T(8,128)(2,1)S(1)} %get-tuple-element.52), channel_id=1, source_target_pairs={{0,1},{1,0},{2,3},{3,2},{4,5},{5,4},{6,7},{7,6},{8,9},{9,8},{10,11... | collective-permute-start | bytes 786440 | tf_op jit(solution)/shard_map/ppermute | solution.py:330
  29.0 7.6 %collective-permute-start.11 = (bf16[64,2048]{1,0:T(8,128)(2,1)S(1)}, bf16[64,2048]{1,0:T(8,128)(2,1)S(1)}, u32[]{:S(2)}, u32[]{:S(2)}) collective-permute-start(bf16[64,2048]{1,0:T(8,128)(2,1)S(1)} %add.31), channel_id=1, source_target_pairs={{0,8},{1,2},{2,1},{3,11},{4,12},{5,6},{6,5},{7,15},{8,0},{9,10},{1... | collective-permute-start | bytes 786440 | tf_op jit(solution)/shard_map/ppermute | solution.py:338
  29.0 14.7 %collective-permute-start.17 = (bf16[32,4096]{1,0:T(8,128)(2,1)S(1)}, bf16[32,4096]{1,0:T(8,128)(2,1)S(1)}, u32[]{:S(2)}, u32[]{:S(2)}) collective-permute-start(bf16[32,4096]{1,0:T(8,128)(2,1)S(1)} %get-tuple-element.56), channel_id=1, source_target_pairs={{0,1},{3,2},{4,5},{7,6},{8,9},{11,10},{12,13},{15,14},{16,17},{19,... | collective-permute-start | bytes 786440 | tf_op jit(solution)/shard_map/ppermute | solution.py:334
  36.4 3.0 %collective-permute-start.15 = (bf16[32,4096]{1,0:T(8,128)(2,1)S(1)}, bf16[32,4096]{1,0:T(8,128)(2,1)S(1)}, u32[]{:S(2)}, u32[]{:S(2)}) collective-permute-start(bf16[32,4096]{1,0:T(8,128)(2,1)S(1)} %add.33), channel_id=1, source_target_pairs={{0,8},{1,2},{2,1},{3,11},{4,12},{5,6},{6,5},{7,15},{8,0},{9,10},{1... | collective-permute-start | bytes 786440 | tf_op jit(solution)/shard_map/ppermute | solution.py:338
  36.7 9.9 %collective-permute-start.12 = (bf16[32,4096]{1,0:T(8,128)(2,1)S(1)}, bf16[32,4096]{1,0:T(8,128)(2,1)S(1)}, u32[]{:S(2)}, u32[]{:S(2)}) collective-permute-start(bf16[32,4096]{1,0:T(8,128)(2,1)S(1)} %slice_add_fusion.1), channel_id=1, source_target_pairs={{0,1},{1,0},{2,3},{3,2},{4,5},{5,4},{6,7},{7,6},{8,9},{9,8},{10,11... | collective-permute-start | bytes 786440 | tf_op jit(solution)/shard_map/ppermute | solution.py:330
  39.4 11.6 %collective-permute-start.16 = (bf16[32,4096]{1,0:T(8,128)(2,1)S(1)}, bf16[32,4096]{1,0:T(8,128)(2,1)S(1)}, u32[]{:S(2)}, u32[]{:S(2)}) collective-permute-start(bf16[32,4096]{1,0:T(8,128)(2,1)S(1)} %select_add_fusion.1), channel_id=1, source_target_pairs={{0,1},{1,0},{2,3},{3,2},{4,5},{5,4},{6,7},{7,6},{8,9},{9,8},{10,11... | collective-permute-start | bytes 786440 | tf_op jit(solution)/shard_map/ppermute | solution.py:330
  43.8 7.2 %collective-permute-start.18 = (bf16[32,4096]{1,0:T(8,128)(2,1)S(1)}, bf16[32,4096]{1,0:T(8,128)(2,1)S(1)}, u32[]{:S(2)}, u32[]{:S(2)}) collective-permute-start(bf16[32,4096]{1,0:T(8,128)(2,1)S(1)} %add.38), channel_id=1, source_target_pairs={{0,8},{1,2},{2,1},{3,11},{4,12},{5,6},{6,5},{7,15},{8,0},{9,10},{1... | collective-permute-start | bytes 786440 | tf_op jit(solution)/shard_map/ppermute | solution.py:338

commit v8 on v7

--- a/solution.py
+++ b/solution.py
@@ -375,7 +375,6 @@
     first_in = swap(late_first)
     second_in = send(late_second)
     passed_rest = swap_inner(early_rest + rest_in)
-    late_near = swap_inner(late_second + second_in)
     near_query, _ = after((near_query, early_rest))
     quarter = rows // 4
     both = passed(jnp.concatenate([passed_on, passed_rest], axis=1))
@@ -384,6 +383,8 @@
     other_near, _ = after((other_near, passed_on))
     third, kept, late_third, late_kept = project_call([near_rows, other_near], weights)
     first_in, _ = after((first_in, third))
+    second_in, _ = after((second_in, third))
+    late_near = swap_inner(late_second + second_in)
     late_far = swap_inner(late_first + first_in)
     last_in = swap(late_third + passed(late_far))
     other = late_kept + last_in + passed(late_near)

time: 52.3 us -> 52.3 us (level)
  waiting for transfers between devices: 9.85 us -> 11 us
  starting transfers between devices: 24 us -> 22.9 us
    ppermute x5, starting transfers between devices: 11.7 us -> 10.5 us  [swap(): return lax.ppermute(value, 'tp', OUTER)]
    ppermute x1, waiting for transfers between devices: 0.01 us -> 1.14 us  [send(): return lax.ppermute(value, 'tp', ((0, 1), (3, 2)))]
  transfers between devices with their start and end apart: 19 -> 19, of which waited for: 7 -> 8; matrix products, arithmetic and copies ran while one was open for 1% -> 1% of each run, Pallas kernels for 25% -> 25%
where the time goes in v8:
time: 52.3 us; the launch traced here: 52 us
  starting transfers between devices  22.9 us (44%)
  Pallas kernels  16.6 us (32%)
  waiting for transfers between devices  11 us (21%)
  other arithmetic  1.38 us (3%)
    ppermute x5, starting transfers between devices, swap(): return lax.ppermute(value, 'tp', OUTER)  10.5 us
    ppermute x5, waiting for transfers between devices, swap(): return lax.ppermute(value, 'tp', OUTER)  7.13 us
    ppermute x7, starting transfers between devices, pair(): return lax.ppermute(value, ('pipe', 'ctx'), [(i, i ^ m) for i in range(8)])  5.24 us
    ppermute x1, starting transfers between devices, send(): return lax.ppermute(value, 'tp', ((0, 1), (3, 2)))  4.92 us
    pallas_call x2, Pallas kernels, project_call(): pl.pallas_call(functools.partial(project_kernel, len(parts)), out_shape=o...  4.7 us
    pallas_call x2, Pallas kernels, attention_call(): pl.pallas_call(functools.partial(kernel, window, heads), out_shape=outs,...  4.38 us
    pallas_call x1, Pallas kernels, load(): pl.pallas_call(functools.partial(load_kernel, heads), out_shape=[pltpu.VM...  3.71 us
    pallas_call x1, Pallas kernels, rest_call(): pl.pallas_call(functools.partial(rest_kernel, columns - width), out_shape...  2.95 us
  transfers between devices with their start and end apart: 19, of which 8 were waited for; matrix products, arithmetic and copies ran while one was open for 1% of the time, Pallas kernels for 25%

profile of v8, /device:TPU:0, one launch (start us, length us, event | category | flops | bytes accessed | tf_op | source)
XLA Modules:
  0.0 52.0 jit_solution(10121166001976340288)
XLA Ops:
  0.0 0.8 %shard_map.56.refs_0_ = bf16[272,128]{1,0:T(8,128)(2,1)S(1)} custom-call(bf16[128,128]{1,0:T(8,128)(2,1)} %bitcast.13, bf16[128,128]{1,0:T(8,128)(2,1)} %bitcast.14, s32[1,128]{1,0:T(1,128)} %bitcast.15), custom_call_target="tpu_custom_call" | custom-call | tf_op jit(solution)/shard_map/pallas_call | solution.py:46
  0.8 4.0 %collective-permute-start.2 = (bf16[272,128]{1,0:T(8,128)(2,1)S(1)}, bf16[272,128]{1,0:T(8,128)(2,1)S(1)}, u32[]{:S(2)}, u32[]{:S(2)}) collective-permute-start(bf16[272,128]{1,0:T(8,128)(2,1)S(1)} %shard_map.56.refs_0_), channel_id=1, source_target_pairs={{0,20},{4,16},{8,28},{12,24},{16,4},{20,0},{24,12},{28,8},{1,21},{... | collective-permute-start | bytes 208904 | tf_op jit(solution)/shard_map/ppermute | solution.py:348
  4.8 0.5 %collective-permute-start.1 = (bf16[272,128]{1,0:T(8,128)(2,1)S(1)}, bf16[272,128]{1,0:T(8,128)(2,1)S(1)}, u32[]{:S(2)}, u32[]{:S(2)}) collective-permute-start(bf16[272,128]{1,0:T(8,128)(2,1)S(1)} %shard_map.56.refs_0_), channel_id=1, source_target_pairs={{0,16},{4,20},{8,24},{12,28},{16,0},{20,4},{24,8},{28,12},{1,17},{... | collective-permute-start | bytes 208904 | tf_op jit(solution)/shard_map/ppermute | solution.py:348
  5.4 3.7 %shard_map.55 = (bf16[2048,2048]{1,0:T(8,128)(2,1)S(1)}, bf16[1024,128]{1,0:T(8,128)(2,1)S(1)}, bf16[1024,128]{1,0:T(8,128)(2,1)S(1)}) custom-call(bf16[2048,4096]{1,0:T(8,128)(2,1)} %weight_ref.4, bf16[2048,128]{1,0:T(8,128)(2,1)} %bitcast.12), custom_call_target="tpu_custom_call" | custom-call | bytes 33554432 | tf_op jit(solution)/shard_map/pallas_call | solution.py:314
  9.2 0.5 collective-permute-done.refs_1_
  10.3 0.6 %collective-permute-done.4.refs_3_ = bf16[272,128]{1,0:T(8,128)(2,1)S(1)} collective-permute-done((bf16[272,128]{1,0:T(8,128)(2,1)S(1)}, bf16[272,128]{1,0:T(8,128)(2,1)S(1)}, u32[]{:S(2)}, u32[]{:S(2)}) %collective-permute-start.4) | collective-permute-done | bytes 69664 | tf_op jit(solution)/shard_map/ppermute | solution.py:348
  11.4 2.8 %shard_map.57 = (bf16[64,2048]{1,0:T(8,128)(2,1)S(1)}, bf16[64,2048]{1,0:T(8,128)(2,1)S(1)}, bf16[2048,1024]{1,0:T(8,128)(2,1)S(1)}) custom-call(bf16[1024,128]{1,0:T(8,128)(2,1)S(1)} %get-tuple-element.34.query_ref, bf16[2048,2048]{1,0:T(8,128)(2,1)S(1)} %get-tuple-element.38.loaded_ref.refs_2_.refs_1_, bf16[2048,4096]{1,0:T(8,128)(2,1)} %weight_ref.4, ...), custom_call_target="tpu_custom_call" | custom-call | flops 872415232 | bytes 1048576 | tf_op jit(solution)/shard_map/pallas_call | solution.py:229
  14.2 1.8 %collective-permute-start.8 = (bf16[64,2048]{1,0:T(8,128)(2,1)S(1)}, bf16[64,2048]{1,0:T(8,128)(2,1)S(1)}, u32[]{:S(2)}, u32[]{:S(2)}) collective-permute-start(bf16[64,2048]{1,0:T(8,128)(2,1)S(1)} %get-tuple-element.46), channel_id=1, source_target_pairs={{0,1},{1,0},{2,3},{3,2},{4,5},{5,4},{6,7},{7,6},{8,9},{9,8},{10,11... | collective-permute-start | bytes 786440 | tf_op jit(solution)/shard_map/ppermute | solution.py:330
  16.0 1.5 %collective-permute-start.13 = (bf16[64,2048]{1,0:T(8,128)(2,1)S(1)}, bf16[64,2048]{1,0:T(8,128)(2,1)S(1)}, u32[]{:S(2)}, u32[]{:S(2)}) collective-permute-start(bf16[64,2048]{1,0:T(8,128)(2,1)S(1)} %get-tuple-element.42.rows_ref), channel_id=1, source_target_pairs={{0,4},{4,0},{1,5},{5,1},{2,6},{6,2},{3,7},{7,3},{8,12},{12,8},{9,1... | collective-permute-start | bytes 786440 | tf_op jit(solution)/shard_map/ppermute | solution.py:362
  17.5 3.0 %shard_map.58 = (bf16[64,2048]{1,0:T(8,128)(2,1)S(1)}, bf16[2048,1024]{1,0:T(8,128)(2,1)S(1)}) custom-call(bf16[64,2048]{1,0:T(8,128)(2,1)S(1)} %get-tuple-element.42.rows_ref, bf16[2048,1024]{1,0:T(8,128)(2,1)S(1)} %get-tuple-element.43.loaded_ref.refs_3_.refs_2_, bf16[2048,4096]{1,0:T(8,128)(2,1)} %weight_ref.4), custom_call_target="tpu_custom_call" | custom-call | flops 536870912 | bytes 8388608 | tf_op jit(solution)/shard_map/pallas_call | solution.py:182
  20.5 0.5 collective-permute-start.10
  21.0 1.6 %shard_map.59.refs_0_ = bf16[64,2048]{1,0:T(8,128)(2,1)S(1)} custom-call(bf16[1024,128]{1,0:T(8,128)(2,1)S(1)} %get-tuple-element.45.query_ref, bf16[272,128]{1,0:T(8,128)(2,1)S(1)} %shard_map.56.refs_0_, bf16[272,128]{1,0:T(8,128)(2,1)S(1)} %collective-permute-done.refs_1_, bf16[272,128]{1,0:T(8,128)(2,1)S(1)} %collective-permute-done.3.refs_2_, ...), custom_call_target="tpu_custom_call" | custom-call | flops 335544320 | bytes 1048576 | tf_op jit(solution)/shard_map/pallas_call | solution.py:229
  22.6 0.4 collective-permute-start.7
  23.2 1.1 %collective-permute-done.13.refs_0_ = bf16[64,2048]{1,0:T(8,128)(2,1)S(1)} collective-permute-done((bf16[64,2048]{1,0:T(8,128)(2,1)S(1)}, bf16[64,2048]{1,0:T(8,128)(2,1)S(1)}, u32[]{:S(2)}, u32[]{:S(2)}) %collective-permute-start.13) | collective-permute-done | bytes 262176 | tf_op jit(solution)/shard_map/ppermute | solution.py:362
  24.3 2.4 %shard_map.61 = (bf16[32,4096]{1,0:T(8,128)(2,1)S(1)}, bf16[32,4096]{1,0:T(8,128)(2,1)S(1)}) custom-call(bf16[64,2048]{1,0:T(8,128)(2,1)S(1)} %collective-permute-done.13.refs_0_, bf16[2048,2048]{1,0:T(8,128)(2,1)S(1)} %get-tuple-element.38.loaded_ref.refs_2_.refs_1_, bf16[2048,1024]{1,0:T(8,128)(2,1)S(1)} %get-tuple-element.43.loaded_ref.refs_3_.refs_2_, ...), custom_call_target="tpu_custom_call" | custom-call | flops 1073741824 | bytes 16777216 | tf_op jit(solution)/shard_map/pallas_call | solution.py:257
  26.6 2.3 %collective-permute-start.14 = (bf16[32,4096]{1,0:T(8,128)(2,1)S(1)}, bf16[32,4096]{1,0:T(8,128)(2,1)S(1)}, u32[]{:S(2)}, u32[]{:S(2)}) collective-permute-start(bf16[32,4096]{1,0:T(8,128)(2,1)S(1)} %get-tuple-element.53), channel_id=1, source_target_pairs={{0,1},{1,0},{2,3},{3,2},{4,5},{5,4},{6,7},{7,6},{8,9},{9,8},{10,11... | collective-permute-start | bytes 786440 | tf_op jit(solution)/shard_map/ppermute | solution.py:330
  29.0 4.9 %collective-permute-start.17 = (bf16[32,4096]{1,0:T(8,128)(2,1)S(1)}, bf16[32,4096]{1,0:T(8,128)(2,1)S(1)}, u32[]{:S(2)}, u32[]{:S(2)}) collective-permute-start(bf16[32,4096]{1,0:T(8,128)(2,1)S(1)} %get-tuple-element.57), channel_id=1, source_target_pairs={{0,1},{3,2},{4,5},{7,6},{8,9},{11,10},{12,13},{15,14},{16,17},{19,... | collective-permute-start | bytes 786440 | tf_op jit(solution)/shard_map/ppermute | solution.py:334
  34.0 2.3 %shard_map.60 = (bf16[32,4096]{1,0:T(8,128)(2,1)S(1)}, bf16[32,4096]{1,0:T(8,128)(2,1)S(1)}, bf16[32,4096]{1,0:T(8,128)(2,1)S(1)}, bf16[32,4096]{1,0:T(8,128)(2,1)S(1)}) custom-call(bf16[64,2048]{1,0:T(8,128)(2,1)S(1)} %shard_map.59.refs_0_, bf16[64,2048]{1,0:T(8,128)(2,1)S(1)} %collective-permute-done.7.refs_1_, ...), custom_call_target="tpu_custom_call" | custom-call | flops 2147483648 | bytes 16777216 | tf_op jit(solution)/shard_map/pallas_call | solution.py:257
  36.7 2.7 %collective-permute-start.12 = (bf16[32,4096]{1,0:T(8,128)(2,1)S(1)}, bf16[32,4096]{1,0:T(8,128)(2,1)S(1)}, u32[]{:S(2)}, u32[]{:S(2)}) collective-permute-start(bf16[32,4096]{1,0:T(8,128)(2,1)S(1)} %slice_add_fusion.1), channel_id=1, source_target_pairs={{0,1},{1,0},{2,3},{3,2},{4,5},{5,4},{6,7},{7,6},{8,9},{9,8},{10,11... | collective-permute-start | bytes 786440 | tf_op jit(solution)/shard_map/ppermute | solution.py:330
  39.4 1.1 %collective-permute-done.17 = bf16[32,4096]{1,0:T(8,128)(2,1)S(1)} collective-permute-done((bf16[32,4096]{1,0:T(8,128)(2,1)S(1)}, bf16[32,4096]{1,0:T(8,128)(2,1)S(1)}, u32[]{:S(2)}, u32[]{:S(2)}) %collective-permute-start.17) | collective-permute-done | bytes 262176 | tf_op jit(solution)/shard_map/ppermute | solution.py:334
  40.6 3.2 %collective-permute-start.16 = (bf16[32,4096]{1,0:T(8,128)(2,1)S(1)}, bf16[32,4096]{1,0:T(8,128)(2,1)S(1)}, u32[]{:S(2)}, u32[]{:S(2)}) collective-permute-start(bf16[32,4096]{1,0:T(8,128)(2,1)S(1)} %select_add_fusion.1), channel_id=1, source_target_pairs={{0,1},{1,0},{2,3},{3,2},{4,5},{5,4},{6,7},{7,6},{8,9},{9,8},{10,11... | collective-permute-start | bytes 786440 | tf_op jit(solution)/shard_map/ppermute | solution.py:330
  43.9 2.6 %collective-permute-done.12 = bf16[32,4096]{1,0:T(8,128)(2,1)S(1)} collective-permute-done((bf16[32,4096]{1,0:T(8,128)(2,1)S(1)}, bf16[32,4096]{1,0:T(8,128)(2,1)S(1)}, u32[]{:S(2)}, u32[]{:S(2)}) %collective-permute-start.12) | collective-permute-done | bytes 262176 | tf_op jit(solution)/shard_map/ppermute | solution.py:330
  46.6 4.5 %collective-permute-done.16 = bf16[32,4096]{1,0:T(8,128)(2,1)S(1)} collective-permute-done((bf16[32,4096]{1,0:T(8,128)(2,1)S(1)}, bf16[32,4096]{1,0:T(8,128)(2,1)S(1)}, u32[]{:S(2)}, u32[]{:S(2)}) %collective-permute-start.16) | collective-permute-done | bytes 262176 | tf_op jit(solution)/shard_map/ppermute | solution.py:330
  51.2 0.8 %maximum_bitcast_fusion = bf16[1,2,1,32,4096]{4,3,2,1,0:T(8,128)(2,1)} fusion(bf16[1,32,4096]{2,1,0:T(8,128)(2,1)S(1)} %select_bitcast_fusion, bf16[1,32,4096]{2,1,0:T(8,128)(2,1)S(1)} %get-tuple-element.59), kind=kLoop, calls=%fused_computation.1 | loop fusion | flops 262144 | bytes 1048576 | tf_op jit(solution)/shard_map/reshape | solution.py:396
  (31 shorter events, 2.1 us)
Async XLA Ops:
  0.8 8.3 %collective-permute-start.2 = (bf16[272,128]{1,0:T(8,128)(2,1)S(1)}, bf16[272,128]{1,0:T(8,128)(2,1)S(1)}, u32[]{:S(2)}, u32[]{:S(2)}) collective-permute-start(bf16[272,128]{1,0:T(8,128)(2,1)S(1)} %shard_map.56.refs_0_), channel_id=1, source_target_pairs={{0,20},{4,16},{8,28},{12,24},{16,4},{20,0},{24,12},{28,8},{1,21},{... | collective-permute-start | bytes 208904 | tf_op jit(solution)/shard_map/ppermute | solution.py:348
  4.8 4.4 %collective-permute-start.1 = (bf16[272,128]{1,0:T(8,128)(2,1)S(1)}, bf16[272,128]{1,0:T(8,128)(2,1)S(1)}, u32[]{:S(2)}, u32[]{:S(2)}) collective-permute-start(bf16[272,128]{1,0:T(8,128)(2,1)S(1)} %shard_map.56.refs_0_), channel_id=1, source_target_pairs={{0,16},{4,20},{8,24},{12,28},{16,0},{20,4},{24,8},{28,12},{1,17},{... | collective-permute-start | bytes 208904 | tf_op jit(solution)/shard_map/ppermute | solution.py:348
  5.3 4.3 %collective-permute-start = (bf16[272,128]{1,0:T(8,128)(2,1)S(1)}, bf16[272,128]{1,0:T(8,128)(2,1)S(1)}, u32[]{:S(2)}, u32[]{:S(2)}) collective-permute-start(bf16[272,128]{1,0:T(8,128)(2,1)S(1)} %shard_map.56.refs_0_), channel_id=1, source_target_pairs={{0,4},{4,0},{8,12},{12,8},{16,20},{20,16},{24,28},{28,24},{1,5},{5... | collective-permute-start | bytes 208904 | tf_op jit(solution)/shard_map/ppermute | solution.py:348
  5.4 4.8 %collective-permute-start.3 = (bf16[272,128]{1,0:T(8,128)(2,1)S(1)}, bf16[272,128]{1,0:T(8,128)(2,1)S(1)}, u32[]{:S(2)}, u32[]{:S(2)}) collective-permute-start(bf16[272,128]{1,0:T(8,128)(2,1)S(1)} %shard_map.56.refs_0_), channel_id=1, source_target_pairs={{0,8},{4,12},{8,0},{12,4},{16,24},{20,28},{24,16},{28,20},{1,9},{5... | collective-permute-start | bytes 208904 | tf_op jit(solution)/shard_map/ppermute | solution.py:348
  9.6 1.3 %collective-permute-start.4 = (bf16[272,128]{1,0:T(8,128)(2,1)S(1)}, bf16[272,128]{1,0:T(8,128)(2,1)S(1)}, u32[]{:S(2)}, u32[]{:S(2)}) collective-permute-start(bf16[272,128]{1,0:T(8,128)(2,1)S(1)} %collective-permute-done.refs_1_), channel_id=1, source_target_pairs={{0,8},{4,12},{8,0},{12,4},{16,24},{20,28},{24,16},{28,20},{1,9},{5... | collective-permute-start | bytes 208904 | tf_op jit(solution)/shard_map/ppermute | solution.py:348
  9.8 1.3 %collective-permute-start.5 = (bf16[272,128]{1,0:T(8,128)(2,1)S(1)}, bf16[272,128]{1,0:T(8,128)(2,1)S(1)}, u32[]{:S(2)}, u32[]{:S(2)}) collective-permute-start(bf16[272,128]{1,0:T(8,128)(2,1)S(1)} %collective-permute-done.1.refs_4_), channel_id=1, source_target_pairs={{0,8},{4,12},{8,0},{12,4},{16,24},{20,28},{24,16},{28,20},{1,9},{5... | collective-permute-start | bytes 208904 | tf_op jit(solution)/shard_map/ppermute | solution.py:348
  10.1 1.3 %collective-permute-start.6 = (bf16[272,128]{1,0:T(8,128)(2,1)S(1)}, bf16[272,128]{1,0:T(8,128)(2,1)S(1)}, u32[]{:S(2)}, u32[]{:S(2)}) collective-permute-start(bf16[272,128]{1,0:T(8,128)(2,1)S(1)} %collective-permute-done.2.refs_5_), channel_id=1, source_target_pairs={{0,8},{4,12},{8,0},{12,4},{16,24},{20,28},{24,16},{28,20},{1,9},{5... | collective-permute-start | bytes 208904 | tf_op jit(solution)/shard_map/ppermute | solution.py:348
  14.2 8.8 %collective-permute-start.8 = (bf16[64,2048]{1,0:T(8,128)(2,1)S(1)}, bf16[64,2048]{1,0:T(8,128)(2,1)S(1)}, u32[]{:S(2)}, u32[]{:S(2)}) collective-permute-start(bf16[64,2048]{1,0:T(8,128)(2,1)S(1)} %get-tuple-element.46), channel_id=1, source_target_pairs={{0,1},{1,0},{2,3},{3,2},{4,5},{5,4},{6,7},{7,6},{8,9},{9,8},{10,11... | collective-permute-start | bytes 786440 | tf_op jit(solution)/shard_map/ppermute | solution.py:330
  16.0 8.3 %collective-permute-start.13 = (bf16[64,2048]{1,0:T(8,128)(2,1)S(1)}, bf16[64,2048]{1,0:T(8,128)(2,1)S(1)}, u32[]{:S(2)}, u32[]{:S(2)}) collective-permute-start(bf16[64,2048]{1,0:T(8,128)(2,1)S(1)} %get-tuple-element.42.rows_ref), channel_id=1, source_target_pairs={{0,4},{4,0},{1,5},{5,1},{2,6},{6,2},{3,7},{7,3},{8,12},{12,8},{9,1... | collective-permute-start | bytes 786440 | tf_op jit(solution)/shard_map/ppermute | solution.py:362
  20.5 8.4 %collective-permute-start.10 = (bf16[64,2048]{1,0:T(8,128)(2,1)S(1)}, bf16[64,2048]{1,0:T(8,128)(2,1)S(1)}, u32[]{:S(2)}, u32[]{:S(2)}) collective-permute-start(bf16[64,2048]{1,0:T(8,128)(2,1)S(1)} %get-tuple-element.44), channel_id=1, source_target_pairs={{0,1},{1,0},{2,3},{3,2},{4,5},{5,4},{6,7},{7,6},{8,9},{9,8},{10,11... | collective-permute-start | bytes 786440 | tf_op jit(solution)/shard_map/ppermute | solution.py:330
  22.6 11.4 %collective-permute-start.7 = (bf16[64,2048]{1,0:T(8,128)(2,1)S(1)}, bf16[64,2048]{1,0:T(8,128)(2,1)S(1)}, u32[]{:S(2)}, u32[]{:S(2)}) collective-permute-start(bf16[64,2048]{1,0:T(8,128)(2,1)S(1)} %shard_map.59.refs_0_), channel_id=1, source_target_pairs={{0,4},{4,0},{1,5},{5,1},{2,6},{6,2},{3,7},{7,3},{8,12},{12,8},{9,1... | collective-permute-start | bytes 786440 | tf_op jit(solution)/shard_map/ppermute | solution.py:362
  23.1 10.9 %collective-permute-start.9 = (bf16[64,2048]{1,0:T(8,128)(2,1)S(1)}, bf16[64,2048]{1,0:T(8,128)(2,1)S(1)}, u32[]{:S(2)}, u32[]{:S(2)}) collective-permute-start(bf16[64,2048]{1,0:T(8,128)(2,1)S(1)} %add.30), channel_id=1, source_target_pairs={{0,8},{1,2},{2,1},{3,11},{4,12},{5,6},{6,5},{7,15},{8,0},{9,10},{1... | collective-permute-start | bytes 786440 | tf_op jit(solution)/shard_map/ppermute | solution.py:338
  26.6 9.7 %collective-permute-start.14 = (bf16[32,4096]{1,0:T(8,128)(2,1)S(1)}, bf16[32,4096]{1,0:T(8,128)(2,1)S(1)}, u32[]{:S(2)}, u32[]{:S(2)}) collective-permute-start(bf16[32,4096]{1,0:T(8,128)(2,1)S(1)} %get-tuple-element.53), channel_id=1, source_target_pairs={{0,1},{1,0},{2,3},{3,2},{4,5},{5,4},{6,7},{7,6},{8,9},{9,8},{10,11... | collective-permute-start | bytes 786440 | tf_op jit(solution)/shard_map/ppermute | solution.py:330
  29.0 7.6 %collective-permute-start.11 = (bf16[64,2048]{1,0:T(8,128)(2,1)S(1)}, bf16[64,2048]{1,0:T(8,128)(2,1)S(1)}, u32[]{:S(2)}, u32[]{:S(2)}) collective-permute-start(bf16[64,2048]{1,0:T(8,128)(2,1)S(1)} %add.31), channel_id=1, source_target_pairs={{0,8},{1,2},{2,1},{3,11},{4,12},{5,6},{6,5},{7,15},{8,0},{9,10},{1... | collective-permute-start | bytes 786440 | tf_op jit(solution)/shard_map/ppermute | solution.py:338
  29.0 11.5 %collective-permute-start.17 = (bf16[32,4096]{1,0:T(8,128)(2,1)S(1)}, bf16[32,4096]{1,0:T(8,128)(2,1)S(1)}, u32[]{:S(2)}, u32[]{:S(2)}) collective-permute-start(bf16[32,4096]{1,0:T(8,128)(2,1)S(1)} %get-tuple-element.57), channel_id=1, source_target_pairs={{0,1},{3,2},{4,5},{7,6},{8,9},{11,10},{12,13},{15,14},{16,17},{19,... | collective-permute-start | bytes 786440 | tf_op jit(solution)/shard_map/ppermute | solution.py:334
  36.4 4.1 %collective-permute-start.15 = (bf16[32,4096]{1,0:T(8,128)(2,1)S(1)}, bf16[32,4096]{1,0:T(8,128)(2,1)S(1)}, u32[]{:S(2)}, u32[]{:S(2)}) collective-permute-start(bf16[32,4096]{1,0:T(8,128)(2,1)S(1)} %add.33), channel_id=1, source_target_pairs={{0,8},{1,2},{2,1},{3,11},{4,12},{5,6},{6,5},{7,15},{8,0},{9,10},{1... | collective-permute-start | bytes 786440 | tf_op jit(solution)/shard_map/ppermute | solution.py:338
  36.7 9.9 %collective-permute-start.12 = (bf16[32,4096]{1,0:T(8,128)(2,1)S(1)}, bf16[32,4096]{1,0:T(8,128)(2,1)S(1)}, u32[]{:S(2)}, u32[]{:S(2)}) collective-permute-start(bf16[32,4096]{1,0:T(8,128)(2,1)S(1)} %slice_add_fusion.1), channel_id=1, source_target_pairs={{0,1},{1,0},{2,3},{3,2},{4,5},{5,4},{6,7},{7,6},{8,9},{9,8},{10,11... | collective-permute-start | bytes 786440 | tf_op jit(solution)/shard_map/ppermute | solution.py:330
  40.6 10.5 %collective-permute-start.16 = (bf16[32,4096]{1,0:T(8,128)(2,1)S(1)}, bf16[32,4096]{1,0:T(8,128)(2,1)S(1)}, u32[]{:S(2)}, u32[]{:S(2)}) collective-permute-start(bf16[32,4096]{1,0:T(8,128)(2,1)S(1)} %select_add_fusion.1), channel_id=1, source_target_pairs={{0,1},{1,0},{2,3},{3,2},{4,5},{5,4},{6,7},{7,6},{8,9},{9,8},{10,11... | collective-permute-start | bytes 786440 | tf_op jit(solution)/shard_map/ppermute | solution.py:330
  43.8 7.2 %collective-permute-start.18 = (bf16[32,4096]{1,0:T(8,128)(2,1)S(1)}, bf16[32,4096]{1,0:T(8,128)(2,1)S(1)}, u32[]{:S(2)}, u32[]{:S(2)}) collective-permute-start(bf16[32,4096]{1,0:T(8,128)(2,1)S(1)} %add.38), channel_id=1, source_target_pairs={{0,8},{1,2},{2,1},{3,11},{4,12},{5,6},{6,5},{7,15},{8,0},{9,10},{1... | collective-permute-start | bytes 786440 | tf_op jit(solution)/shard_map/ppermute | solution.py:338
